TPU v7x, 32 devices: a whole 2x2x4 slice. The times are simulated.
32 devices in a mesh: cam: 8 (over y, x, core), pts: 4 (over z).
Axes of the slice: x: 2, y: 2, z: 4, core: 2. Of those that a mesh axis runs over, the one named last changes fastest.
Arguments:
- rhs: float32 [9, 65536], P(None, 'cam'), may hold values from -6 to 6
- cam_block: float32 [9, 9, 65536], P(None, None, 'cam'), as said below
- coupling: bfloat16 [256, 144, 6144], P('pts', None, 'cam'), may hold values from -0.0390625 to 0.0390625
- point_inverse: float32 [3, 3, 16384], P(None, None, 'pts'), as said below
- precond: float32 [9, 9, 65536], P(None, None, 'cam'), as said below
- tile_index: int32 [256, 32], P('pts', 'cam'), may hold values from 0 to 511
- tile_count: int32 [256, 8], P('pts', 'cam'), may hold values from 1 to 4, as said below
Outputs:
- solution: float32 [9, 65536], P(None, 'cam')
- residual: float32 [9, 65536], P(None, 'cam')
Inputs may be any that keep to these rules, and one draw needn't show every extreme that they name: `tile_count`: every entry is at least 1 and at most 4; both ends occur. `cam_block`: symmetric with a dominant positive diagonal for each camera. `precond`: symmetric with a dominant positive diagonal for each camera. `point_inverse`: symmetric with a dominant positive diagonal for each point.
All inputs are finite; a program needn't handle non-finite values.
Results may differ from a plain program's by a relative error of at most 0.0024.
Values may be sent and summed in bfloat16 or wider, within the bound.
No kernel may reach another device: no remote copies, remote signals or barrier semaphores. Data moves between devices by JAX's collectives and lax.ppermute only.
A program may use at most 128 MiB of HBM per device.

v0:
```python
import jax
import jax.numpy as jnp
from jax import lax
from jax.sharding import PartitionSpec as P

ITERS = 3


def camera_tiles(vector):
    comps, count = vector.shape
    return (
        vector.reshape(comps, count // 16, 16).transpose(1, 0, 2).reshape(count // 16, comps * 16)
    )


def camera_cols(tiles):
    count = tiles.shape[0]
    return tiles.reshape(count, 9, 16).transpose(1, 0, 2).reshape(9, count * 16)


def point_cols(tiles):
    count = tiles.shape[0]
    return tiles.reshape(count, 3, 64).transpose(1, 0, 2).reshape(3, count * 64)


def point_tiles(vector):
    count = vector.shape[1] // 64
    return vector.reshape(3, count, 64).transpose(1, 0, 2).reshape(count, 192)


def per_device(rhs, cam_block, coupling, point_inverse, precond, tile_index, tile_count):
    tiles_here, slot_count = tile_index.shape
    cam_count = rhs.shape[1] // 16
    blocks = coupling.reshape(tiles_here, 144, slot_count, 192)
    usable = (jnp.arange(slot_count)[None, :] < tile_count).astype(jnp.bfloat16)
    flat_index = tile_index.reshape(-1)
    onehot_t = (jnp.arange(cam_count)[:, None] == flat_index[None, :]).astype(
        jnp.float32
    ) * usable.reshape(1, -1).astype(jnp.float32)

    def global_sum(value):
        return lax.psum(value, "cam")

    solution = jnp.zeros_like(rhs)
    residual = rhs
    precond_res = jnp.sum(precond * residual[None, :, :], axis=1)
    direction = precond_res
    inner_now = global_sum(jnp.sum(residual * precond_res))
    for iteration in range(ITERS):
        dir_rows = jnp.take(
            camera_tiles(direction.astype(jnp.bfloat16)), flat_index, axis=0
        ).reshape(tiles_here, slot_count, 144)
        dir_rows = dir_rows * usable[:, :, None]
        point_part = jnp.einsum(
            "tckp,tkc->tp", blocks, dir_rows, preferred_element_type=jnp.float32
        )
        point_part = point_cols(point_part)
        summed = lax.psum(point_part.astype(jnp.bfloat16), "cam").astype(jnp.float32)
        solved = jnp.sum(point_inverse * summed[None, :, :], axis=1).astype(jnp.bfloat16)
        contrib = jnp.einsum(
            "tckp,tp->tkc", blocks, point_tiles(solved), preferred_element_type=jnp.float32
        )
        cam_part = jnp.dot(
            onehot_t,
            contrib.reshape(-1, 144),
            precision=lax.Precision.HIGHEST,
            preferred_element_type=jnp.float32,
        )
        image = jnp.sum(cam_block * direction[None, :, :], axis=1) - lax.psum(
            camera_cols(cam_part).astype(jnp.bfloat16), "pts"
        ).astype(jnp.float32)
        step_size = inner_now / global_sum(jnp.sum(direction * image))
        solution = solution + step_size * direction
        residual = residual - step_size * image
        if iteration + 1 < ITERS:
            precond_res = jnp.sum(precond * residual[None, :, :], axis=1)
            inner_new = global_sum(jnp.sum(residual * precond_res))
            direction = precond_res + inner_new / inner_now * direction
            inner_now = inner_new
    return (solution, residual)


def solution(mesh):
    in_specs = (
        P(None, "cam"),
        P(None, None, "cam"),
        P("pts", None, "cam"),
        P(None, None, "pts"),
        P(None, None, "cam"),
        P("pts", "cam"),
        P("pts", "cam"),
    )
    out_specs = (P(None, "cam"), P(None, "cam"))
    return jax.shard_map(
        per_device, mesh=mesh, in_specs=in_specs, out_specs=out_specs, check_vma=False
    )
```

profile of v0, /device:TPU:0, one launch (start us, length us, event | category | flops | bytes accessed | tf_op | source)
XLA Modules:
  0.0 431.5 jit_solution(18186521413559238750)
XLA Ops:
  8.1 3.4 multiply_reduce_fusion.5
  14.6 35.9 %reshape.168 = bf16[64,144,4,192]{3,2,1,0:T(4,128)(2,1)} reshape(bf16[64,144,768]{2,1,0:T(8,128)(2,1)} %param.11) | data formatting | bytes 28311552 | tf_op jit(solution)/shard_map/reshape | solution.py:34
  50.6 9.1 %fusion.7 = bf16[64,1,192,1]{2,1,3,0:T(2,128)(2,1)S(1)} fusion(bf16[64,144,4,192]{3,2,1,0:T(4,128)(2,1)} %reshape.168, bf16[64,4,144,1]{2,1,0,3:T(4,128)(2,1)S(1)} %multiply_bitcast_fusion.2), kind=kOutput, calls=%fused_computation.13 | convolution fusion | flops 14155776 | bytes 14254080 | tf_op jit(solution)/shard_map/tckp,tkc->tp/dot_general | solution.py:54
  60.1 26.2 %psum.85 = bf16[3,4096]{1,0:T(4,128)(2,1)S(1)} all-reduce(bf16[3,4096]{1,0:T(4,128)(2,1)S(1)} %convert_element_type.154), channel_id=1, replica_groups=mesh['cam'=8,'pts'=4] {'cam'}, use_global_device_ids=true, to_apply=%region_4.6 | all-reduce | flops 12288 | bytes 49152 | tf_op jit(solution)/shard_map/psum | solution.py:58
  86.8 16.4 %fusion = f32[64,144,4]{2,1,0:T(8,128)} fusion(f32[64,192]{1,0:T(8,128)S(1)} %copy.66, bf16[64,144,4,192]{3,2,1,0:T(4,128)(2,1)} %reshape.168), kind=kLoop, calls=%fused_computation.6 | loop fusion | flops 21196800 | bytes 14352384
  103.2 4.1 copy.51
  111.5 3.3 multiply_reduce_fusion.4
  114.8 31.5 %all-reduce.5.cloned.1.call-done = bf16[9,8192]{1,0:T(8,128)(2,1)} async-done(((bf16[9,8192]{1,0:T(8,128)(2,1)}), bf16[9,8192]{1,0:T(8,128)(2,1)}) %all-reduce.5.cloned.1.call-update) | async-done | bytes 147472 | tf_op jit(solution)/shard_map/psum | solution.py:69
  148.0 12.8 %all-reduce = (f32[]{:T(128)}, f32[]{:T(128)}) all-reduce(f32[]{:T(128)} %get-tuple-element.4, f32[]{:T(128)} %get-tuple-element.3), channel_id=1, replica_groups=mesh['cam'=8,'pts'=4] {'cam'}, use_global_device_ids=true, to_apply=%region_2.0 | all-reduce | flops 2 | bytes 16 | tf_op jit(solution)/shard_map/psum | solution.py:42
  163.2 3.3 multiply_reduce_fusion.3
  167.2 12.6 %psum.88 = f32[]{:T(128)} all-reduce(f32[]{:T(128)} %multiply_reduce_fusion.9), channel_id=1, replica_groups=mesh['cam'=8,'pts'=4] {'cam'}, use_global_device_ids=true, to_apply=%region_11.13 | all-reduce | flops 1 | bytes 8 | tf_op jit(solution)/shard_map/psum | solution.py:42
  184.1 9.1 %fusion.5 = bf16[64,1,192,1]{2,1,3,0:T(2,128)(2,1)S(1)} fusion(bf16[64,144,4,192]{3,2,1,0:T(4,128)(2,1)} %reshape.168, bf16[64,4,144,1]{2,1,0,3:T(4,128)(2,1)S(1)} %multiply_bitcast_fusion.1), kind=kOutput, calls=%fused_computation.11 | convolution fusion | flops 14155776 | bytes 14254080 | tf_op jit(solution)/shard_map/tckp,tkc->tp/dot_general | solution.py:54
  193.6 22.4 %psum.89 = bf16[3,4096]{1,0:T(4,128)(2,1)S(1)} all-reduce(bf16[3,4096]{1,0:T(4,128)(2,1)S(1)} %convert_element_type.167), channel_id=1, replica_groups=mesh['cam'=8,'pts'=4] {'cam'}, use_global_device_ids=true, to_apply=%region_13.15 | all-reduce | flops 12288 | bytes 49152 | tf_op jit(solution)/shard_map/psum | solution.py:58
  216.4 16.4 %fusion.1 = f32[64,144,4]{2,1,0:T(8,128)} fusion(f32[64,192]{1,0:T(8,128)S(1)} %copy.67, bf16[64,144,4,192]{3,2,1,0:T(4,128)(2,1)} %reshape.168), kind=kLoop, calls=%fused_computation.7 | loop fusion | flops 21196800 | bytes 14352384
  232.8 4.1 copy.58
  244.3 30.6 %all-reduce.7.cloned.1.call-done = bf16[9,8192]{1,0:T(8,128)(2,1)} async-done(((bf16[9,8192]{1,0:T(8,128)(2,1)}), bf16[9,8192]{1,0:T(8,128)(2,1)}) %all-reduce.7.cloned.1.call-update) | async-done | bytes 147472 | tf_op jit(solution)/shard_map/psum | solution.py:69
  276.6 13.1 %psum.91 = f32[]{:T(128)} all-reduce(f32[]{:T(128)} %multiply_reduce_fusion.8), channel_id=1, replica_groups=mesh['cam'=8,'pts'=4] {'cam'}, use_global_device_ids=true, to_apply=%region_17.19 | all-reduce | flops 1 | bytes 8 | tf_op jit(solution)/shard_map/psum | solution.py:42
  295.9 12.4 %psum.92 = f32[]{:T(128)} all-reduce(f32[]{:T(128)} %multiply_reduce_fusion.7), channel_id=1, replica_groups=mesh['cam'=8,'pts'=4] {'cam'}, use_global_device_ids=true, to_apply=%region_20.22 | all-reduce | flops 1 | bytes 8 | tf_op jit(solution)/shard_map/psum | solution.py:42
  315.8 9.1 %fusion.3 = bf16[64,1,192,1]{2,1,3,0:T(2,128)(2,1)S(1)} fusion(bf16[64,144,4,192]{3,2,1,0:T(4,128)(2,1)} %reshape.168, bf16[64,4,144,1]{2,1,0,3:T(4,128)(2,1)S(1)} %multiply_bitcast_fusion), kind=kOutput, calls=%fused_computation.9 | convolution fusion | flops 14155776 | bytes 14254080 | tf_op jit(solution)/shard_map/tckp,tkc->tp/dot_general | solution.py:54
  325.3 22.6 %psum.93 = bf16[3,4096]{1,0:T(4,128)(2,1)S(1)} all-reduce(bf16[3,4096]{1,0:T(4,128)(2,1)S(1)} %convert_element_type.178), channel_id=1, replica_groups=mesh['cam'=8,'pts'=4] {'cam'}, use_global_device_ids=true, to_apply=%region_22.24 | all-reduce | flops 12288 | bytes 49152 | tf_op jit(solution)/shard_map/psum | solution.py:58
  348.4 16.4 %fusion.2 = f32[64,144,4]{2,1,0:T(8,128)} fusion(f32[64,192]{1,0:T(8,128)S(1)} %copy.68, bf16[64,144,4,192]{3,2,1,0:T(4,128)(2,1)} %reshape.168), kind=kLoop, calls=%fused_computation.8 | loop fusion | flops 21196800 | bytes 14352384
  364.8 4.1 copy.65
  376.2 30.6 %all-reduce.9.cloned.1.call-done = bf16[9,8192]{1,0:T(8,128)(2,1)} async-done(((bf16[9,8192]{1,0:T(8,128)(2,1)}), bf16[9,8192]{1,0:T(8,128)(2,1)}) %all-reduce.9.cloned.1.call-update) | async-done | bytes 147472 | tf_op jit(solution)/shard_map/psum | solution.py:69
  408.5 12.8 %psum.95 = f32[]{:T(128)} all-reduce(f32[]{:T(128)} %multiply_reduce_fusion.6), channel_id=1, replica_groups=mesh['cam'=8,'pts'=4] {'cam'}, use_global_device_ids=true, to_apply=%region_26.28 | all-reduce | flops 1 | bytes 8 | tf_op jit(solution)/shard_map/psum | solution.py:42
  (96 shorter events, 48.4 us)
Async XLA Ops:
  7.2 139.1 %all-reduce.5.cloned.1.call-start = ((), (), s32[]{:S(2)}) async-start(), calls=%async_computation | async-start | bytes 524288 | tf_op jit(solution)/shard_map/psum | solution.py:69
  8.1 6.4 %copy-start.2 = (s32[64,1]{0,1:T(1,128)S(1)}, s32[64,1]{0,1:T(1,128)}, u32[]{:S(2)}) copy-start(s32[64,1]{0,1:T(1,128)} %param.15) | copy-start | bytes 772
  50.6 35.7 %copy-start.1 = (f32[3,3,4096]{2,1,0:T(4,128)S(1)}, f32[3,3,4096]{2,1,0:T(4,128)}, u32[]{:S(2)}) copy-start(f32[3,3,4096]{2,1,0:T(4,128)} %param.12) | copy-start | bytes 442372
  107.5 38.8 %copy-start = (f32[9,8192]{1,0:T(8,128)S(1)}, f32[9,8192]{1,0:T(8,128)}, u32[]{:S(2)}) copy-start(f32[9,8192]{1,0:T(8,128)} %param.9) | copy-start | bytes 884740
  111.4 163.4 %all-reduce.7.cloned.1.call-start = ((), (), s32[]{:S(2)}) async-start(), calls=%async_computation.1 | async-start | bytes 524288 | tf_op jit(solution)/shard_map/psum | solution.py:69
  241.0 165.8 %all-reduce.9.cloned.1.call-start = ((), (), s32[]{:S(2)}) async-start(), calls=%async_computation.2 | async-start | bytes 524288 | tf_op jit(solution)/shard_map/psum | solution.py:69
Sparse Core Ops, SparseCore 0:
  111.5 34.6 all-reduce.4
  241.1 33.7 all-reduce.6
  373.0 33.7 all-reduce.8
where the time goes:
time: 439 us; the launch traced here: 432 us
  blocking collectives  135 us (31%)
  waiting for transfers between devices  92.7 us (21%)
  other arithmetic  82 us (19%)
  local copies, waits for them, and re-layouts  71.4 us (16%)
  matrix products  29.6 us (7%)
  between operations  20.9 us (5%)
    psum x3, waiting for transfers between devices, per_device(): lax.psum(camera_cols(cam_part).astype(jnp.bfloat16), 'pts')  92.6 us
    psum x3, blocking collectives, per_device(): lax.psum(point_part.astype(jnp.bfloat16), 'cam').astype(jnp.float32)  71.2 us
    psum x5, blocking collectives, global_sum(): return lax.psum(value, 'cam')  63.7 us
    unnamed x6, other arithmetic  49.2 us
    reshape x1, local copies, waits for them, and re-layouts, per_device(): blocks = coupling.reshape(tiles_here, 144, slot_count, 192)  35.9 us
    dot_general x3, matrix products, per_device(): jnp.einsum('tckp,tkc->tp', blocks, dir_rows, preferred_element_type=jnp.f...  27.4 us
    dot_general x3, local copies, waits for them, and re-layouts, per_device(): jnp.einsum('tckp,tp->tkc', blocks, point_tiles(solved), preferred_element...  12.3 us
    reduce_sum x3, other arithmetic, per_device(): precond_res = jnp.sum(precond * residual[None, :, :], axis=1)  10 us
  transfers between devices with their start and end apart: 3, of which 3 were waited for; matrix products, arithmetic and copies ran while one was open for 2% of the time, Pallas kernels for 0%

commit v1 on v0

v1 whole, which is shorter than its diff:
```python
import functools

import jax
import jax.numpy as jnp
from jax import lax
from jax.experimental import pallas as pl
from jax.experimental.pallas import tpu as pltpu
from jax.sharding import PartitionSpec as P


ITERS = 3
F32 = jnp.float32
BF16 = jnp.bfloat16
VMEM = pl.BlockSpec(memory_space=pltpu.VMEM)
HBM = pl.BlockSpec(memory_space=pltpu.HBM)
NT = (((1,), (1,)), ((), ()))
FETCHES = 8


def iota(shape, dim):
    return lax.broadcasted_iota(jnp.int32, shape, dim)


def tree_sum(values):
    while len(values) > 1:
        values = [a + b for a, b in zip(values[::2], values[1::2])] + values[
            len(values) - len(values) % 2 :
        ]
    return values[0]


def sym(size, i, j):
    i, j = min(i, j), max(i, j)
    return i * size - i * (i - 1) // 2 + (j - i)


def total(value):
    return jnp.sum(value, keepdims=True)


def pieces(value):
    high = value.astype(BF16).astype(F32)
    rest = value - high
    middle = rest.astype(BF16).astype(F32)
    return [high, middle, rest - middle]


def scalar_lanes(scalars, rows):
    lane = iota((rows, 64), 1)
    tile = jnp.zeros((rows, 64), F32)
    for at, piece in enumerate(p for s in scalars for p in pieces(s)):
        tile = jnp.where(lane == at, piece, tile)
    return tile


def read_scalars(tile, count):
    row = tile[0:1, :]
    return [
        row[:, 3 * n : 3 * n + 1] + row[:, 3 * n + 1 : 3 * n + 2] + row[:, 3 * n + 2 : 3 * n + 3]
        for n in range(count)
    ]


def sym_rows(matrix, size, rows, vector):
    return [
        tree_sum([matrix[sym(size, i, j), rows, :] * vector[j] for j in range(size)])
        for i in range(size)
    ]


def tile_onehot(row_a, row_q, tiles, planes):
    column = jnp.where(row_a >= 0, row_q * planes + row_a, -1.0).astype(jnp.int32)
    return jnp.where(iota((tiles, column.shape[1]), 0) == column, 1.0, 0.0).astype(BF16)


def to_tiles(z_ref, zt_ref):
    planes = z_ref.shape[1]
    for j in range(z_ref.shape[0]):
        turned = z_ref[j].T
        parts = [turned[16 * q : 16 * q + 16, :] for q in range(8)]
        zt_ref[16 * j : 16 * j + 16, :] = jnp.concatenate(parts, axis=1).astype(BF16)


def from_tiles(tiles, t4_ref):
    planes = t4_ref.shape[1]
    for j in range(t4_ref.shape[0]):
        block = tiles[16 * j : 16 * j + 16, :]
        parts = [block[:, q * planes : (q + 1) * planes] for q in range(8)]
        t4_ref[j] = jnp.concatenate(parts, axis=0).T


def gather_rows(zt_ref, onehot, rows_ref):
    rows_ref[...] = jnp.dot(zt_ref[...], onehot, preferred_element_type=F32).T


def forward_pairs(e_ref, rows_ref, part_ref, first, count, unroll):
    sub = iota((8, rows_ref.shape[1]), 0)

    def body(pair, carry):
        rows = rows_ref[pl.ds(pl.multiple_of(pair * 8, 8), 8), :]
        top = jnp.where(sub < 4, rows, 0.0).astype(BF16)
        low = jnp.where(sub >= 4, rows, 0.0).astype(BF16)
        part = jnp.dot(top, e_ref[2 * pair], preferred_element_type=F32) + jnp.dot(
            low, e_ref[2 * pair + 1], preferred_element_type=F32
        )
        for i in range(6):
            part_ref[i, pl.ds(pl.multiple_of(pair * 8, 8), 8), :] = part[:, 128 * i : 128 * i + 128]
        return carry

    lax.fori_loop(first, first + count, body, 0, unroll=unroll)


def forward_sum(part_ref, count):
    def pick(i, s):
        return part_ref[i, pl.ds(s, count, 4), :]

    even = jnp.concatenate([pick(0, 0) + pick(3, 2), pick(1, 0) + pick(4, 2)], axis=1)
    odd = jnp.concatenate([pick(1, 1) + pick(4, 3), pick(2, 1) + pick(5, 3)], axis=1)
    return even[:, :192] + odd[:, 64:]


def backward(e_ref, y, yc_ref, c_ref, unroll):
    count = e_ref.shape[0]
    wide = [jnp.concatenate(pair, axis=1) for pair in ((y[0], y[1]), (y[2], y[0]), (y[1], y[2]))]
    for i in range(6):
        yc_ref[:, 128 * i : 128 * i + 128] = wide[i % 3]
    row, col = iota((8, 768), 0), iota((8, 768), 1)
    masks = [(col >= 192 * (row - r)) & (col < 192 * (row - r) + 192) for r in (0, 4)]

    def body(pair, carry):
        part = None
        for k in range(2):
            wide_row = jnp.broadcast_to(yc_ref[pl.ds(2 * pair + k, 1), :], (8, 768))
            lhs = jnp.where(masks[k], wide_row, 0.0).astype(BF16)
            one = lax.dot_general(lhs, e_ref[2 * pair + k], NT, preferred_element_type=F32)
            part = one if part is None else part + one
        c_ref[pl.ds(pl.multiple_of(pair * 8, 8), 8), :] = part
        return carry

    lax.fori_loop(0, count // 2, body, 0, unroll=unroll)


def start_kernel(
    rhs_hbm, m_hbm, c_hbm, e_hbm, v_hbm, index_ref, count_ref,
    e_ref, m_ref, c_ref, v_ref, r_ref, z_ref, cz_ref, slot_ref, msg_ref,
    rn, mn, m8, cn, c8, vn, split, vrow, zt_ref, rows_ref, part_ref, sems, e_sems,
):
    planes, count = r_ref.shape[1], e_ref.shape[0]
    step = count // FETCHES
    inner = pl.ds(0, 8)
    copies = [
        pltpu.make_async_copy(src, dst, sems.at[n])
        for n, (src, dst) in enumerate(
            (
                (rhs_hbm, rn),
                (m_hbm.at[inner, inner], mn),
                (m_hbm.at[8], m8),
                (c_hbm.at[inner, inner], cn),
                (c_hbm.at[8], c8),
                (v_hbm, vn),
            )
        )
    ]
    for copy in copies:
        copy.start()

    def fetch(n):
        part = pl.ds(n * step, step)
        return pltpu.make_async_copy(e_hbm.at[part], e_ref.at[part], e_sems.at[n])

    for n in range(FETCHES):
        fetch(n).start()

    def split_rows(src, buffer):
        def body(a, carry):
            lanes = pl.ds(pl.multiple_of(a * 128, 128), 128)
            buffer[pl.ds(pl.multiple_of(a * 8, 8), 8), :] = src[inner, lanes]
            return carry

        lax.fori_loop(0, planes, body, 0, unroll=16)

    def split_last(src, store):
        def body(a, carry):
            lanes = pl.ds(pl.multiple_of(a * 128, 128), 128)
            store(a, src[pl.ds(8, 1), lanes])
            return carry

        lax.fori_loop(0, planes, body, 0, unroll=16)

    def split_matrix(inner_ref, last_ref, out_ref):
        for i in range(9):
            buffer = split.at[i % 2]
            split_rows(inner_ref.at[i] if i < 8 else last_ref, buffer)
            for j in range(i if i < 8 else 0, 8):
                out_ref[sym(9, i, j)] = buffer[pl.ds(j, planes, 8), :]

        def store(a, row):
            out_ref[sym(9, 8, 8), pl.ds(a, 1), :] = row

        split_last(last_ref, store)

    slots = index_ref.shape[1]
    index = index_ref[...]
    used = iota(index.shape, 1) < count_ref[...]
    spread = jnp.where(iota((count, count * slots), 1) // slots == iota((count, count * slots), 0), 1.0, 0.0)
    mine = iota((8, count * slots), 1) % slots == iota((8, count * slots), 0)
    pad = jnp.zeros((count, 128 - slots), F32)
    slot_rows = []
    for part in (jnp.where(used, index // 8, -1), index % 8):
        turned = jnp.concatenate([part.astype(F32), pad], axis=1).T[0:8, :]
        moved = jnp.dot(turned.astype(BF16), spread.astype(BF16), preferred_element_type=F32)
        slot_rows.append(jnp.sum(jnp.where(mine, moved, 0.0), axis=0, keepdims=True))
    row = iota((8, count * slots), 0)
    slot_ref[...] = jnp.where(row == 0, slot_rows[0], jnp.where(row == 1, slot_rows[1], 0.0))
    onehot = tile_onehot(slot_rows[0], slot_rows[1], 8 * planes, planes)

    copies[0].wait()
    split_rows(rn, split.at[0])
    for j in range(8):
        r_ref[j] = split[0, pl.ds(j, planes, 8), :]

    def store_last(a, value):
        r_ref[8, pl.ds(a, 1), :] = value

    split_last(rn, store_last)
    copies[1].wait()
    copies[2].wait()
    split_matrix(mn, m8, m_ref)

    def precondition(g, inner_sum):
        rows = pl.ds(pl.multiple_of(g * 8, 8), 8)
        r = [r_ref[j, rows, :] for j in range(9)]
        z = sym_rows(m_ref, 9, rows, r)
        for j in range(9):
            z_ref[j, rows, :] = z[j]
        return inner_sum + tree_sum([a * b for a, b in zip(r, z)])

    zero = jnp.zeros((8, 128), F32)
    inner_sum = lax.fori_loop(0, planes // 8, precondition, zero)
    to_tiles(z_ref, zt_ref)
    gather_rows(zt_ref, onehot, rows_ref)

    copies[3].wait()
    copies[4].wait()
    split_matrix(cn, c8, c_ref)

    def apply_camera(g, curve):
        rows = pl.ds(pl.multiple_of(g * 8, 8), 8)
        z = [z_ref[j, rows, :] for j in range(9)]
        cz = sym_rows(c_ref, 9, rows, z)
        for j in range(9):
            cz_ref[j, rows, :] = cz[j]
        return curve + tree_sum([a * b for a, b in zip(z, cz)])

    curve = lax.fori_loop(0, planes // 8, apply_camera, zero)

    copies[5].wait()
    half = vrow.shape[0]
    for i in range(3):
        for j in range(i, 3):

            def body(u, carry):
                lanes = pl.ds(pl.multiple_of(u * 128, 128), 128)
                vrow[pl.ds(u, 1), :] = vn[i, j : j + 1, lanes]
                return carry

            lax.fori_loop(0, half, body, 0, unroll=16)
            plane = vrow[...]
            v_ref[sym(3, i, j), pl.ds(0, half, 2), :] = plane
            v_ref[sym(3, i, j), pl.ds(1, half, 2), :] = jnp.concatenate(
                [plane[:, 64:], plane[:, :64]], axis=1
            )

    def chunk(n, carry):
        fetch(n).wait()
        forward_pairs(e_ref, rows_ref, part_ref, n * (step // 2), step // 2, True)
        return carry

    lax.fori_loop(0, FETCHES, chunk, 0)
    scalars = scalar_lanes([total(inner_sum), total(curve), jnp.zeros((1, 1), F32)], count)
    msg_ref[...] = jnp.concatenate([forward_sum(part_ref, count), scalars], axis=1).astype(BF16)


def pair_kernel(*refs):
    *in_refs, out_ref = refs
    value = tree_sum([ref[...].astype(F32) for ref in in_refs])
    scalars = scalar_lanes(read_scalars(value[:, 192:], 3), value.shape[0])
    out_ref[...] = jnp.concatenate([value[:, :192], scalars], axis=1).astype(BF16)


def points_kernel(parts, first, *refs):
    summed = tree_sum([ref[...].astype(F32) for ref in refs[:parts]])
    refs = refs[parts:]
    if not first:
        p_old_ref, scal_old_ref, *refs = refs
    e_ref, v_ref, slot_ref, msg_ref, p_ref, scal_ref, yc_ref, c_ref = refs
    inner_now, z_c_z, z_c_d = read_scalars(summed[:, 192:], 3)
    point_sum = summed[:, :192]
    beta, curve = jnp.zeros((1, 1), F32), z_c_z
    if not first:
        beta = inner_now / scal_old_ref[0:1, 0:1]
        curve = z_c_z + beta * (2.0 * z_c_d + beta * scal_old_ref[1:2, 0:1])
        point_sum = point_sum + beta * p_old_ref[...]
    p_ref[...] = point_sum
    row = iota((8, 128), 0)
    scal_ref[...] = jnp.where(row == 0, inner_now, jnp.where(row == 1, curve, beta))
    p = [point_sum[:, 64 * i : 64 * i + 64] for i in range(3)]
    y = [tree_sum([v_ref[sym(3, i, j)][:, :64] * p[j] for j in range(3)]) for i in range(3)]
    taken = total(tree_sum([a * b for a, b in zip(p, y)]))
    backward(e_ref, y, yc_ref, c_ref, 16)
    rows = c_ref.shape[1]
    msg_ref[0:rows, :] = c_ref[...].T.astype(BF16)
    width = msg_ref.shape[1]
    row = iota((16, width), 0)
    tail = jnp.zeros((16, width), F32)
    for at, value in enumerate([slot_ref[0:1, :], slot_ref[1:2, :], *pieces(taken)]):
        tail = jnp.where(row == at, value, tail)
    msg_ref[rows : rows + 16, :] = tail.astype(BF16)


def camera_kernel(parts, first, last, *refs):
    msgs, refs = refs[:parts], refs[parts:]
    scal_ref, z_ref, cz_ref, r_ref, *refs = refs
    if not first:
        d_old_ref, cd_old_ref, sol_old_ref, *refs = refs
    if last:
        sol_out, res_out, all_ref, t4_ref, sol_ref, split = refs
        res_ref = t4_ref
    else:
        e_ref, m_ref, c_ref, slot_ref, *refs = refs
        msg_ref, res_ref, sol_ref, zn_ref, czn_ref, *refs = refs
        if not first:
            d_ref, cd_ref, *refs = refs
        all_ref, t4_ref, zt_ref, rows_ref, part_ref = refs
    planes = z_ref.shape[1]
    rows_all = all_ref.shape[1] - 16
    me = lax.axis_index("pts")
    for k in range(parts):
        all_ref[me ^ k] = msgs[k][...]
    taken, tiles = [], []
    for k in range(parts):
        tail = all_ref[k, rows_all : rows_all + 16, :].astype(F32)
        taken.append(tail[2:3, 0:1] + tail[3:4, 0:1] + tail[4:5, 0:1])
        onehot = tile_onehot(tail[0:1, :], tail[1:2, :], 8 * planes, planes)
        tiles.append(
            lax.dot_general(all_ref[k, 0:rows_all, :], onehot, NT, preferred_element_type=F32)
        )
    inner_now, curve, beta = scal_ref[0:1, 0:1], scal_ref[1:2, 0:1], scal_ref[2:3, 0:1]
    step_size = inner_now / (curve - tree_sum(taken))
    from_tiles(tree_sum(tiles), t4_ref)

    def update(g, sums):
        rows = pl.ds(pl.multiple_of(g * 8, 8), 8)
        r, cd = [], []
        for j in range(9):
            d, c_d = z_ref[j, rows, :], cz_ref[j, rows, :]
            if not first:
                d = d + beta * d_old_ref[j, rows, :]
                c_d = c_d + beta * cd_old_ref[j, rows, :]
                if not last:
                    d_ref[j, rows, :] = d
                    cd_ref[j, rows, :] = c_d
            step = step_size * d
            sol_ref[j, rows, :] = step if first else sol_old_ref[j, rows, :] + step
            r.append(r_ref[j, rows, :] - step_size * (c_d - t4_ref[j, rows, :]))
            cd.append(c_d)
        for j in range(9):
            res_ref[j, rows, :] = r[j]
        if last:
            return sums
        z = sym_rows(m_ref, 9, rows, r)
        cz = sym_rows(c_ref, 9, rows, z)
        for j in range(9):
            zn_ref[j, rows, :] = z[j]
            czn_ref[j, rows, :] = cz[j]
        pairs = (zip(r, z), zip(z, cz), zip(z, cd))
        return tuple(s + tree_sum([a * b for a, b in p]) for s, p in zip(sums, pairs))

    sums = lax.fori_loop(0, planes // 8, update, (jnp.zeros((8, 128), F32),) * 3)
    if last:
        for src, dst in ((sol_ref, sol_out), (res_ref, res_out)):
            for j in range(8):
                split[pl.ds(j, planes, 8), :] = src[j]

            def body(a, carry):
                lanes = pl.ds(pl.multiple_of(a * 128, 128), 128)
                dst[0:8, lanes] = split[pl.ds(pl.multiple_of(a * 8, 8), 8), :]
                dst[8:9, lanes] = src[8, pl.ds(a, 1), :]
                return carry

            lax.fori_loop(0, planes, body, 0, unroll=16)
        return
    to_tiles(zn_ref, zt_ref)
    onehot = tile_onehot(slot_ref[0:1, :], slot_ref[1:2, :], 8 * planes, planes)
    gather_rows(zt_ref, onehot, rows_ref)
    count = e_ref.shape[0]
    forward_pairs(e_ref, rows_ref, part_ref, 0, count // 2, 16)
    scalars = scalar_lanes([total(s) for s in sums], count)
    msg_ref[...] = jnp.concatenate([forward_sum(part_ref, count), scalars], axis=1).astype(BF16)


def per_device(n_cam, n_pts, rhs, cam_block, coupling, point_inverse, precond, tile_index, tile_count):
    count, slots = tile_index.shape
    size, cams = rhs.shape
    rows, cols = coupling.shape[1:]
    planes, tiles, width = cams // 128, cams // 16, count * slots
    points = point_inverse.shape[2]
    shape = jax.ShapeDtypeStruct
    vector = shape((size, planes, 128), F32)
    message = shape((count, 256), BF16)
    planes_of = size * (size + 1) // 2
    part_scratch = pltpu.VMEM((cols // 128, width, 128), F32)
    rows_scratch = pltpu.VMEM((width, rows), F32)
    zt_scratch = pltpu.VMEM((rows, tiles), BF16)

    def call(kernel, outs, args, in_specs=None, scratch=(), megabytes=8, name=None):
        return pl.pallas_call(
            kernel,
            out_shape=outs,
            in_specs=in_specs or [VMEM] * len(args),
            out_specs=jax.tree.map(lambda _: VMEM, outs),
            scratch_shapes=list(scratch),
            compiler_params=pltpu.CompilerParams(vmem_limit_bytes=megabytes * 2**20),
            name=name,
        )(*args)

    def exchange(value, axis, axis_size, masks):
        return [value] + [
            lax.ppermute(value, axis, [(i, i ^ k) for i in range(axis_size)]) for k in masks
        ]

    coupling, m4, c4, v6, residual, z, cz, slot, message_now = call(
        start_kernel,
        [
            pltpu.VMEM(coupling.shape, BF16),
            pltpu.VMEM((planes_of, planes, 128), F32),
            pltpu.VMEM((planes_of, planes, 128), F32),
            pltpu.VMEM((6, count, 128), F32),
            vector,
            vector,
            vector,
            shape((8, width), F32),
            message,
        ],
        (rhs, precond, cam_block, coupling, point_inverse, tile_index, tile_count),
        in_specs=[HBM] * 5 + [VMEM] * 2,
        scratch=[
            pltpu.VMEM((size, cams), F32),
            pltpu.VMEM((8, 8, cams), F32),
            pltpu.VMEM((size, cams), F32),
            pltpu.VMEM((8, 8, cams), F32),
            pltpu.VMEM((size, cams), F32),
            pltpu.VMEM((3, 3, points), F32),
            pltpu.VMEM((2, 8 * planes, 128), F32),
            pltpu.VMEM((points // 128, 128), F32),
            zt_scratch,
            rows_scratch,
            part_scratch,
            pltpu.SemaphoreType.DMA((6,)),
            pltpu.SemaphoreType.DMA((FETCHES,)),
        ],
        megabytes=16,
        name="start",
    )
    inner = max(1, n_cam // 4)
    old_points, old_camera = (), ()
    for iteration in range(ITERS):
        first, last = iteration == 0, iteration + 1 == ITERS
        if inner > 1:
            pair = exchange(message_now, "cam", n_cam, range(1, inner))
            message_now = call(pair_kernel, message, pair, name="pair")
        parts = exchange(message_now, "cam", n_cam, range(inner, n_cam, inner))
        tile_message, point_sum, scal = call(
            functools.partial(points_kernel, len(parts), first),
            [
                shape((rows + 16, width), BF16),
                shape((count, 192), F32),
                shape((8, 128), F32),
            ],
            (*parts, *old_points, coupling, v6, slot),
            scratch=[pltpu.VMEM((count, cols), F32), rows_scratch],
            name="points",
        )
        old_points = (point_sum, scal)
        parts = exchange(tile_message, "pts", n_pts, range(1, n_pts))
        kernel = functools.partial(camera_kernel, len(parts), first, last)
        common = [
            pltpu.VMEM((n_pts, rows + 16, width), BF16),
            pltpu.VMEM((size, planes, 128), F32),
        ]
        args = (*parts, scal, z, cz, residual, *old_camera)
        if last:
            plain = shape((size, cams), F32)
            scratch = [*common, pltpu.VMEM((size, planes, 128), F32), pltpu.VMEM((8 * planes, 128), F32)]
            return tuple(call(kernel, [plain, plain], args, scratch=scratch, name="finish"))
        outs = [message, vector, vector, vector, vector] + ([] if first else [vector, vector])
        message_now, residual, solution, z_new, cz_new, *direction = call(
            kernel,
            outs,
            (*args, coupling, m4, c4, slot),
            scratch=[*common, zt_scratch, rows_scratch, part_scratch],
            name="camera",
        )
        d, cd = direction if direction else (z, cz)
        old_camera = (d, cd, solution)
        z, cz = z_new, cz_new


def solution(mesh):
    in_specs = (
        P(None, "cam"),
        P(None, None, "cam"),
        P("pts", None, "cam"),
        P(None, None, "pts"),
        P(None, None, "cam"),
        P("pts", "cam"),
        P("pts", "cam"),
    )
    out_specs = (P(None, "cam"), P(None, "cam"))
    return jax.shard_map(
        functools.partial(per_device, mesh.shape["cam"], mesh.shape["pts"]),
        mesh=mesh,
        in_specs=in_specs,
        out_specs=out_specs,
        check_vma=False,
    )
```

time: 439 us -> 99.1 us (0.23); the launches traced: 432 us -> 98.8 us
  blocking collectives: 135 us -> 0 us
  other arithmetic: 82 us -> 0 us
  waiting for transfers between devices: 92.7 us -> 27.2 us
  local copies, waits for them, and re-layouts: 71.4 us -> 8.16 us
  Pallas kernels: 0 us -> 37.4 us
  matrix products: 29.6 us -> 0 us
  starting transfers between devices: 0.12 us -> 25.3 us
  between operations: 20.9 us -> 0.7 us
    psum x8 -> x0, blocking collectives: 135 us -> none  [the longest x3 71.2 us: per_device(): lax.psum(point_part.astype(jnp.bfloat16), 'cam').astype(jnp.float32)]
    psum x3 -> x0, waiting for transfers between devices: 92.6 us -> none  [per_device(): lax.psum(camera_cols(cam_part).astype(jnp.bfloat16), 'pts')]
    unnamed x6 -> x0, other arithmetic: 49.2 us -> none
    reshape x10 -> x0, local copies, waits for them, and re-layouts: 37.7 us -> none  [the longest x1 35.9 us: per_device(): blocks = coupling.reshape(tiles_here, 144, slot_count, 192)]
    pallas_call x0 -> x10, Pallas kernels: none -> 37.4 us  [call(): pl.pallas_call(kernel, out_shape=outs, in_specs=in_specs or [VMEM] * len(...]
    dot_general x6 -> x0, matrix products: 29.6 us -> none  [the longest x3 27.4 us: per_device(): jnp.einsum('tckp,tkc->tp', blocks, dir_rows, preferred_element_type=jnp.f...]
    ppermute x0 -> x21, waiting for transfers between devices: none -> 27.2 us  [exchange(): lax.ppermute(value, axis, [(i, i ^ k) for i in range(axis_size)])]
    reduce_sum x14 -> x0, other arithmetic: 26.9 us -> none  [the longest x3 10 us: per_device(): precond_res = jnp.sum(precond * residual[None, :, :], axis=1)]
  transfers between devices with their start and end apart: 3 -> 21, of which waited for: 3 -> 18; matrix products, arithmetic and copies ran while one was open for 2% -> 0% of each run, Pallas kernels for 0% -> 0%
where the time goes in v1:
time: 99.1 us; the launch traced here: 98.8 us
  Pallas kernels  37.4 us (38%)
  waiting for transfers between devices  27.2 us (27%)
  starting transfers between devices  25.3 us (26%)
  local copies, waits for them, and re-layouts  8.16 us (8%)
    pallas_call x10, Pallas kernels, call(): pl.pallas_call(kernel, out_shape=outs, in_specs=in_specs or [VMEM] * len(...  37.4 us
    ppermute x21, waiting for transfers between devices, exchange(): lax.ppermute(value, axis, [(i, i ^ k) for i in range(axis_size)])  27.2 us
    ppermute x21, starting transfers between devices, exchange(): lax.ppermute(value, axis, [(i, i ^ k) for i in range(axis_size)])  25.3 us
    unnamed x10, local copies, waits for them, and re-layouts  8.16 us
  transfers between devices with their start and end apart: 21, of which 18 were waited for; matrix products, arithmetic and copies ran while one was open for 0% of the time, Pallas kernels for 0%

profile of v1, /device:TPU:0, one launch (start us, length us, event | category | flops | bytes accessed | tf_op | source)
XLA Modules:
  0.0 98.8 jit_solution(15305990217651664385)
XLA Ops:
  2.1 2.3 %copy-done = f32[9,9,8192]{2,1,0:T(8,128)S(1)} copy-done((f32[9,9,8192]{2,1,0:T(8,128)S(1)}, f32[9,9,8192]{2,1,0:T(8,128)}, u32[]{:S(2)}) %copy-start) | copy-done | bytes 2654232
  4.5 2.3 %copy-done.1 = f32[9,9,8192]{2,1,0:T(8,128)S(1)} copy-done((f32[9,9,8192]{2,1,0:T(8,128)S(1)}, f32[9,9,8192]{2,1,0:T(8,128)}, u32[]{:S(2)}) %copy-start.1) | copy-done | bytes 2654232
  8.8 11.3 %start.1 = (bf16[64,144,768]{2,1,0:T(8,128)(2,1)S(1)}, f32[45,64,128]{2,1,0:T(8,128)S(1)}, f32[45,64,128]{2,1,0:T(8,128)S(1)}, f32[6,64,128]{2,1,0:T(8,128)S(1)}...) custom-call(f32[9,8192]{1,0:T(8,128)S(1)} %copy-done.2, ...), custom_call_target="tpu_custom_call" | custom-call | tf_op jit(solution)/shard_map/start/pallas_call | solution.py:417
  21.8 3.8 %collective-permute-start.3 = (bf16[64,256]{1,0:T(8,128)(2,1)S(1)}, bf16[64,256]{1,0:T(8,128)(2,1)S(1)}, u32[]{:S(2)}, u32[]{:S(2)}) collective-permute-start(bf16[64,256]{1,0:T(8,128)(2,1)S(1)} %pair.3.refs_0_), channel_id=1, source_target_pairs={{0,24},{4,28},{8,16},{12,20},{16,8},{20,12},{24,0},{28,4},{1,25},{... | collective-permute-start | bytes 98312 | tf_op jit(solution)/shard_map/ppermute | solution.py:429
  27.5 2.0 %collective-permute-done.2.refs_2_ = bf16[64,256]{1,0:T(8,128)(2,1)S(1)} collective-permute-done((bf16[64,256]{1,0:T(8,128)(2,1)S(1)}, bf16[64,256]{1,0:T(8,128)(2,1)S(1)}, u32[]{:S(2)}, u32[]{:S(2)}) %collective-permute-start.2) | collective-permute-done | bytes 32800 | tf_op jit(solution)/shard_map/ppermute | solution.py:429
  30.0 4.3 %points.3 = (bf16[160,256]{1,0:T(8,128)(2,1)S(1)}, f32[64,192]{1,0:T(8,128)S(1)}, f32[8,128]{1,0:T(8,128)S(1)}) custom-call(bf16[64,256]{1,0:T(8,128)(2,1)S(1)} %pair.3.refs_0_, bf16[64,256]{1,0:T(8,128)(2,1)S(1)} %collective-permute-done.1.refs_1_, bf16[64,256]{1,0:T(8,128)(2,1)S(1)} %collective-permute-done.2.refs_2_, ...), custom_call_target="tpu_custom_call" | custom-call | tf_op jit(solution)/shard_map/points/pallas_call | solution.py:417
  34.3 3.7 %collective-permute-start.6 = (bf16[160,256]{1,0:T(8,128)(2,1)S(1)}, bf16[160,256]{1,0:T(8,128)(2,1)S(1)}, u32[]{:S(2)}, u32[]{:S(2)}) collective-permute-start(bf16[160,256]{1,0:T(8,128)(2,1)S(1)} %get-tuple-element.35.refs_0_), channel_id=1, source_target_pairs={{0,3},{1,2},{2,1},{3,0},{4,7},{5,6},{6,5},{7,4},{8,11},{9,10},{10,... | collective-permute-start | bytes 245768 | tf_op jit(solution)/shard_map/ppermute | solution.py:429
  38.8 1.9 %collective-permute-done.6.refs_3_ = bf16[160,256]{1,0:T(8,128)(2,1)S(1)} collective-permute-done((bf16[160,256]{1,0:T(8,128)(2,1)S(1)}, bf16[160,256]{1,0:T(8,128)(2,1)S(1)}, u32[]{:S(2)}, u32[]{:S(2)}) %collective-permute-start.6) | collective-permute-done | bytes 81952 | tf_op jit(solution)/shard_map/ppermute | solution.py:429
  40.6 3.3 %collective-permute-done.5.refs_2_ = bf16[160,256]{1,0:T(8,128)(2,1)S(1)} collective-permute-done((bf16[160,256]{1,0:T(8,128)(2,1)S(1)}, bf16[160,256]{1,0:T(8,128)(2,1)S(1)}, u32[]{:S(2)}, u32[]{:S(2)}) %collective-permute-start.5) | collective-permute-done | bytes 81952 | tf_op jit(solution)/shard_map/ppermute | solution.py:429
  43.9 4.4 %camera.2 = (bf16[64,256]{1,0:T(8,128)(2,1)S(1)}, f32[9,64,128]{2,1,0:T(8,128)S(1)}, f32[9,64,128]{2,1,0:T(8,128)S(1)}, f32[9,64,128]{2,1,0:T(8,128)S(1)}, f32[9,64,128]{2,1,0:T(8,128)S(1)}) custom-call(bf16[160,256]{1,0:T(8,128)(2,1)S(1)} %get-tuple-element.35.refs_0_, bf16[160,256]{1,0:T(8,128)(2,1)S(1)} %collective-permute-done.4.refs_1_, ...), custom_call_target="tpu_custom_call" | custom-call | tf_op jit(solution)/shard_map/camera/pallas_call | solution.py:417
  49.8 1.8 %collective-permute-start.10 = (bf16[64,256]{1,0:T(8,128)(2,1)S(1)}, bf16[64,256]{1,0:T(8,128)(2,1)S(1)}, u32[]{:S(2)}, u32[]{:S(2)}) collective-permute-start(bf16[64,256]{1,0:T(8,128)(2,1)S(1)} %pair.4.refs_0_), channel_id=1, source_target_pairs={{0,24},{4,28},{8,16},{12,20},{16,8},{20,12},{24,0},{28,4},{1,25},{... | collective-permute-start | bytes 98312 | tf_op jit(solution)/shard_map/ppermute | solution.py:429
  56.0 4.5 %points.4 = (bf16[160,256]{1,0:T(8,128)(2,1)S(1)}, f32[64,192]{1,0:T(8,128)S(1)}, f32[8,128]{1,0:T(8,128)S(1)}) custom-call(bf16[64,256]{1,0:T(8,128)(2,1)S(1)} %pair.4.refs_0_, bf16[64,256]{1,0:T(8,128)(2,1)S(1)} %collective-permute-done.8.refs_1_, bf16[64,256]{1,0:T(8,128)(2,1)S(1)} %collective-permute-done.9.refs_2_, ...), custom_call_target="tpu_custom_call" | custom-call | tf_op jit(solution)/shard_map/points/pallas_call | solution.py:417
  60.6 2.3 %collective-permute-start.13 = (bf16[160,256]{1,0:T(8,128)(2,1)S(1)}, bf16[160,256]{1,0:T(8,128)(2,1)S(1)}, u32[]{:S(2)}, u32[]{:S(2)}) collective-permute-start(bf16[160,256]{1,0:T(8,128)(2,1)S(1)} %get-tuple-element.44.refs_0_), channel_id=1, source_target_pairs={{0,3},{1,2},{2,1},{3,0},{4,7},{5,6},{6,5},{7,4},{8,11},{9,10},{10,... | collective-permute-start | bytes 245768 | tf_op jit(solution)/shard_map/ppermute | solution.py:429
  62.9 2.1 %collective-permute-start.11 = (bf16[160,256]{1,0:T(8,128)(2,1)S(1)}, bf16[160,256]{1,0:T(8,128)(2,1)S(1)}, u32[]{:S(2)}, u32[]{:S(2)}) collective-permute-start(bf16[160,256]{1,0:T(8,128)(2,1)S(1)} %get-tuple-element.44.refs_0_), channel_id=1, source_target_pairs={{0,1},{1,0},{2,3},{3,2},{4,5},{5,4},{6,7},{7,6},{8,9},{9,8},{10,11... | collective-permute-start | bytes 245768 | tf_op jit(solution)/shard_map/ppermute | solution.py:429
  65.0 2.7 %collective-permute-done.13.refs_3_ = bf16[160,256]{1,0:T(8,128)(2,1)S(1)} collective-permute-done((bf16[160,256]{1,0:T(8,128)(2,1)S(1)}, bf16[160,256]{1,0:T(8,128)(2,1)S(1)}, u32[]{:S(2)}, u32[]{:S(2)}) %collective-permute-start.13) | collective-permute-done | bytes 81952 | tf_op jit(solution)/shard_map/ppermute | solution.py:429
  67.7 2.1 %collective-permute-done.12.refs_2_ = bf16[160,256]{1,0:T(8,128)(2,1)S(1)} collective-permute-done((bf16[160,256]{1,0:T(8,128)(2,1)S(1)}, bf16[160,256]{1,0:T(8,128)(2,1)S(1)}, u32[]{:S(2)}, u32[]{:S(2)}) %collective-permute-start.12) | collective-permute-done | bytes 81952 | tf_op jit(solution)/shard_map/ppermute | solution.py:429
  69.9 4.6 %camera.3 = (bf16[64,256]{1,0:T(8,128)(2,1)S(1)}, f32[9,64,128]{2,1,0:T(8,128)S(1)}, f32[9,64,128]{2,1,0:T(8,128)S(1)}, f32[9,64,128]{2,1,0:T(8,128)S(1)}, f32[9...) custom-call(bf16[160,256]{1,0:T(8,128)(2,1)S(1)} %get-tuple-element.44.refs_0_, ...), custom_call_target="tpu_custom_call" | custom-call | tf_op jit(solution)/shard_map/camera/pallas_call | solution.py:417
  76.0 2.1 %collective-permute-start.17 = (bf16[64,256]{1,0:T(8,128)(2,1)S(1)}, bf16[64,256]{1,0:T(8,128)(2,1)S(1)}, u32[]{:S(2)}, u32[]{:S(2)}) collective-permute-start(bf16[64,256]{1,0:T(8,128)(2,1)S(1)} %pair.5.refs_0_), channel_id=1, source_target_pairs={{0,24},{4,28},{8,16},{12,20},{16,8},{20,12},{24,0},{28,4},{1,25},{... | collective-permute-start | bytes 98312 | tf_op jit(solution)/shard_map/ppermute | solution.py:429
  82.3 5.1 %points.5 = (bf16[160,256]{1,0:T(8,128)(2,1)S(1)}, f32[64,192]{1,0:T(8,128)}, f32[8,128]{1,0:T(8,128)S(1)}) custom-call(bf16[64,256]{1,0:T(8,128)(2,1)S(1)} %pair.5.refs_0_, bf16[64,256]{1,0:T(8,128)(2,1)S(1)} %collective-permute-done.15.refs_1_, bf16[64,256]{1,0:T(8,128)(2,1)S(1)} %collective-permute-done.16.refs_2_, ...), custom_call_target="tpu_custom_call" | custom-call | tf_op jit(solution)/shard_map/points/pallas_call | solution.py:417
  87.4 2.2 %collective-permute-start.20 = (bf16[160,256]{1,0:T(8,128)(2,1)S(1)}, bf16[160,256]{1,0:T(8,128)(2,1)S(1)}, u32[]{:S(2)}, u32[]{:S(2)}) collective-permute-start(bf16[160,256]{1,0:T(8,128)(2,1)S(1)} %get-tuple-element.52.refs_0_), channel_id=1, source_target_pairs={{0,3},{1,2},{2,1},{3,0},{4,7},{5,6},{6,5},{7,4},{8,11},{9,10},{10,... | collective-permute-start | bytes 245768 | tf_op jit(solution)/shard_map/ppermute | solution.py:429
  89.6 2.2 %collective-permute-start.18 = (bf16[160,256]{1,0:T(8,128)(2,1)S(1)}, bf16[160,256]{1,0:T(8,128)(2,1)S(1)}, u32[]{:S(2)}, u32[]{:S(2)}) collective-permute-start(bf16[160,256]{1,0:T(8,128)(2,1)S(1)} %get-tuple-element.52.refs_0_), channel_id=1, source_target_pairs={{0,1},{1,0},{2,3},{3,2},{4,5},{5,4},{6,7},{7,6},{8,9},{9,8},{10,11... | collective-permute-start | bytes 245768 | tf_op jit(solution)/shard_map/ppermute | solution.py:429
  91.8 2.8 %collective-permute-done.20.refs_3_ = bf16[160,256]{1,0:T(8,128)(2,1)S(1)} collective-permute-done((bf16[160,256]{1,0:T(8,128)(2,1)S(1)}, bf16[160,256]{1,0:T(8,128)(2,1)S(1)}, u32[]{:S(2)}, u32[]{:S(2)}) %collective-permute-start.20) | collective-permute-done | bytes 81952 | tf_op jit(solution)/shard_map/ppermute | solution.py:429
  94.5 1.8 %collective-permute-done.19.refs_2_ = bf16[160,256]{1,0:T(8,128)(2,1)S(1)} collective-permute-done((bf16[160,256]{1,0:T(8,128)(2,1)S(1)}, bf16[160,256]{1,0:T(8,128)(2,1)S(1)}, u32[]{:S(2)}, u32[]{:S(2)}) %collective-permute-start.19) | collective-permute-done | bytes 81952 | tf_op jit(solution)/shard_map/ppermute | solution.py:429
  96.3 2.4 %finish.1 = (f32[9,8192]{1,0:T(8,128)}, f32[9,8192]{1,0:T(8,128)}) custom-call(bf16[160,256]{1,0:T(8,128)(2,1)S(1)} %get-tuple-element.52.refs_0_, bf16[160,256]{1,0:T(8,128)(2,1)S(1)} %collective-permute-done.18.refs_1_, bf16[160,256]{1,0:T(8,128)(2,1)S(1)} %collective-permute-done.19.refs_2_, bf16[160,256]{1,0:T(8,128)(2,1)S(1)} %collective-permute-done.20.refs_3_, ...), custom_call_target="tpu_custom_call" | custom-call | tf_op jit(solution)/shard_map/finish/pallas_call | solution.py:417
  (38 shorter events, 20.0 us)
Async XLA Ops:
  2.1 2.3 %copy-start = (f32[9,9,8192]{2,1,0:T(8,128)S(1)}, f32[9,9,8192]{2,1,0:T(8,128)}, u32[]{:S(2)}) copy-start(f32[9,9,8192]{2,1,0:T(8,128)} %m_hbm.1) | copy-start | bytes 7962628
  4.5 2.3 %copy-start.1 = (f32[9,9,8192]{2,1,0:T(8,128)S(1)}, f32[9,9,8192]{2,1,0:T(8,128)}, u32[]{:S(2)}) copy-start(f32[9,9,8192]{2,1,0:T(8,128)} %c_hbm.1) | copy-start | bytes 7962628
  6.8 1.0 %copy-start.2 = (f32[9,8192]{1,0:T(8,128)S(1)}, f32[9,8192]{1,0:T(8,128)}, u32[]{:S(2)}) copy-start(f32[9,8192]{1,0:T(8,128)} %rhs_hbm.1) | copy-start | bytes 884740
  20.1 1.4 %collective-permute-start = (bf16[64,256]{1,0:T(8,128)(2,1)S(1)}, bf16[64,256]{1,0:T(8,128)(2,1)S(1)}, u32[]{:S(2)}, u32[]{:S(2)}) collective-permute-start(bf16[64,256]{1,0:T(8,128)(2,1)S(1)} %get-tuple-element.31.refs_0_), channel_id=1, source_target_pairs={{0,4},{4,0},{8,12},{12,8},{16,20},{20,16},{24,28},{28,24},{1,5},{5... | collective-permute-start | bytes 98312 | tf_op jit(solution)/shard_map/ppermute | solution.py:429
  21.8 5.7 %collective-permute-start.3 = (bf16[64,256]{1,0:T(8,128)(2,1)S(1)}, bf16[64,256]{1,0:T(8,128)(2,1)S(1)}, u32[]{:S(2)}, u32[]{:S(2)}) collective-permute-start(bf16[64,256]{1,0:T(8,128)(2,1)S(1)} %pair.3.refs_0_), channel_id=1, source_target_pairs={{0,24},{4,28},{8,16},{12,20},{16,8},{20,12},{24,0},{28,4},{1,25},{... | collective-permute-start | bytes 98312 | tf_op jit(solution)/shard_map/ppermute | solution.py:429
  25.6 3.9 %collective-permute-start.2 = (bf16[64,256]{1,0:T(8,128)(2,1)S(1)}, bf16[64,256]{1,0:T(8,128)(2,1)S(1)}, u32[]{:S(2)}, u32[]{:S(2)}) collective-permute-start(bf16[64,256]{1,0:T(8,128)(2,1)S(1)} %pair.3.refs_0_), channel_id=1, source_target_pairs={{0,16},{4,20},{8,24},{12,28},{16,0},{20,4},{24,8},{28,12},{1,17},{... | collective-permute-start | bytes 98312 | tf_op jit(solution)/shard_map/ppermute | solution.py:429
  26.1 3.9 %collective-permute-start.1 = (bf16[64,256]{1,0:T(8,128)(2,1)S(1)}, bf16[64,256]{1,0:T(8,128)(2,1)S(1)}, u32[]{:S(2)}, u32[]{:S(2)}) collective-permute-start(bf16[64,256]{1,0:T(8,128)(2,1)S(1)} %pair.3.refs_0_), channel_id=1, source_target_pairs={{0,8},{4,12},{8,0},{12,4},{16,24},{20,28},{24,16},{28,20},{1,9},{5... | collective-permute-start | bytes 98312 | tf_op jit(solution)/shard_map/ppermute | solution.py:429
  34.3 6.3 %collective-permute-start.6 = (bf16[160,256]{1,0:T(8,128)(2,1)S(1)}, bf16[160,256]{1,0:T(8,128)(2,1)S(1)}, u32[]{:S(2)}, u32[]{:S(2)}) collective-permute-start(bf16[160,256]{1,0:T(8,128)(2,1)S(1)} %get-tuple-element.35.refs_0_), channel_id=1, source_target_pairs={{0,3},{1,2},{2,1},{3,0},{4,7},{5,6},{6,5},{7,4},{8,11},{9,10},{10,... | collective-permute-start | bytes 245768 | tf_op jit(solution)/shard_map/ppermute | solution.py:429
  38.0 5.9 %collective-permute-start.5 = (bf16[160,256]{1,0:T(8,128)(2,1)S(1)}, bf16[160,256]{1,0:T(8,128)(2,1)S(1)}, u32[]{:S(2)}, u32[]{:S(2)}) collective-permute-start(bf16[160,256]{1,0:T(8,128)(2,1)S(1)} %get-tuple-element.35.refs_0_), channel_id=1, source_target_pairs={{0,2},{1,3},{2,0},{3,1},{4,6},{5,7},{6,4},{7,5},{8,10},{9,11},{10,... | collective-permute-start | bytes 245768 | tf_op jit(solution)/shard_map/ppermute | solution.py:429
  38.0 5.9 %collective-permute-start.4 = (bf16[160,256]{1,0:T(8,128)(2,1)S(1)}, bf16[160,256]{1,0:T(8,128)(2,1)S(1)}, u32[]{:S(2)}, u32[]{:S(2)}) collective-permute-start(bf16[160,256]{1,0:T(8,128)(2,1)S(1)} %get-tuple-element.35.refs_0_), channel_id=1, source_target_pairs={{0,1},{1,0},{2,3},{3,2},{4,5},{5,4},{6,7},{7,6},{8,9},{9,8},{10,11... | collective-permute-start | bytes 245768 | tf_op jit(solution)/shard_map/ppermute | solution.py:429
  48.3 1.2 %collective-permute-start.7 = (bf16[64,256]{1,0:T(8,128)(2,1)S(1)}, bf16[64,256]{1,0:T(8,128)(2,1)S(1)}, u32[]{:S(2)}, u32[]{:S(2)}) collective-permute-start(bf16[64,256]{1,0:T(8,128)(2,1)S(1)} %get-tuple-element.42.refs_0_), channel_id=1, source_target_pairs={{0,4},{4,0},{8,12},{12,8},{16,20},{20,16},{24,28},{28,24},{1,5},{5... | collective-permute-start | bytes 98312 | tf_op jit(solution)/shard_map/ppermute | solution.py:429
  49.8 4.9 %collective-permute-start.10 = (bf16[64,256]{1,0:T(8,128)(2,1)S(1)}, bf16[64,256]{1,0:T(8,128)(2,1)S(1)}, u32[]{:S(2)}, u32[]{:S(2)}) collective-permute-start(bf16[64,256]{1,0:T(8,128)(2,1)S(1)} %pair.4.refs_0_), channel_id=1, source_target_pairs={{0,24},{4,28},{8,16},{12,20},{16,8},{20,12},{24,0},{28,4},{1,25},{... | collective-permute-start | bytes 98312 | tf_op jit(solution)/shard_map/ppermute | solution.py:429
  51.6 3.9 %collective-permute-start.9 = (bf16[64,256]{1,0:T(8,128)(2,1)S(1)}, bf16[64,256]{1,0:T(8,128)(2,1)S(1)}, u32[]{:S(2)}, u32[]{:S(2)}) collective-permute-start(bf16[64,256]{1,0:T(8,128)(2,1)S(1)} %pair.4.refs_0_), channel_id=1, source_target_pairs={{0,16},{4,20},{8,24},{12,28},{16,0},{20,4},{24,8},{28,12},{1,17},{... | collective-permute-start | bytes 98312 | tf_op jit(solution)/shard_map/ppermute | solution.py:429
  52.1 3.9 %collective-permute-start.8 = (bf16[64,256]{1,0:T(8,128)(2,1)S(1)}, bf16[64,256]{1,0:T(8,128)(2,1)S(1)}, u32[]{:S(2)}, u32[]{:S(2)}) collective-permute-start(bf16[64,256]{1,0:T(8,128)(2,1)S(1)} %pair.4.refs_0_), channel_id=1, source_target_pairs={{0,8},{4,12},{8,0},{12,4},{16,24},{20,28},{24,16},{28,20},{1,9},{5... | collective-permute-start | bytes 98312 | tf_op jit(solution)/shard_map/ppermute | solution.py:429
  60.6 7.2 %collective-permute-start.13 = (bf16[160,256]{1,0:T(8,128)(2,1)S(1)}, bf16[160,256]{1,0:T(8,128)(2,1)S(1)}, u32[]{:S(2)}, u32[]{:S(2)}) collective-permute-start(bf16[160,256]{1,0:T(8,128)(2,1)S(1)} %get-tuple-element.44.refs_0_), channel_id=1, source_target_pairs={{0,3},{1,2},{2,1},{3,0},{4,7},{5,6},{6,5},{7,4},{8,11},{9,10},{10,... | collective-permute-start | bytes 245768 | tf_op jit(solution)/shard_map/ppermute | solution.py:429
  62.9 7.0 %collective-permute-start.12 = (bf16[160,256]{1,0:T(8,128)(2,1)S(1)}, bf16[160,256]{1,0:T(8,128)(2,1)S(1)}, u32[]{:S(2)}, u32[]{:S(2)}) collective-permute-start(bf16[160,256]{1,0:T(8,128)(2,1)S(1)} %get-tuple-element.44.refs_0_), channel_id=1, source_target_pairs={{0,2},{1,3},{2,0},{3,1},{4,6},{5,7},{6,4},{7,5},{8,10},{9,11},{10,... | collective-permute-start | bytes 245768 | tf_op jit(solution)/shard_map/ppermute | solution.py:429
  62.9 7.0 %collective-permute-start.11 = (bf16[160,256]{1,0:T(8,128)(2,1)S(1)}, bf16[160,256]{1,0:T(8,128)(2,1)S(1)}, u32[]{:S(2)}, u32[]{:S(2)}) collective-permute-start(bf16[160,256]{1,0:T(8,128)(2,1)S(1)} %get-tuple-element.44.refs_0_), channel_id=1, source_target_pairs={{0,1},{1,0},{2,3},{3,2},{4,5},{5,4},{6,7},{7,6},{8,9},{9,8},{10,11... | collective-permute-start | bytes 245768 | tf_op jit(solution)/shard_map/ppermute | solution.py:429
  74.5 1.2 %collective-permute-start.14 = (bf16[64,256]{1,0:T(8,128)(2,1)S(1)}, bf16[64,256]{1,0:T(8,128)(2,1)S(1)}, u32[]{:S(2)}, u32[]{:S(2)}) collective-permute-start(bf16[64,256]{1,0:T(8,128)(2,1)S(1)} %get-tuple-element.50.refs_0_), channel_id=1, source_target_pairs={{0,4},{4,0},{8,12},{12,8},{16,20},{20,16},{24,28},{28,24},{1,5},{5... | collective-permute-start | bytes 98312 | tf_op jit(solution)/shard_map/ppermute | solution.py:429
  76.0 4.8 %collective-permute-start.17 = (bf16[64,256]{1,0:T(8,128)(2,1)S(1)}, bf16[64,256]{1,0:T(8,128)(2,1)S(1)}, u32[]{:S(2)}, u32[]{:S(2)}) collective-permute-start(bf16[64,256]{1,0:T(8,128)(2,1)S(1)} %pair.5.refs_0_), channel_id=1, source_target_pairs={{0,24},{4,28},{8,16},{12,20},{16,8},{20,12},{24,0},{28,4},{1,25},{... | collective-permute-start | bytes 98312 | tf_op jit(solution)/shard_map/ppermute | solution.py:429
  78.1 3.9 %collective-permute-start.16 = (bf16[64,256]{1,0:T(8,128)(2,1)S(1)}, bf16[64,256]{1,0:T(8,128)(2,1)S(1)}, u32[]{:S(2)}, u32[]{:S(2)}) collective-permute-start(bf16[64,256]{1,0:T(8,128)(2,1)S(1)} %pair.5.refs_0_), channel_id=1, source_target_pairs={{0,16},{4,20},{8,24},{12,28},{16,0},{20,4},{24,8},{28,12},{1,17},{... | collective-permute-start | bytes 98312 | tf_op jit(solution)/shard_map/ppermute | solution.py:429
  78.4 3.9 %collective-permute-start.15 = (bf16[64,256]{1,0:T(8,128)(2,1)S(1)}, bf16[64,256]{1,0:T(8,128)(2,1)S(1)}, u32[]{:S(2)}, u32[]{:S(2)}) collective-permute-start(bf16[64,256]{1,0:T(8,128)(2,1)S(1)} %pair.5.refs_0_), channel_id=1, source_target_pairs={{0,8},{4,12},{8,0},{12,4},{16,24},{20,28},{24,16},{28,20},{1,9},{5... | collective-permute-start | bytes 98312 | tf_op jit(solution)/shard_map/ppermute | solution.py:429
  87.4 7.2 %collective-permute-start.20 = (bf16[160,256]{1,0:T(8,128)(2,1)S(1)}, bf16[160,256]{1,0:T(8,128)(2,1)S(1)}, u32[]{:S(2)}, u32[]{:S(2)}) collective-permute-start(bf16[160,256]{1,0:T(8,128)(2,1)S(1)} %get-tuple-element.52.refs_0_), channel_id=1, source_target_pairs={{0,3},{1,2},{2,1},{3,0},{4,7},{5,6},{6,5},{7,4},{8,11},{9,10},{10,... | collective-permute-start | bytes 245768 | tf_op jit(solution)/shard_map/ppermute | solution.py:429
  89.6 6.7 %collective-permute-start.19 = (bf16[160,256]{1,0:T(8,128)(2,1)S(1)}, bf16[160,256]{1,0:T(8,128)(2,1)S(1)}, u32[]{:S(2)}, u32[]{:S(2)}) collective-permute-start(bf16[160,256]{1,0:T(8,128)(2,1)S(1)} %get-tuple-element.52.refs_0_), channel_id=1, source_target_pairs={{0,2},{1,3},{2,0},{3,1},{4,6},{5,7},{6,4},{7,5},{8,10},{9,11},{10,... | collective-permute-start | bytes 245768 | tf_op jit(solution)/shard_map/ppermute | solution.py:429
  89.6 6.7 %collective-permute-start.18 = (bf16[160,256]{1,0:T(8,128)(2,1)S(1)}, bf16[160,256]{1,0:T(8,128)(2,1)S(1)}, u32[]{:S(2)}, u32[]{:S(2)}) collective-permute-start(bf16[160,256]{1,0:T(8,128)(2,1)S(1)} %get-tuple-element.52.refs_0_), channel_id=1, source_target_pairs={{0,1},{1,0},{2,3},{3,2},{4,5},{5,4},{6,7},{7,6},{8,9},{9,8},{10,11... | collective-permute-start | bytes 245768 | tf_op jit(solution)/shard_map/ppermute | solution.py:429
  (1 other events, 0.9 us)

commit v2 on v1

--- a/solution.py
+++ b/solution.py
@@ -15,6 +15,11 @@
 HBM = pl.BlockSpec(memory_space=pltpu.HBM)
 NT = (((1,), (1,)), ((), ()))
 FETCHES = 8
+TAIL = 8
+
+
+def in_hbm(value):
+    return pltpu.with_memory_space_constraint(value, pltpu.HBM)
 
 
 def iota(shape, dim):
@@ -68,9 +73,10 @@
     ]
 
 
-def tile_onehot(row_a, row_q, tiles, planes):
-    column = jnp.where(row_a >= 0, row_q * planes + row_a, -1.0).astype(jnp.int32)
-    return jnp.where(iota((tiles, column.shape[1]), 0) == column, 1.0, 0.0).astype(BF16)
+def tile_onehot(rows, tiles, planes):
+    row_a, row_q = rows[0:1, :], rows[1:2, :]
+    at = jnp.where(row_a >= 0, row_q * planes + row_a, -1.0).astype(jnp.int32)
+    return jnp.where(iota((tiles, at.shape[1]), 0) == at, 1.0, 0.0).astype(BF16)
 
 
 def to_tiles(z_ref, zt_ref):
@@ -93,21 +99,18 @@
     rows_ref[...] = jnp.dot(zt_ref[...], onehot, preferred_element_type=F32).T
 
 
-def forward_pairs(e_ref, rows_ref, part_ref, first, count, unroll):
+def forward_pairs(e_ref, rows_ref, part_ref, pairs):
     sub = iota((8, rows_ref.shape[1]), 0)
-
-    def body(pair, carry):
-        rows = rows_ref[pl.ds(pl.multiple_of(pair * 8, 8), 8), :]
+    for pair in pairs:
+        at = pl.ds(8 * pair, 8)
+        rows = rows_ref[at, :]
         top = jnp.where(sub < 4, rows, 0.0).astype(BF16)
         low = jnp.where(sub >= 4, rows, 0.0).astype(BF16)
         part = jnp.dot(top, e_ref[2 * pair], preferred_element_type=F32) + jnp.dot(
             low, e_ref[2 * pair + 1], preferred_element_type=F32
         )
-        for i in range(6):
-            part_ref[i, pl.ds(pl.multiple_of(pair * 8, 8), 8), :] = part[:, 128 * i : 128 * i + 128]
-        return carry
-
-    lax.fori_loop(first, first + count, body, 0, unroll=unroll)
+        for i in range(part_ref.shape[0]):
+            part_ref[i, at, :] = part[:, 128 * i : 128 * i + 128]
 
 
 def forward_sum(part_ref, count):
@@ -119,7 +122,7 @@
     return even[:, :192] + odd[:, 64:]
 
 
-def backward(e_ref, y, yc_ref, c_ref, unroll):
+def backward(e_ref, y, yc_ref, c_ref):
     count = e_ref.shape[0]
     wide = [jnp.concatenate(pair, axis=1) for pair in ((y[0], y[1]), (y[2], y[0]), (y[1], y[2]))]
     for i in range(6):
@@ -127,104 +130,86 @@
     row, col = iota((8, 768), 0), iota((8, 768), 1)
     masks = [(col >= 192 * (row - r)) & (col < 192 * (row - r) + 192) for r in (0, 4)]
 
-    def body(pair, carry):
+    for pair in range(count // 2):
         part = None
         for k in range(2):
             wide_row = jnp.broadcast_to(yc_ref[pl.ds(2 * pair + k, 1), :], (8, 768))
             lhs = jnp.where(masks[k], wide_row, 0.0).astype(BF16)
             one = lax.dot_general(lhs, e_ref[2 * pair + k], NT, preferred_element_type=F32)
             part = one if part is None else part + one
-        c_ref[pl.ds(pl.multiple_of(pair * 8, 8), 8), :] = part
-        return carry
-
-    lax.fori_loop(0, count // 2, body, 0, unroll=unroll)
+        c_ref[pl.ds(8 * pair, 8), :] = part
 
 
 def start_kernel(
-    rhs_hbm, m_hbm, c_hbm, e_hbm, v_hbm, index_ref, count_ref,
+    rhs_hbm, m_hbm, c_hbm, e_hbm, v_hbm, index_hbm, count_hbm,
     e_ref, m_ref, c_ref, v_ref, r_ref, z_ref, cz_ref, slot_ref, msg_ref,
-    rn, mn, m8, cn, c8, vn, split, vrow, zt_ref, rows_ref, part_ref, sems, e_sems,
+    rn, mn, m8, cn, c8, vn, index_ref, count_ref, split, vrow, zt_ref, rows_ref, part_ref, sems, e_sems,
 ):
     planes, count = r_ref.shape[1], e_ref.shape[0]
     step = count // FETCHES
     inner = pl.ds(0, 8)
-    copies = [
-        pltpu.make_async_copy(src, dst, sems.at[n])
-        for n, (src, dst) in enumerate(
-            (
-                (rhs_hbm, rn),
-                (m_hbm.at[inner, inner], mn),
-                (m_hbm.at[8], m8),
-                (c_hbm.at[inner, inner], cn),
-                (c_hbm.at[8], c8),
-                (v_hbm, vn),
-            )
-        )
-    ]
-    for copy in copies:
-        copy.start()
 
     def fetch(n):
         part = pl.ds(n * step, step)
         return pltpu.make_async_copy(e_hbm.at[part], e_ref.at[part], e_sems.at[n])
 
-    for n in range(FETCHES):
-        fetch(n).start()
-
-    def split_rows(src, buffer):
-        def body(a, carry):
-            lanes = pl.ds(pl.multiple_of(a * 128, 128), 128)
-            buffer[pl.ds(pl.multiple_of(a * 8, 8), 8), :] = src[inner, lanes]
-            return carry
-
-        lax.fori_loop(0, planes, body, 0, unroll=16)
-
-    def split_last(src, store):
-        def body(a, carry):
-            lanes = pl.ds(pl.multiple_of(a * 128, 128), 128)
-            store(a, src[pl.ds(8, 1), lanes])
-            return carry
-
-        lax.fori_loop(0, planes, body, 0, unroll=16)
+    def copy(n, src, dst):
+        return pltpu.make_async_copy(src, dst, sems.at[n])
+
+    indices = [copy(0, index_hbm, index_ref), copy(1, count_hbm, count_ref)]
+    rhs = [copy(2, rhs_hbm, rn)]
+    precond = [copy(3, m_hbm.at[inner, inner], mn), copy(4, m_hbm.at[8], m8)]
+    camera = [copy(5, c_hbm.at[inner, inner], cn), copy(6, c_hbm.at[8], c8)]
+    inverse = [copy(7, v_hbm, vn)]
+    early = [fetch(n) for n in range(FETCHES // 2)]
+    late = [fetch(n) for n in range(FETCHES // 2, FETCHES)]
+    for one in rhs + precond + indices + early + camera + inverse + late:
+        one.start()
+
+    def wait(copies):
+        for one in copies:
+            one.wait()
+
+    def split_rows(src, buffer, used):
+        for a in range(src.shape[1] // 128):
+            buffer[8 * a : 8 * a + used, :] = src[0:used, 128 * a : 128 * a + 128]
+
+    def split_last(src, out_ref, at):
+        for a in range(planes):
+            out_ref[at, a : a + 1, :] = src[8:9, 128 * a : 128 * a + 128]
 
     def split_matrix(inner_ref, last_ref, out_ref):
         for i in range(9):
             buffer = split.at[i % 2]
-            split_rows(inner_ref.at[i] if i < 8 else last_ref, buffer)
+            split_rows(inner_ref.at[i] if i < 8 else last_ref, buffer, 8)
             for j in range(i if i < 8 else 0, 8):
                 out_ref[sym(9, i, j)] = buffer[pl.ds(j, planes, 8), :]
-
-        def store(a, row):
-            out_ref[sym(9, 8, 8), pl.ds(a, 1), :] = row
-
-        split_last(last_ref, store)
-
-    slots = index_ref.shape[1]
+        split_last(last_ref, out_ref, sym(9, 8, 8))
+
+    wait(rhs)
+    split_rows(rn, split.at[0], 8)
+    for j in range(8):
+        r_ref[j] = split[0, pl.ds(j, planes, 8), :]
+    split_last(rn, r_ref, 8)
+
+    wait(indices)
+    slots = index_ref.shape[0]
+    width = count * slots
     index = index_ref[...]
-    used = iota(index.shape, 1) < count_ref[...]
-    spread = jnp.where(iota((count, count * slots), 1) // slots == iota((count, count * slots), 0), 1.0, 0.0)
-    mine = iota((8, count * slots), 1) % slots == iota((8, count * slots), 0)
-    pad = jnp.zeros((count, 128 - slots), F32)
+    used = iota(index.shape, 0) < count_ref[...]
+    spread = jnp.where(iota((count, width), 1) // slots == iota((count, width), 0), 1.0, 0.0)
+    mine = iota((8, width), 1) % slots == iota((8, width), 0)
+    pad = jnp.zeros((8 - slots, count), F32)
     slot_rows = []
     for part in (jnp.where(used, index // 8, -1), index % 8):
-        turned = jnp.concatenate([part.astype(F32), pad], axis=1).T[0:8, :]
-        moved = jnp.dot(turned.astype(BF16), spread.astype(BF16), preferred_element_type=F32)
+        padded = jnp.concatenate([part.astype(F32), pad], axis=0).astype(BF16)
+        moved = jnp.dot(padded, spread.astype(BF16), preferred_element_type=F32)
         slot_rows.append(jnp.sum(jnp.where(mine, moved, 0.0), axis=0, keepdims=True))
-    row = iota((8, count * slots), 0)
+    row = iota((8, width), 0)
     slot_ref[...] = jnp.where(row == 0, slot_rows[0], jnp.where(row == 1, slot_rows[1], 0.0))
-    onehot = tile_onehot(slot_rows[0], slot_rows[1], 8 * planes, planes)
-
-    copies[0].wait()
-    split_rows(rn, split.at[0])
-    for j in range(8):
-        r_ref[j] = split[0, pl.ds(j, planes, 8), :]
-
-    def store_last(a, value):
-        r_ref[8, pl.ds(a, 1), :] = value
-
-    split_last(rn, store_last)
-    copies[1].wait()
-    copies[2].wait()
+    onehot = tile_onehot(slot_ref[...], 8 * planes, planes)
+
+    wait(precond)
     split_matrix(mn, m8, m_ref)
 
     def precondition(g, inner_sum):
@@ -236,12 +221,18 @@
         return inner_sum + tree_sum([a * b for a, b in zip(r, z)])
 
     zero = jnp.zeros((8, 128), F32)
-    inner_sum = lax.fori_loop(0, planes // 8, precondition, zero)
+    inner_sum = lax.fori_loop(0, planes // 8, precondition, zero, unroll=True)
     to_tiles(z_ref, zt_ref)
     gather_rows(zt_ref, onehot, rows_ref)
 
-    copies[3].wait()
-    copies[4].wait()
+    def forward_chunk(n, one):
+        one.wait()
+        forward_pairs(e_ref, rows_ref, part_ref, range(n * (step // 2), (n + 1) * (step // 2)))
+
+    for n, one in enumerate(early):
+        forward_chunk(n, one)
+
+    wait(camera)
     split_matrix(cn, c8, c_ref)
 
     def apply_camera(g, curve):
@@ -252,31 +243,21 @@
             cz_ref[j, rows, :] = cz[j]
         return curve + tree_sum([a * b for a, b in zip(z, cz)])
 
-    curve = lax.fori_loop(0, planes // 8, apply_camera, zero)
-
-    copies[5].wait()
+    curve = lax.fori_loop(0, planes // 8, apply_camera, zero, unroll=True)
+
+    wait(inverse)
     half = vrow.shape[0]
     for i in range(3):
+        split_rows(vn.at[i], split.at[i % 2], 3)
         for j in range(i, 3):
-
-            def body(u, carry):
-                lanes = pl.ds(pl.multiple_of(u * 128, 128), 128)
-                vrow[pl.ds(u, 1), :] = vn[i, j : j + 1, lanes]
-                return carry
-
-            lax.fori_loop(0, half, body, 0, unroll=16)
-            plane = vrow[...]
+            plane = split[i % 2, pl.ds(j, half, 8), :]
             v_ref[sym(3, i, j), pl.ds(0, half, 2), :] = plane
             v_ref[sym(3, i, j), pl.ds(1, half, 2), :] = jnp.concatenate(
                 [plane[:, 64:], plane[:, :64]], axis=1
             )
 
-    def chunk(n, carry):
-        fetch(n).wait()
-        forward_pairs(e_ref, rows_ref, part_ref, n * (step // 2), step // 2, True)
-        return carry
-
-    lax.fori_loop(0, FETCHES, chunk, 0)
+    for n, one in enumerate(late):
+        forward_chunk(len(early) + n, one)
     scalars = scalar_lanes([total(inner_sum), total(curve), jnp.zeros((1, 1), F32)], count)
     msg_ref[...] = jnp.concatenate([forward_sum(part_ref, count), scalars], axis=1).astype(BF16)
 
@@ -307,15 +288,15 @@
     p = [point_sum[:, 64 * i : 64 * i + 64] for i in range(3)]
     y = [tree_sum([v_ref[sym(3, i, j)][:, :64] * p[j] for j in range(3)]) for i in range(3)]
     taken = total(tree_sum([a * b for a, b in zip(p, y)]))
-    backward(e_ref, y, yc_ref, c_ref, 16)
+    backward(e_ref, y, yc_ref, c_ref)
     rows = c_ref.shape[1]
     msg_ref[0:rows, :] = c_ref[...].T.astype(BF16)
     width = msg_ref.shape[1]
-    row = iota((16, width), 0)
-    tail = jnp.zeros((16, width), F32)
+    row = iota((TAIL, width), 0)
+    tail = jnp.zeros((TAIL, width), F32)
     for at, value in enumerate([slot_ref[0:1, :], slot_ref[1:2, :], *pieces(taken)]):
         tail = jnp.where(row == at, value, tail)
-    msg_ref[rows : rows + 16, :] = tail.astype(BF16)
+    msg_ref[rows : rows + TAIL, :] = tail.astype(BF16)
 
 
 def camera_kernel(parts, first, last, *refs):
@@ -333,15 +314,15 @@
             d_ref, cd_ref, *refs = refs
         all_ref, t4_ref, zt_ref, rows_ref, part_ref = refs
     planes = z_ref.shape[1]
-    rows_all = all_ref.shape[1] - 16
+    rows_all = all_ref.shape[1] - TAIL
     me = lax.axis_index("pts")
     for k in range(parts):
         all_ref[me ^ k] = msgs[k][...]
     taken, tiles = [], []
     for k in range(parts):
-        tail = all_ref[k, rows_all : rows_all + 16, :].astype(F32)
+        tail = all_ref[k, rows_all : rows_all + TAIL, :].astype(F32)
         taken.append(tail[2:3, 0:1] + tail[3:4, 0:1] + tail[4:5, 0:1])
-        onehot = tile_onehot(tail[0:1, :], tail[1:2, :], 8 * planes, planes)
+        onehot = tile_onehot(tail, 8 * planes, planes)
         tiles.append(
             lax.dot_general(all_ref[k, 0:rows_all, :], onehot, NT, preferred_element_type=F32)
         )
@@ -376,7 +357,7 @@
         pairs = (zip(r, z), zip(z, cz), zip(z, cd))
         return tuple(s + tree_sum([a * b for a, b in p]) for s, p in zip(sums, pairs))
 
-    sums = lax.fori_loop(0, planes // 8, update, (jnp.zeros((8, 128), F32),) * 3)
+    sums = lax.fori_loop(0, planes // 8, update, (jnp.zeros((8, 128), F32),) * 3, unroll=True)
     if last:
         for src, dst in ((sol_ref, sol_out), (res_ref, res_out)):
             for j in range(8):
@@ -391,10 +372,10 @@
             lax.fori_loop(0, planes, body, 0, unroll=16)
         return
     to_tiles(zn_ref, zt_ref)
-    onehot = tile_onehot(slot_ref[0:1, :], slot_ref[1:2, :], 8 * planes, planes)
+    onehot = tile_onehot(slot_ref[...], 8 * planes, planes)
     gather_rows(zt_ref, onehot, rows_ref)
     count = e_ref.shape[0]
-    forward_pairs(e_ref, rows_ref, part_ref, 0, count // 2, 16)
+    forward_pairs(e_ref, rows_ref, part_ref, range(count // 2))
     scalars = scalar_lanes([total(s) for s in sums], count)
     msg_ref[...] = jnp.concatenate([forward_sum(part_ref, count), scalars], axis=1).astype(BF16)
 
@@ -442,8 +423,13 @@
             shape((8, width), F32),
             message,
         ],
-        (rhs, precond, cam_block, coupling, point_inverse, tile_index, tile_count),
-        in_specs=[HBM] * 5 + [VMEM] * 2,
+        [
+            in_hbm(value)
+            for value in (
+                rhs, precond, cam_block, coupling, point_inverse, tile_index.T, tile_count.T,
+            )
+        ],
+        in_specs=[HBM] * 7,
         scratch=[
             pltpu.VMEM((size, cams), F32),
             pltpu.VMEM((8, 8, cams), F32),
@@ -451,12 +437,14 @@
             pltpu.VMEM((8, 8, cams), F32),
             pltpu.VMEM((size, cams), F32),
             pltpu.VMEM((3, 3, points), F32),
+            pltpu.VMEM((slots, count), jnp.int32),
+            pltpu.VMEM((1, count), jnp.int32),
             pltpu.VMEM((2, 8 * planes, 128), F32),
             pltpu.VMEM((points // 128, 128), F32),
             zt_scratch,
             rows_scratch,
             part_scratch,
-            pltpu.SemaphoreType.DMA((6,)),
+            pltpu.SemaphoreType.DMA((8,)),
             pltpu.SemaphoreType.DMA((FETCHES,)),
         ],
         megabytes=16,
@@ -473,7 +461,7 @@
         tile_message, point_sum, scal = call(
             functools.partial(points_kernel, len(parts), first),
             [
-                shape((rows + 16, width), BF16),
+                shape((rows + TAIL, width), BF16),
                 shape((count, 192), F32),
                 shape((8, 128), F32),
             ],
@@ -485,7 +473,7 @@
         parts = exchange(tile_message, "pts", n_pts, range(1, n_pts))
         kernel = functools.partial(camera_kernel, len(parts), first, last)
         common = [
-            pltpu.VMEM((n_pts, rows + 16, width), BF16),
+            pltpu.VMEM((n_pts, rows + TAIL, width), BF16),
             pltpu.VMEM((size, planes, 128), F32),
         ]
         args = (*parts, scal, z, cz, residual, *old_camera)

time: 99.1 us -> 84.3 us (0.85)
  local copies, waits for them, and re-layouts: 8.16 us -> 0 us
  Pallas kernels: 37.4 us -> 31.7 us
    unnamed x10 -> x0, local copies, waits for them, and re-layouts: 8.16 us -> none
    pallas_call x10, Pallas kernels: 37.4 us -> 31.7 us  [call(): pl.pallas_call(kernel, out_shape=outs, in_specs=in_specs or [VMEM] * len(...]
where the time goes in v2:
time: 84.3 us; the launch traced here: 84.2 us
  Pallas kernels  31.7 us (38%)
  waiting for transfers between devices  26.5 us (31%)
  starting transfers between devices  25.3 us (30%)
    pallas_call x10, Pallas kernels, call(): pl.pallas_call(kernel, out_shape=outs, in_specs=in_specs or [VMEM] * len(...  31.7 us
    ppermute x21, waiting for transfers between devices, exchange(): lax.ppermute(value, axis, [(i, i ^ k) for i in range(axis_size)])  26.5 us
    ppermute x21, starting transfers between devices, exchange(): lax.ppermute(value, axis, [(i, i ^ k) for i in range(axis_size)])  25.3 us
  transfers between devices with their start and end apart: 21, of which 18 were waited for; matrix products, arithmetic and copies ran while one was open for 0% of the time, Pallas kernels for 0%

profile of v2, /device:TPU:0, one launch (start us, length us, event | category | flops | bytes accessed | tf_op | source)
XLA Modules:
  0.0 84.2 jit_solution(5840457407559600380)
XLA Ops:
  0.6 8.8 %start.1 = (bf16[64,144,768]{2,1,0:T(8,128)(2,1)S(1)}, f32[45,64,128]{2,1,0:T(8,128)S(1)}, f32[45,64,128]{2,1,0:T(8,128)S(1)}, f32[6,64,128]{2,1,0:T(8,128)S(1)}...) custom-call(f32[9,8192]{1,0:T(8,128)} %rhs_hbm.1, ...), custom_call_target="tpu_custom_call" | custom-call | tf_op jit(solution)/shard_map/start/pallas_call | solution.py:398
  11.1 3.8 %collective-permute-start.3 = (bf16[64,256]{1,0:T(8,128)(2,1)S(1)}, bf16[64,256]{1,0:T(8,128)(2,1)S(1)}, u32[]{:S(2)}, u32[]{:S(2)}) collective-permute-start(bf16[64,256]{1,0:T(8,128)(2,1)S(1)} %pair.3.refs_0_), channel_id=1, source_target_pairs={{0,24},{4,28},{8,16},{12,20},{16,8},{20,12},{24,0},{28,4},{1,25},{... | collective-permute-start | bytes 98312 | tf_op jit(solution)/shard_map/ppermute | solution.py:410
  16.8 2.0 %collective-permute-done.2.refs_2_ = bf16[64,256]{1,0:T(8,128)(2,1)S(1)} collective-permute-done((bf16[64,256]{1,0:T(8,128)(2,1)S(1)}, bf16[64,256]{1,0:T(8,128)(2,1)S(1)}, u32[]{:S(2)}, u32[]{:S(2)}) %collective-permute-start.2) | collective-permute-done | bytes 32800 | tf_op jit(solution)/shard_map/ppermute | solution.py:410
  19.3 4.0 %points.3 = (bf16[152,256]{1,0:T(8,128)(2,1)S(1)}, f32[64,192]{1,0:T(8,128)S(1)}, f32[8,128]{1,0:T(8,128)S(1)}) custom-call(bf16[64,256]{1,0:T(8,128)(2,1)S(1)} %pair.3.refs_0_, bf16[64,256]{1,0:T(8,128)(2,1)S(1)} %collective-permute-done.1.refs_1_, bf16[64,256]{1,0:T(8,128)(2,1)S(1)} %collective-permute-done.2.refs_2_, ...), custom_call_target="tpu_custom_call" | custom-call | tf_op jit(solution)/shard_map/points/pallas_call | solution.py:398
  23.3 3.7 %collective-permute-start.6 = (bf16[152,256]{1,0:T(8,128)(2,1)S(1)}, bf16[152,256]{1,0:T(8,128)(2,1)S(1)}, u32[]{:S(2)}, u32[]{:S(2)}) collective-permute-start(bf16[152,256]{1,0:T(8,128)(2,1)S(1)} %get-tuple-element.35.refs_0_), channel_id=1, source_target_pairs={{0,3},{1,2},{2,1},{3,0},{4,7},{5,6},{6,5},{7,4},{8,11},{9,10},{10,... | collective-permute-start | bytes 233480 | tf_op jit(solution)/shard_map/ppermute | solution.py:410
  27.8 1.8 %collective-permute-done.6.refs_3_ = bf16[152,256]{1,0:T(8,128)(2,1)S(1)} collective-permute-done((bf16[152,256]{1,0:T(8,128)(2,1)S(1)}, bf16[152,256]{1,0:T(8,128)(2,1)S(1)}, u32[]{:S(2)}, u32[]{:S(2)}) %collective-permute-start.6) | collective-permute-done | bytes 77856 | tf_op jit(solution)/shard_map/ppermute | solution.py:410
  29.6 3.1 %collective-permute-done.5.refs_2_ = bf16[152,256]{1,0:T(8,128)(2,1)S(1)} collective-permute-done((bf16[152,256]{1,0:T(8,128)(2,1)S(1)}, bf16[152,256]{1,0:T(8,128)(2,1)S(1)}, u32[]{:S(2)}, u32[]{:S(2)}) %collective-permute-start.5) | collective-permute-done | bytes 77856 | tf_op jit(solution)/shard_map/ppermute | solution.py:410
  32.6 3.5 %camera.2 = (bf16[64,256]{1,0:T(8,128)(2,1)S(1)}, f32[9,64,128]{2,1,0:T(8,128)S(1)}, f32[9,64,128]{2,1,0:T(8,128)S(1)}, f32[9,64,128]{2,1,0:T(8,128)S(1)}, f32[9,64,128]{2,1,0:T(8,128)S(1)}) custom-call(bf16[152,256]{1,0:T(8,128)(2,1)S(1)} %get-tuple-element.35.refs_0_, bf16[152,256]{1,0:T(8,128)(2,1)S(1)} %collective-permute-done.4.refs_1_, ...), custom_call_target="tpu_custom_call" | custom-call | tf_op jit(solution)/shard_map/camera/pallas_call | solution.py:398
  37.7 1.8 %collective-permute-start.10 = (bf16[64,256]{1,0:T(8,128)(2,1)S(1)}, bf16[64,256]{1,0:T(8,128)(2,1)S(1)}, u32[]{:S(2)}, u32[]{:S(2)}) collective-permute-start(bf16[64,256]{1,0:T(8,128)(2,1)S(1)} %pair.4.refs_0_), channel_id=1, source_target_pairs={{0,24},{4,28},{8,16},{12,20},{16,8},{20,12},{24,0},{28,4},{1,25},{... | collective-permute-start | bytes 98312 | tf_op jit(solution)/shard_map/ppermute | solution.py:410
  41.2 1.4 %collective-permute-done.10.refs_3_ = bf16[64,256]{1,0:T(8,128)(2,1)S(1)} collective-permute-done((bf16[64,256]{1,0:T(8,128)(2,1)S(1)}, bf16[64,256]{1,0:T(8,128)(2,1)S(1)}, u32[]{:S(2)}, u32[]{:S(2)}) %collective-permute-start.10) | collective-permute-done | bytes 32800 | tf_op jit(solution)/shard_map/ppermute | solution.py:410
  43.9 4.2 %points.4 = (bf16[152,256]{1,0:T(8,128)(2,1)S(1)}, f32[64,192]{1,0:T(8,128)S(1)}, f32[8,128]{1,0:T(8,128)S(1)}) custom-call(bf16[64,256]{1,0:T(8,128)(2,1)S(1)} %pair.4.refs_0_, bf16[64,256]{1,0:T(8,128)(2,1)S(1)} %collective-permute-done.8.refs_1_, bf16[64,256]{1,0:T(8,128)(2,1)S(1)} %collective-permute-done.9.refs_2_, ...), custom_call_target="tpu_custom_call" | custom-call | tf_op jit(solution)/shard_map/points/pallas_call | solution.py:398
  48.1 2.3 %collective-permute-start.13 = (bf16[152,256]{1,0:T(8,128)(2,1)S(1)}, bf16[152,256]{1,0:T(8,128)(2,1)S(1)}, u32[]{:S(2)}, u32[]{:S(2)}) collective-permute-start(bf16[152,256]{1,0:T(8,128)(2,1)S(1)} %get-tuple-element.44.refs_0_), channel_id=1, source_target_pairs={{0,3},{1,2},{2,1},{3,0},{4,7},{5,6},{6,5},{7,4},{8,11},{9,10},{10,... | collective-permute-start | bytes 233480 | tf_op jit(solution)/shard_map/ppermute | solution.py:410
  50.3 2.2 %collective-permute-start.11 = (bf16[152,256]{1,0:T(8,128)(2,1)S(1)}, bf16[152,256]{1,0:T(8,128)(2,1)S(1)}, u32[]{:S(2)}, u32[]{:S(2)}) collective-permute-start(bf16[152,256]{1,0:T(8,128)(2,1)S(1)} %get-tuple-element.44.refs_0_), channel_id=1, source_target_pairs={{0,1},{1,0},{2,3},{3,2},{4,5},{5,4},{6,7},{7,6},{8,9},{9,8},{10,11... | collective-permute-start | bytes 233480 | tf_op jit(solution)/shard_map/ppermute | solution.py:410
  52.5 2.7 %collective-permute-done.13.refs_3_ = bf16[152,256]{1,0:T(8,128)(2,1)S(1)} collective-permute-done((bf16[152,256]{1,0:T(8,128)(2,1)S(1)}, bf16[152,256]{1,0:T(8,128)(2,1)S(1)}, u32[]{:S(2)}, u32[]{:S(2)}) %collective-permute-start.13) | collective-permute-done | bytes 77856 | tf_op jit(solution)/shard_map/ppermute | solution.py:410
  55.2 1.8 %collective-permute-done.12.refs_2_ = bf16[152,256]{1,0:T(8,128)(2,1)S(1)} collective-permute-done((bf16[152,256]{1,0:T(8,128)(2,1)S(1)}, bf16[152,256]{1,0:T(8,128)(2,1)S(1)}, u32[]{:S(2)}, u32[]{:S(2)}) %collective-permute-start.12) | collective-permute-done | bytes 77856 | tf_op jit(solution)/shard_map/ppermute | solution.py:410
  57.1 3.8 %camera.3 = (bf16[64,256]{1,0:T(8,128)(2,1)S(1)}, f32[9,64,128]{2,1,0:T(8,128)S(1)}, f32[9,64,128]{2,1,0:T(8,128)S(1)}, f32[9,64,128]{2,1,0:T(8,128)S(1)}, f32[9...) custom-call(bf16[152,256]{1,0:T(8,128)(2,1)S(1)} %get-tuple-element.44.refs_0_, ...), custom_call_target="tpu_custom_call" | custom-call | tf_op jit(solution)/shard_map/camera/pallas_call | solution.py:398
  62.3 2.1 %collective-permute-start.17 = (bf16[64,256]{1,0:T(8,128)(2,1)S(1)}, bf16[64,256]{1,0:T(8,128)(2,1)S(1)}, u32[]{:S(2)}, u32[]{:S(2)}) collective-permute-start(bf16[64,256]{1,0:T(8,128)(2,1)S(1)} %pair.5.refs_0_), channel_id=1, source_target_pairs={{0,24},{4,28},{8,16},{12,20},{16,8},{20,12},{24,0},{28,4},{1,25},{... | collective-permute-start | bytes 98312 | tf_op jit(solution)/shard_map/ppermute | solution.py:410
  65.8 1.3 %collective-permute-done.17.refs_3_ = bf16[64,256]{1,0:T(8,128)(2,1)S(1)} collective-permute-done((bf16[64,256]{1,0:T(8,128)(2,1)S(1)}, bf16[64,256]{1,0:T(8,128)(2,1)S(1)}, u32[]{:S(2)}, u32[]{:S(2)}) %collective-permute-start.17) | collective-permute-done | bytes 32800 | tf_op jit(solution)/shard_map/ppermute | solution.py:410
  68.6 4.6 %points.5 = (bf16[152,256]{1,0:T(8,128)(2,1)S(1)}, f32[64,192]{1,0:T(8,128)}, f32[8,128]{1,0:T(8,128)S(1)}) custom-call(bf16[64,256]{1,0:T(8,128)(2,1)S(1)} %pair.5.refs_0_, bf16[64,256]{1,0:T(8,128)(2,1)S(1)} %collective-permute-done.15.refs_1_, bf16[64,256]{1,0:T(8,128)(2,1)S(1)} %collective-permute-done.16.refs_2_, ...), custom_call_target="tpu_custom_call" | custom-call | tf_op jit(solution)/shard_map/points/pallas_call | solution.py:398
  73.2 2.2 %collective-permute-start.20 = (bf16[152,256]{1,0:T(8,128)(2,1)S(1)}, bf16[152,256]{1,0:T(8,128)(2,1)S(1)}, u32[]{:S(2)}, u32[]{:S(2)}) collective-permute-start(bf16[152,256]{1,0:T(8,128)(2,1)S(1)} %get-tuple-element.52.refs_0_), channel_id=1, source_target_pairs={{0,3},{1,2},{2,1},{3,0},{4,7},{5,6},{6,5},{7,4},{8,11},{9,10},{10,... | collective-permute-start | bytes 233480 | tf_op jit(solution)/shard_map/ppermute | solution.py:410
  75.4 2.2 %collective-permute-start.18 = (bf16[152,256]{1,0:T(8,128)(2,1)S(1)}, bf16[152,256]{1,0:T(8,128)(2,1)S(1)}, u32[]{:S(2)}, u32[]{:S(2)}) collective-permute-start(bf16[152,256]{1,0:T(8,128)(2,1)S(1)} %get-tuple-element.52.refs_0_), channel_id=1, source_target_pairs={{0,1},{1,0},{2,3},{3,2},{4,5},{5,4},{6,7},{7,6},{8,9},{9,8},{10,11... | collective-permute-start | bytes 233480 | tf_op jit(solution)/shard_map/ppermute | solution.py:410
  77.6 2.7 %collective-permute-done.20.refs_3_ = bf16[152,256]{1,0:T(8,128)(2,1)S(1)} collective-permute-done((bf16[152,256]{1,0:T(8,128)(2,1)S(1)}, bf16[152,256]{1,0:T(8,128)(2,1)S(1)}, u32[]{:S(2)}, u32[]{:S(2)}) %collective-permute-start.20) | collective-permute-done | bytes 77856 | tf_op jit(solution)/shard_map/ppermute | solution.py:410
  80.3 1.8 %collective-permute-done.19.refs_2_ = bf16[152,256]{1,0:T(8,128)(2,1)S(1)} collective-permute-done((bf16[152,256]{1,0:T(8,128)(2,1)S(1)}, bf16[152,256]{1,0:T(8,128)(2,1)S(1)}, u32[]{:S(2)}, u32[]{:S(2)}) %collective-permute-start.19) | collective-permute-done | bytes 77856 | tf_op jit(solution)/shard_map/ppermute | solution.py:410
  82.1 2.1 %finish.1 = (f32[9,8192]{1,0:T(8,128)}, f32[9,8192]{1,0:T(8,128)}) custom-call(bf16[152,256]{1,0:T(8,128)(2,1)S(1)} %get-tuple-element.52.refs_0_, bf16[152,256]{1,0:T(8,128)(2,1)S(1)} %collective-permute-done.18.refs_1_, bf16[152,256]{1,0:T(8,128)(2,1)S(1)} %collective-permute-done.19.refs_2_, bf16[152,256]{1,0:T(8,128)(2,1)S(1)} %collective-permute-done.20.refs_3_, ...), custom_call_target="tpu_custom_call" | custom-call | tf_op jit(solution)/shard_map/finish/pallas_call | solution.py:398
  (28 shorter events, 13.7 us)
Async XLA Ops:
  9.4 1.4 %collective-permute-start = (bf16[64,256]{1,0:T(8,128)(2,1)S(1)}, bf16[64,256]{1,0:T(8,128)(2,1)S(1)}, u32[]{:S(2)}, u32[]{:S(2)}) collective-permute-start(bf16[64,256]{1,0:T(8,128)(2,1)S(1)} %get-tuple-element.31.refs_0_), channel_id=1, source_target_pairs={{0,4},{4,0},{8,12},{12,8},{16,20},{20,16},{24,28},{28,24},{1,5},{5... | collective-permute-start | bytes 98312 | tf_op jit(solution)/shard_map/ppermute | solution.py:410
  11.1 5.7 %collective-permute-start.3 = (bf16[64,256]{1,0:T(8,128)(2,1)S(1)}, bf16[64,256]{1,0:T(8,128)(2,1)S(1)}, u32[]{:S(2)}, u32[]{:S(2)}) collective-permute-start(bf16[64,256]{1,0:T(8,128)(2,1)S(1)} %pair.3.refs_0_), channel_id=1, source_target_pairs={{0,24},{4,28},{8,16},{12,20},{16,8},{20,12},{24,0},{28,4},{1,25},{... | collective-permute-start | bytes 98312 | tf_op jit(solution)/shard_map/ppermute | solution.py:410
  14.9 3.9 %collective-permute-start.2 = (bf16[64,256]{1,0:T(8,128)(2,1)S(1)}, bf16[64,256]{1,0:T(8,128)(2,1)S(1)}, u32[]{:S(2)}, u32[]{:S(2)}) collective-permute-start(bf16[64,256]{1,0:T(8,128)(2,1)S(1)} %pair.3.refs_0_), channel_id=1, source_target_pairs={{0,16},{4,20},{8,24},{12,28},{16,0},{20,4},{24,8},{28,12},{1,17},{... | collective-permute-start | bytes 98312 | tf_op jit(solution)/shard_map/ppermute | solution.py:410
  15.4 3.9 %collective-permute-start.1 = (bf16[64,256]{1,0:T(8,128)(2,1)S(1)}, bf16[64,256]{1,0:T(8,128)(2,1)S(1)}, u32[]{:S(2)}, u32[]{:S(2)}) collective-permute-start(bf16[64,256]{1,0:T(8,128)(2,1)S(1)} %pair.3.refs_0_), channel_id=1, source_target_pairs={{0,8},{4,12},{8,0},{12,4},{16,24},{20,28},{24,16},{28,20},{1,9},{5... | collective-permute-start | bytes 98312 | tf_op jit(solution)/shard_map/ppermute | solution.py:410
  23.3 6.3 %collective-permute-start.6 = (bf16[152,256]{1,0:T(8,128)(2,1)S(1)}, bf16[152,256]{1,0:T(8,128)(2,1)S(1)}, u32[]{:S(2)}, u32[]{:S(2)}) collective-permute-start(bf16[152,256]{1,0:T(8,128)(2,1)S(1)} %get-tuple-element.35.refs_0_), channel_id=1, source_target_pairs={{0,3},{1,2},{2,1},{3,0},{4,7},{5,6},{6,5},{7,4},{8,11},{9,10},{10,... | collective-permute-start | bytes 233480 | tf_op jit(solution)/shard_map/ppermute | solution.py:410
  27.0 5.7 %collective-permute-start.5 = (bf16[152,256]{1,0:T(8,128)(2,1)S(1)}, bf16[152,256]{1,0:T(8,128)(2,1)S(1)}, u32[]{:S(2)}, u32[]{:S(2)}) collective-permute-start(bf16[152,256]{1,0:T(8,128)(2,1)S(1)} %get-tuple-element.35.refs_0_), channel_id=1, source_target_pairs={{0,2},{1,3},{2,0},{3,1},{4,6},{5,7},{6,4},{7,5},{8,10},{9,11},{10,... | collective-permute-start | bytes 233480 | tf_op jit(solution)/shard_map/ppermute | solution.py:410
  27.0 5.7 %collective-permute-start.4 = (bf16[152,256]{1,0:T(8,128)(2,1)S(1)}, bf16[152,256]{1,0:T(8,128)(2,1)S(1)}, u32[]{:S(2)}, u32[]{:S(2)}) collective-permute-start(bf16[152,256]{1,0:T(8,128)(2,1)S(1)} %get-tuple-element.35.refs_0_), channel_id=1, source_target_pairs={{0,1},{1,0},{2,3},{3,2},{4,5},{5,4},{6,7},{7,6},{8,9},{9,8},{10,11... | collective-permute-start | bytes 233480 | tf_op jit(solution)/shard_map/ppermute | solution.py:410
  36.2 1.2 %collective-permute-start.7 = (bf16[64,256]{1,0:T(8,128)(2,1)S(1)}, bf16[64,256]{1,0:T(8,128)(2,1)S(1)}, u32[]{:S(2)}, u32[]{:S(2)}) collective-permute-start(bf16[64,256]{1,0:T(8,128)(2,1)S(1)} %get-tuple-element.42.refs_0_), channel_id=1, source_target_pairs={{0,4},{4,0},{8,12},{12,8},{16,20},{20,16},{24,28},{28,24},{1,5},{5... | collective-permute-start | bytes 98312 | tf_op jit(solution)/shard_map/ppermute | solution.py:410
  37.7 4.9 %collective-permute-start.10 = (bf16[64,256]{1,0:T(8,128)(2,1)S(1)}, bf16[64,256]{1,0:T(8,128)(2,1)S(1)}, u32[]{:S(2)}, u32[]{:S(2)}) collective-permute-start(bf16[64,256]{1,0:T(8,128)(2,1)S(1)} %pair.4.refs_0_), channel_id=1, source_target_pairs={{0,24},{4,28},{8,16},{12,20},{16,8},{20,12},{24,0},{28,4},{1,25},{... | collective-permute-start | bytes 98312 | tf_op jit(solution)/shard_map/ppermute | solution.py:410
  39.5 3.9 %collective-permute-start.9 = (bf16[64,256]{1,0:T(8,128)(2,1)S(1)}, bf16[64,256]{1,0:T(8,128)(2,1)S(1)}, u32[]{:S(2)}, u32[]{:S(2)}) collective-permute-start(bf16[64,256]{1,0:T(8,128)(2,1)S(1)} %pair.4.refs_0_), channel_id=1, source_target_pairs={{0,16},{4,20},{8,24},{12,28},{16,0},{20,4},{24,8},{28,12},{1,17},{... | collective-permute-start | bytes 98312 | tf_op jit(solution)/shard_map/ppermute | solution.py:410
  40.0 3.9 %collective-permute-start.8 = (bf16[64,256]{1,0:T(8,128)(2,1)S(1)}, bf16[64,256]{1,0:T(8,128)(2,1)S(1)}, u32[]{:S(2)}, u32[]{:S(2)}) collective-permute-start(bf16[64,256]{1,0:T(8,128)(2,1)S(1)} %pair.4.refs_0_), channel_id=1, source_target_pairs={{0,8},{4,12},{8,0},{12,4},{16,24},{20,28},{24,16},{28,20},{1,9},{5... | collective-permute-start | bytes 98312 | tf_op jit(solution)/shard_map/ppermute | solution.py:410
  48.1 7.1 %collective-permute-start.13 = (bf16[152,256]{1,0:T(8,128)(2,1)S(1)}, bf16[152,256]{1,0:T(8,128)(2,1)S(1)}, u32[]{:S(2)}, u32[]{:S(2)}) collective-permute-start(bf16[152,256]{1,0:T(8,128)(2,1)S(1)} %get-tuple-element.44.refs_0_), channel_id=1, source_target_pairs={{0,3},{1,2},{2,1},{3,0},{4,7},{5,6},{6,5},{7,4},{8,11},{9,10},{10,... | collective-permute-start | bytes 233480 | tf_op jit(solution)/shard_map/ppermute | solution.py:410
  50.3 6.7 %collective-permute-start.12 = (bf16[152,256]{1,0:T(8,128)(2,1)S(1)}, bf16[152,256]{1,0:T(8,128)(2,1)S(1)}, u32[]{:S(2)}, u32[]{:S(2)}) collective-permute-start(bf16[152,256]{1,0:T(8,128)(2,1)S(1)} %get-tuple-element.44.refs_0_), channel_id=1, source_target_pairs={{0,2},{1,3},{2,0},{3,1},{4,6},{5,7},{6,4},{7,5},{8,10},{9,11},{10,... | collective-permute-start | bytes 233480 | tf_op jit(solution)/shard_map/ppermute | solution.py:410
  50.3 6.7 %collective-permute-start.11 = (bf16[152,256]{1,0:T(8,128)(2,1)S(1)}, bf16[152,256]{1,0:T(8,128)(2,1)S(1)}, u32[]{:S(2)}, u32[]{:S(2)}) collective-permute-start(bf16[152,256]{1,0:T(8,128)(2,1)S(1)} %get-tuple-element.44.refs_0_), channel_id=1, source_target_pairs={{0,1},{1,0},{2,3},{3,2},{4,5},{5,4},{6,7},{7,6},{8,9},{9,8},{10,11... | collective-permute-start | bytes 233480 | tf_op jit(solution)/shard_map/ppermute | solution.py:410
  60.8 1.2 %collective-permute-start.14 = (bf16[64,256]{1,0:T(8,128)(2,1)S(1)}, bf16[64,256]{1,0:T(8,128)(2,1)S(1)}, u32[]{:S(2)}, u32[]{:S(2)}) collective-permute-start(bf16[64,256]{1,0:T(8,128)(2,1)S(1)} %get-tuple-element.50.refs_0_), channel_id=1, source_target_pairs={{0,4},{4,0},{8,12},{12,8},{16,20},{20,16},{24,28},{28,24},{1,5},{5... | collective-permute-start | bytes 98312 | tf_op jit(solution)/shard_map/ppermute | solution.py:410
  62.3 4.8 %collective-permute-start.17 = (bf16[64,256]{1,0:T(8,128)(2,1)S(1)}, bf16[64,256]{1,0:T(8,128)(2,1)S(1)}, u32[]{:S(2)}, u32[]{:S(2)}) collective-permute-start(bf16[64,256]{1,0:T(8,128)(2,1)S(1)} %pair.5.refs_0_), channel_id=1, source_target_pairs={{0,24},{4,28},{8,16},{12,20},{16,8},{20,12},{24,0},{28,4},{1,25},{... | collective-permute-start | bytes 98312 | tf_op jit(solution)/shard_map/ppermute | solution.py:410
  64.4 3.9 %collective-permute-start.16 = (bf16[64,256]{1,0:T(8,128)(2,1)S(1)}, bf16[64,256]{1,0:T(8,128)(2,1)S(1)}, u32[]{:S(2)}, u32[]{:S(2)}) collective-permute-start(bf16[64,256]{1,0:T(8,128)(2,1)S(1)} %pair.5.refs_0_), channel_id=1, source_target_pairs={{0,16},{4,20},{8,24},{12,28},{16,0},{20,4},{24,8},{28,12},{1,17},{... | collective-permute-start | bytes 98312 | tf_op jit(solution)/shard_map/ppermute | solution.py:410
  64.7 3.9 %collective-permute-start.15 = (bf16[64,256]{1,0:T(8,128)(2,1)S(1)}, bf16[64,256]{1,0:T(8,128)(2,1)S(1)}, u32[]{:S(2)}, u32[]{:S(2)}) collective-permute-start(bf16[64,256]{1,0:T(8,128)(2,1)S(1)} %pair.5.refs_0_), channel_id=1, source_target_pairs={{0,8},{4,12},{8,0},{12,4},{16,24},{20,28},{24,16},{28,20},{1,9},{5... | collective-permute-start | bytes 98312 | tf_op jit(solution)/shard_map/ppermute | solution.py:410
  73.2 7.1 %collective-permute-start.20 = (bf16[152,256]{1,0:T(8,128)(2,1)S(1)}, bf16[152,256]{1,0:T(8,128)(2,1)S(1)}, u32[]{:S(2)}, u32[]{:S(2)}) collective-permute-start(bf16[152,256]{1,0:T(8,128)(2,1)S(1)} %get-tuple-element.52.refs_0_), channel_id=1, source_target_pairs={{0,3},{1,2},{2,1},{3,0},{4,7},{5,6},{6,5},{7,4},{8,11},{9,10},{10,... | collective-permute-start | bytes 233480 | tf_op jit(solution)/shard_map/ppermute | solution.py:410
  75.4 6.7 %collective-permute-start.19 = (bf16[152,256]{1,0:T(8,128)(2,1)S(1)}, bf16[152,256]{1,0:T(8,128)(2,1)S(1)}, u32[]{:S(2)}, u32[]{:S(2)}) collective-permute-start(bf16[152,256]{1,0:T(8,128)(2,1)S(1)} %get-tuple-element.52.refs_0_), channel_id=1, source_target_pairs={{0,2},{1,3},{2,0},{3,1},{4,6},{5,7},{6,4},{7,5},{8,10},{9,11},{10,... | collective-permute-start | bytes 233480 | tf_op jit(solution)/shard_map/ppermute | solution.py:410
  75.4 6.7 %collective-permute-start.18 = (bf16[152,256]{1,0:T(8,128)(2,1)S(1)}, bf16[152,256]{1,0:T(8,128)(2,1)S(1)}, u32[]{:S(2)}, u32[]{:S(2)}) collective-permute-start(bf16[152,256]{1,0:T(8,128)(2,1)S(1)} %get-tuple-element.52.refs_0_), channel_id=1, source_target_pairs={{0,1},{1,0},{2,3},{3,2},{4,5},{5,4},{6,7},{7,6},{8,9},{9,8},{10,11... | collective-permute-start | bytes 233480 | tf_op jit(solution)/shard_map/ppermute | solution.py:410

commit v3 on v2

--- a/solution.py
+++ b/solution.py
@@ -14,8 +14,9 @@
 VMEM = pl.BlockSpec(memory_space=pltpu.VMEM)
 HBM = pl.BlockSpec(memory_space=pltpu.HBM)
 NT = (((1,), (1,)), ((), ()))
-FETCHES = 8
+FETCHES = 4
 TAIL = 8
+BACKWARD_SHARE = 7
 
 
 def in_hbm(value):
@@ -99,13 +100,17 @@
     rows_ref[...] = jnp.dot(zt_ref[...], onehot, preferred_element_type=F32).T
 
 
+def on_vector_unit(pair, share):
+    return (pair + 1) * share // 16 > pair * share // 16
+
+
 def forward_pairs(e_ref, rows_ref, part_ref, pairs):
     sub = iota((8, rows_ref.shape[1]), 0)
     for pair in pairs:
         at = pl.ds(8 * pair, 8)
-        rows = rows_ref[at, :]
-        top = jnp.where(sub < 4, rows, 0.0).astype(BF16)
-        low = jnp.where(sub >= 4, rows, 0.0).astype(BF16)
+        both = rows_ref[at, :]
+        top = jnp.where(sub < 4, both, 0.0).astype(BF16)
+        low = jnp.where(sub >= 4, both, 0.0).astype(BF16)
         part = jnp.dot(top, e_ref[2 * pair], preferred_element_type=F32) + jnp.dot(
             low, e_ref[2 * pair + 1], preferred_element_type=F32
         )
@@ -122,22 +127,39 @@
     return even[:, :192] + odd[:, 64:]
 
 
-def backward(e_ref, y, yc_ref, c_ref):
-    count = e_ref.shape[0]
+def backward(e_ref, y, yc_ref, rows_ref, cols_ref):
+    count, rows = e_ref.shape[:2]
     wide = [jnp.concatenate(pair, axis=1) for pair in ((y[0], y[1]), (y[2], y[0]), (y[1], y[2]))]
     for i in range(6):
         yc_ref[:, 128 * i : 128 * i + 128] = wide[i % 3]
     row, col = iota((8, 768), 0), iota((8, 768), 1)
     masks = [(col >= 192 * (row - r)) & (col < 192 * (row - r) + 192) for r in (0, 4)]
-
+    low_lanes = iota((1, 128), 1) < 64
     for pair in range(count // 2):
+        if on_vector_unit(pair, BACKWARD_SHARE):
+            for t in (2 * pair, 2 * pair + 1):
+                e = [e_ref[t, :, 128 * i : 128 * i + 128].astype(F32) for i in range(6)]
+                w = [yc_ref[pl.ds(t, 1), 128 * i : 128 * i + 128] for i in range(3)]
+                w_low, w_high = jnp.where(low_lanes, w[1], 0.0), jnp.where(low_lanes, 0.0, w[1])
+                sums = (
+                    e[0] * w[0] + e[1] * w_low,
+                    e[1] * w_high + e[2] * w[2],
+                    e[3] * w[0] + e[4] * w_low,
+                    e[4] * w_high + e[5] * w[2],
+                )
+                for s, value in enumerate(sums):
+                    cols_ref[:, 4 * t + s : 4 * t + s + 1] = jnp.sum(value, axis=1, keepdims=True)
+            continue
         part = None
         for k in range(2):
             wide_row = jnp.broadcast_to(yc_ref[pl.ds(2 * pair + k, 1), :], (8, 768))
             lhs = jnp.where(masks[k], wide_row, 0.0).astype(BF16)
             one = lax.dot_general(lhs, e_ref[2 * pair + k], NT, preferred_element_type=F32)
             part = one if part is None else part + one
-        c_ref[pl.ds(8 * pair, 8), :] = part
+        rows_ref[pl.ds(8 * pair, 8), :] = part
+    pair_of = iota((rows, 4 * count), 1) // 8
+    vector = on_vector_unit(pair_of, BACKWARD_SHARE)
+    return jnp.where(vector, cols_ref[...], rows_ref[...].T)
 
 
 def start_kernel(
@@ -227,7 +249,7 @@
 
     def forward_chunk(n, one):
         one.wait()
-        forward_pairs(e_ref, rows_ref, part_ref, range(n * (step // 2), (n + 1) * (step // 2)))
+        forward_pairs(e_ref, rows_ref, part_ref, range(n * step // 2, (n + 1) * step // 2))
 
     for n, one in enumerate(early):
         forward_chunk(n, one)
@@ -269,12 +291,13 @@
     out_ref[...] = jnp.concatenate([value[:, :192], scalars], axis=1).astype(BF16)
 
 
-def points_kernel(parts, first, *refs):
+def points_kernel(parts, first, last, *refs):
     summed = tree_sum([ref[...].astype(F32) for ref in refs[:parts]])
     refs = refs[parts:]
     if not first:
         p_old_ref, scal_old_ref, *refs = refs
-    e_ref, v_ref, slot_ref, msg_ref, p_ref, scal_ref, yc_ref, c_ref = refs
+    e_ref, v_ref, slot_ref, msg_ref, scal_ref, *refs = refs
+    *p_out, yc_ref, c_ref, ct_ref = refs
     inner_now, z_c_z, z_c_d = read_scalars(summed[:, 192:], 3)
     point_sum = summed[:, :192]
     beta, curve = jnp.zeros((1, 1), F32), z_c_z
@@ -282,15 +305,15 @@
         beta = inner_now / scal_old_ref[0:1, 0:1]
         curve = z_c_z + beta * (2.0 * z_c_d + beta * scal_old_ref[1:2, 0:1])
         point_sum = point_sum + beta * p_old_ref[...]
-    p_ref[...] = point_sum
+    if not last:
+        p_out[0][...] = point_sum
     row = iota((8, 128), 0)
     scal_ref[...] = jnp.where(row == 0, inner_now, jnp.where(row == 1, curve, beta))
     p = [point_sum[:, 64 * i : 64 * i + 64] for i in range(3)]
     y = [tree_sum([v_ref[sym(3, i, j)][:, :64] * p[j] for j in range(3)]) for i in range(3)]
     taken = total(tree_sum([a * b for a, b in zip(p, y)]))
-    backward(e_ref, y, yc_ref, c_ref)
     rows = c_ref.shape[1]
-    msg_ref[0:rows, :] = c_ref[...].T.astype(BF16)
+    msg_ref[0:rows, :] = backward(e_ref, y, yc_ref, c_ref, ct_ref).astype(BF16)
     width = msg_ref.shape[1]
     row = iota((TAIL, width), 0)
     tail = jnp.zeros((TAIL, width), F32)
@@ -392,6 +415,7 @@
     planes_of = size * (size + 1) // 2
     part_scratch = pltpu.VMEM((cols // 128, width, 128), F32)
     rows_scratch = pltpu.VMEM((width, rows), F32)
+    cols_scratch = pltpu.VMEM((rows, width), F32)
     zt_scratch = pltpu.VMEM((rows, tiles), BF16)
 
     def call(kernel, outs, args, in_specs=None, scratch=(), megabytes=8, name=None):
@@ -458,18 +482,15 @@
             pair = exchange(message_now, "cam", n_cam, range(1, inner))
             message_now = call(pair_kernel, message, pair, name="pair")
         parts = exchange(message_now, "cam", n_cam, range(inner, n_cam, inner))
-        tile_message, point_sum, scal = call(
-            functools.partial(points_kernel, len(parts), first),
-            [
-                shape((rows + TAIL, width), BF16),
-                shape((count, 192), F32),
-                shape((8, 128), F32),
-            ],
+        outs = [shape((rows + TAIL, width), BF16), shape((8, 128), F32)]
+        tile_message, scal, *point_sum = call(
+            functools.partial(points_kernel, len(parts), first, last),
+            outs + ([] if last else [shape((count, 192), F32)]),
             (*parts, *old_points, coupling, v6, slot),
-            scratch=[pltpu.VMEM((count, cols), F32), rows_scratch],
+            scratch=[pltpu.VMEM((count, cols), F32), rows_scratch, cols_scratch],
             name="points",
         )
-        old_points = (point_sum, scal)
+        old_points = (*point_sum, scal)
         parts = exchange(tile_message, "pts", n_pts, range(1, n_pts))
         kernel = functools.partial(camera_kernel, len(parts), first, last)
         common = [

time: 84.3 us -> 78.4 us (0.930)
  Pallas kernels: 31.7 us -> 25.7 us
    pallas_call x10, Pallas kernels: 31.7 us -> 25.7 us  [call(): pl.pallas_call(kernel, out_shape=outs, in_specs=in_specs or [VMEM] * len(...]
where the time goes in v3:
time: 78.4 us; the launch traced here: 78.3 us
  waiting for transfers between devices  26.5 us (34%)
  Pallas kernels  25.7 us (33%)
  starting transfers between devices  25.3 us (32%)
    ppermute x21, waiting for transfers between devices, exchange(): lax.ppermute(value, axis, [(i, i ^ k) for i in range(axis_size)])  26.5 us
    pallas_call x10, Pallas kernels, call(): pl.pallas_call(kernel, out_shape=outs, in_specs=in_specs or [VMEM] * len(...  25.7 us
    ppermute x21, starting transfers between devices, exchange(): lax.ppermute(value, axis, [(i, i ^ k) for i in range(axis_size)])  25.3 us
  transfers between devices with their start and end apart: 21, of which 18 were waited for; matrix products, arithmetic and copies ran while one was open for 0% of the time, Pallas kernels for 0%

profile of v3, /device:TPU:0, one launch (start us, length us, event | category | flops | bytes accessed | tf_op | source)
XLA Modules:
  0.0 78.3 jit_solution(934789484181265396)
XLA Ops:
  0.6 7.6 %start.1 = (bf16[64,144,768]{2,1,0:T(8,128)(2,1)S(1)}, f32[45,64,128]{2,1,0:T(8,128)S(1)}, f32[45,64,128]{2,1,0:T(8,128)S(1)}, f32[6,64,128]{2,1,0:T(8,128)S(1)}...) custom-call(f32[9,8192]{1,0:T(8,128)} %rhs_hbm.1, ...), custom_call_target="tpu_custom_call" | custom-call | tf_op jit(solution)/shard_map/start/pallas_call | solution.py:422
  9.9 3.8 %collective-permute-start.3 = (bf16[64,256]{1,0:T(8,128)(2,1)S(1)}, bf16[64,256]{1,0:T(8,128)(2,1)S(1)}, u32[]{:S(2)}, u32[]{:S(2)}) collective-permute-start(bf16[64,256]{1,0:T(8,128)(2,1)S(1)} %pair.3.refs_0_), channel_id=1, source_target_pairs={{0,24},{4,28},{8,16},{12,20},{16,8},{20,12},{24,0},{28,4},{1,25},{... | collective-permute-start | bytes 98312 | tf_op jit(solution)/shard_map/ppermute | solution.py:434
  15.6 2.0 %collective-permute-done.2.refs_2_ = bf16[64,256]{1,0:T(8,128)(2,1)S(1)} collective-permute-done((bf16[64,256]{1,0:T(8,128)(2,1)S(1)}, bf16[64,256]{1,0:T(8,128)(2,1)S(1)}, u32[]{:S(2)}, u32[]{:S(2)}) %collective-permute-start.2) | collective-permute-done | bytes 32800 | tf_op jit(solution)/shard_map/ppermute | solution.py:434
  18.1 2.6 %points.3 = (bf16[152,256]{1,0:T(8,128)(2,1)S(1)}, f32[8,128]{1,0:T(8,128)S(1)}, f32[64,192]{1,0:T(8,128)S(1)}) custom-call(bf16[64,256]{1,0:T(8,128)(2,1)S(1)} %pair.3.refs_0_, bf16[64,256]{1,0:T(8,128)(2,1)S(1)} %collective-permute-done.1.refs_1_, bf16[64,256]{1,0:T(8,128)(2,1)S(1)} %collective-permute-done.2.refs_2_, ...), custom_call_target="tpu_custom_call" | custom-call | tf_op jit(solution)/shard_map/points/pallas_call | solution.py:422
  20.7 3.7 %collective-permute-start.6 = (bf16[152,256]{1,0:T(8,128)(2,1)S(1)}, bf16[152,256]{1,0:T(8,128)(2,1)S(1)}, u32[]{:S(2)}, u32[]{:S(2)}) collective-permute-start(bf16[152,256]{1,0:T(8,128)(2,1)S(1)} %get-tuple-element.35.refs_0_), channel_id=1, source_target_pairs={{0,3},{1,2},{2,1},{3,0},{4,7},{5,6},{6,5},{7,4},{8,11},{9,10},{10,... | collective-permute-start | bytes 233480 | tf_op jit(solution)/shard_map/ppermute | solution.py:434
  25.1 1.8 %collective-permute-done.6.refs_3_ = bf16[152,256]{1,0:T(8,128)(2,1)S(1)} collective-permute-done((bf16[152,256]{1,0:T(8,128)(2,1)S(1)}, bf16[152,256]{1,0:T(8,128)(2,1)S(1)}, u32[]{:S(2)}, u32[]{:S(2)}) %collective-permute-start.6) | collective-permute-done | bytes 77856 | tf_op jit(solution)/shard_map/ppermute | solution.py:434
  26.9 3.1 %collective-permute-done.5.refs_2_ = bf16[152,256]{1,0:T(8,128)(2,1)S(1)} collective-permute-done((bf16[152,256]{1,0:T(8,128)(2,1)S(1)}, bf16[152,256]{1,0:T(8,128)(2,1)S(1)}, u32[]{:S(2)}, u32[]{:S(2)}) %collective-permute-start.5) | collective-permute-done | bytes 77856 | tf_op jit(solution)/shard_map/ppermute | solution.py:434
  30.0 3.6 %camera.2 = (bf16[64,256]{1,0:T(8,128)(2,1)S(1)}, f32[9,64,128]{2,1,0:T(8,128)S(1)}, f32[9,64,128]{2,1,0:T(8,128)S(1)}, f32[9,64,128]{2,1,0:T(8,128)S(1)}, f32[9,64,128]{2,1,0:T(8,128)S(1)}) custom-call(bf16[152,256]{1,0:T(8,128)(2,1)S(1)} %get-tuple-element.35.refs_0_, bf16[152,256]{1,0:T(8,128)(2,1)S(1)} %collective-permute-done.4.refs_1_, ...), custom_call_target="tpu_custom_call" | custom-call | tf_op jit(solution)/shard_map/camera/pallas_call | solution.py:422
  35.0 1.8 %collective-permute-start.10 = (bf16[64,256]{1,0:T(8,128)(2,1)S(1)}, bf16[64,256]{1,0:T(8,128)(2,1)S(1)}, u32[]{:S(2)}, u32[]{:S(2)}) collective-permute-start(bf16[64,256]{1,0:T(8,128)(2,1)S(1)} %pair.4.refs_0_), channel_id=1, source_target_pairs={{0,24},{4,28},{8,16},{12,20},{16,8},{20,12},{24,0},{28,4},{1,25},{... | collective-permute-start | bytes 98312 | tf_op jit(solution)/shard_map/ppermute | solution.py:434
  38.5 1.4 %collective-permute-done.10.refs_3_ = bf16[64,256]{1,0:T(8,128)(2,1)S(1)} collective-permute-done((bf16[64,256]{1,0:T(8,128)(2,1)S(1)}, bf16[64,256]{1,0:T(8,128)(2,1)S(1)}, u32[]{:S(2)}, u32[]{:S(2)}) %collective-permute-start.10) | collective-permute-done | bytes 32800 | tf_op jit(solution)/shard_map/ppermute | solution.py:434
  41.3 2.9 %points.4 = (bf16[152,256]{1,0:T(8,128)(2,1)S(1)}, f32[8,128]{1,0:T(8,128)S(1)}, f32[64,192]{1,0:T(8,128)S(1)}) custom-call(bf16[64,256]{1,0:T(8,128)(2,1)S(1)} %pair.4.refs_0_, bf16[64,256]{1,0:T(8,128)(2,1)S(1)} %collective-permute-done.8.refs_1_, bf16[64,256]{1,0:T(8,128)(2,1)S(1)} %collective-permute-done.9.refs_2_, ...), custom_call_target="tpu_custom_call" | custom-call | tf_op jit(solution)/shard_map/points/pallas_call | solution.py:422
  44.2 2.3 %collective-permute-start.13 = (bf16[152,256]{1,0:T(8,128)(2,1)S(1)}, bf16[152,256]{1,0:T(8,128)(2,1)S(1)}, u32[]{:S(2)}, u32[]{:S(2)}) collective-permute-start(bf16[152,256]{1,0:T(8,128)(2,1)S(1)} %get-tuple-element.44.refs_0_), channel_id=1, source_target_pairs={{0,3},{1,2},{2,1},{3,0},{4,7},{5,6},{6,5},{7,4},{8,11},{9,10},{10,... | collective-permute-start | bytes 233480 | tf_op jit(solution)/shard_map/ppermute | solution.py:434
  46.4 2.2 %collective-permute-start.11 = (bf16[152,256]{1,0:T(8,128)(2,1)S(1)}, bf16[152,256]{1,0:T(8,128)(2,1)S(1)}, u32[]{:S(2)}, u32[]{:S(2)}) collective-permute-start(bf16[152,256]{1,0:T(8,128)(2,1)S(1)} %get-tuple-element.44.refs_0_), channel_id=1, source_target_pairs={{0,1},{1,0},{2,3},{3,2},{4,5},{5,4},{6,7},{7,6},{8,9},{9,8},{10,11... | collective-permute-start | bytes 233480 | tf_op jit(solution)/shard_map/ppermute | solution.py:434
  48.6 2.7 %collective-permute-done.13.refs_3_ = bf16[152,256]{1,0:T(8,128)(2,1)S(1)} collective-permute-done((bf16[152,256]{1,0:T(8,128)(2,1)S(1)}, bf16[152,256]{1,0:T(8,128)(2,1)S(1)}, u32[]{:S(2)}, u32[]{:S(2)}) %collective-permute-start.13) | collective-permute-done | bytes 77856 | tf_op jit(solution)/shard_map/ppermute | solution.py:434
  51.3 1.9 %collective-permute-done.12.refs_2_ = bf16[152,256]{1,0:T(8,128)(2,1)S(1)} collective-permute-done((bf16[152,256]{1,0:T(8,128)(2,1)S(1)}, bf16[152,256]{1,0:T(8,128)(2,1)S(1)}, u32[]{:S(2)}, u32[]{:S(2)}) %collective-permute-start.12) | collective-permute-done | bytes 77856 | tf_op jit(solution)/shard_map/ppermute | solution.py:434
  53.2 3.6 %camera.3 = (bf16[64,256]{1,0:T(8,128)(2,1)S(1)}, f32[9,64,128]{2,1,0:T(8,128)S(1)}, f32[9,64,128]{2,1,0:T(8,128)S(1)}, f32[9,64,128]{2,1,0:T(8,128)S(1)}, f32[9...) custom-call(bf16[152,256]{1,0:T(8,128)(2,1)S(1)} %get-tuple-element.44.refs_0_, ...), custom_call_target="tpu_custom_call" | custom-call | tf_op jit(solution)/shard_map/camera/pallas_call | solution.py:422
  58.2 2.1 %collective-permute-start.17 = (bf16[64,256]{1,0:T(8,128)(2,1)S(1)}, bf16[64,256]{1,0:T(8,128)(2,1)S(1)}, u32[]{:S(2)}, u32[]{:S(2)}) collective-permute-start(bf16[64,256]{1,0:T(8,128)(2,1)S(1)} %pair.5.refs_0_), channel_id=1, source_target_pairs={{0,24},{4,28},{8,16},{12,20},{16,8},{20,12},{24,0},{28,4},{1,25},{... | collective-permute-start | bytes 98312 | tf_op jit(solution)/shard_map/ppermute | solution.py:434
  61.7 1.3 %collective-permute-done.17.refs_3_ = bf16[64,256]{1,0:T(8,128)(2,1)S(1)} collective-permute-done((bf16[64,256]{1,0:T(8,128)(2,1)S(1)}, bf16[64,256]{1,0:T(8,128)(2,1)S(1)}, u32[]{:S(2)}, u32[]{:S(2)}) %collective-permute-start.17) | collective-permute-done | bytes 32800 | tf_op jit(solution)/shard_map/ppermute | solution.py:434
  64.5 2.7 %points.5 = (bf16[152,256]{1,0:T(8,128)(2,1)S(1)}, f32[8,128]{1,0:T(8,128)S(1)}) custom-call(bf16[64,256]{1,0:T(8,128)(2,1)S(1)} %pair.5.refs_0_, bf16[64,256]{1,0:T(8,128)(2,1)S(1)} %collective-permute-done.15.refs_1_, bf16[64,256]{1,0:T(8,128)(2,1)S(1)} %collective-permute-done.16.refs_2_, bf16[64,256]{1,0:T(8,128)(2,1)S(1)} %collective-permute-done.17.refs_3_, ...), custom_call_target="tpu_custom_call" | custom-call | tf_op jit(solution)/shard_map/points/pallas_call | solution.py:422
  67.3 2.3 %collective-permute-start.20 = (bf16[152,256]{1,0:T(8,128)(2,1)S(1)}, bf16[152,256]{1,0:T(8,128)(2,1)S(1)}, u32[]{:S(2)}, u32[]{:S(2)}) collective-permute-start(bf16[152,256]{1,0:T(8,128)(2,1)S(1)} %get-tuple-element.52.refs_0_), channel_id=1, source_target_pairs={{0,3},{1,2},{2,1},{3,0},{4,7},{5,6},{6,5},{7,4},{8,11},{9,10},{10,... | collective-permute-start | bytes 233480 | tf_op jit(solution)/shard_map/ppermute | solution.py:434
  69.5 2.2 %collective-permute-start.18 = (bf16[152,256]{1,0:T(8,128)(2,1)S(1)}, bf16[152,256]{1,0:T(8,128)(2,1)S(1)}, u32[]{:S(2)}, u32[]{:S(2)}) collective-permute-start(bf16[152,256]{1,0:T(8,128)(2,1)S(1)} %get-tuple-element.52.refs_0_), channel_id=1, source_target_pairs={{0,1},{1,0},{2,3},{3,2},{4,5},{5,4},{6,7},{7,6},{8,9},{9,8},{10,11... | collective-permute-start | bytes 233480 | tf_op jit(solution)/shard_map/ppermute | solution.py:434
  71.7 2.7 %collective-permute-done.20.refs_3_ = bf16[152,256]{1,0:T(8,128)(2,1)S(1)} collective-permute-done((bf16[152,256]{1,0:T(8,128)(2,1)S(1)}, bf16[152,256]{1,0:T(8,128)(2,1)S(1)}, u32[]{:S(2)}, u32[]{:S(2)}) %collective-permute-start.20) | collective-permute-done | bytes 77856 | tf_op jit(solution)/shard_map/ppermute | solution.py:434
  74.4 1.8 %collective-permute-done.19.refs_2_ = bf16[152,256]{1,0:T(8,128)(2,1)S(1)} collective-permute-done((bf16[152,256]{1,0:T(8,128)(2,1)S(1)}, bf16[152,256]{1,0:T(8,128)(2,1)S(1)}, u32[]{:S(2)}, u32[]{:S(2)}) %collective-permute-start.19) | collective-permute-done | bytes 77856 | tf_op jit(solution)/shard_map/ppermute | solution.py:434
  76.3 2.0 %finish.1 = (f32[9,8192]{1,0:T(8,128)}, f32[9,8192]{1,0:T(8,128)}) custom-call(bf16[152,256]{1,0:T(8,128)(2,1)S(1)} %get-tuple-element.52.refs_0_, bf16[152,256]{1,0:T(8,128)(2,1)S(1)} %collective-permute-done.18.refs_1_, bf16[152,256]{1,0:T(8,128)(2,1)S(1)} %collective-permute-done.19.refs_2_, bf16[152,256]{1,0:T(8,128)(2,1)S(1)} %collective-permute-done.20.refs_3_, ...), custom_call_target="tpu_custom_call" | custom-call | tf_op jit(solution)/shard_map/finish/pallas_call | solution.py:422
  (28 shorter events, 13.6 us)
Async XLA Ops:
  8.2 1.4 %collective-permute-start = (bf16[64,256]{1,0:T(8,128)(2,1)S(1)}, bf16[64,256]{1,0:T(8,128)(2,1)S(1)}, u32[]{:S(2)}, u32[]{:S(2)}) collective-permute-start(bf16[64,256]{1,0:T(8,128)(2,1)S(1)} %get-tuple-element.31.refs_0_), channel_id=1, source_target_pairs={{0,4},{4,0},{8,12},{12,8},{16,20},{20,16},{24,28},{28,24},{1,5},{5... | collective-permute-start | bytes 98312 | tf_op jit(solution)/shard_map/ppermute | solution.py:434
  9.9 5.7 %collective-permute-start.3 = (bf16[64,256]{1,0:T(8,128)(2,1)S(1)}, bf16[64,256]{1,0:T(8,128)(2,1)S(1)}, u32[]{:S(2)}, u32[]{:S(2)}) collective-permute-start(bf16[64,256]{1,0:T(8,128)(2,1)S(1)} %pair.3.refs_0_), channel_id=1, source_target_pairs={{0,24},{4,28},{8,16},{12,20},{16,8},{20,12},{24,0},{28,4},{1,25},{... | collective-permute-start | bytes 98312 | tf_op jit(solution)/shard_map/ppermute | solution.py:434
  13.7 3.9 %collective-permute-start.2 = (bf16[64,256]{1,0:T(8,128)(2,1)S(1)}, bf16[64,256]{1,0:T(8,128)(2,1)S(1)}, u32[]{:S(2)}, u32[]{:S(2)}) collective-permute-start(bf16[64,256]{1,0:T(8,128)(2,1)S(1)} %pair.3.refs_0_), channel_id=1, source_target_pairs={{0,16},{4,20},{8,24},{12,28},{16,0},{20,4},{24,8},{28,12},{1,17},{... | collective-permute-start | bytes 98312 | tf_op jit(solution)/shard_map/ppermute | solution.py:434
  14.2 3.9 %collective-permute-start.1 = (bf16[64,256]{1,0:T(8,128)(2,1)S(1)}, bf16[64,256]{1,0:T(8,128)(2,1)S(1)}, u32[]{:S(2)}, u32[]{:S(2)}) collective-permute-start(bf16[64,256]{1,0:T(8,128)(2,1)S(1)} %pair.3.refs_0_), channel_id=1, source_target_pairs={{0,8},{4,12},{8,0},{12,4},{16,24},{20,28},{24,16},{28,20},{1,9},{5... | collective-permute-start | bytes 98312 | tf_op jit(solution)/shard_map/ppermute | solution.py:434
  20.7 6.3 %collective-permute-start.6 = (bf16[152,256]{1,0:T(8,128)(2,1)S(1)}, bf16[152,256]{1,0:T(8,128)(2,1)S(1)}, u32[]{:S(2)}, u32[]{:S(2)}) collective-permute-start(bf16[152,256]{1,0:T(8,128)(2,1)S(1)} %get-tuple-element.35.refs_0_), channel_id=1, source_target_pairs={{0,3},{1,2},{2,1},{3,0},{4,7},{5,6},{6,5},{7,4},{8,11},{9,10},{10,... | collective-permute-start | bytes 233480 | tf_op jit(solution)/shard_map/ppermute | solution.py:434
  24.3 5.7 %collective-permute-start.5 = (bf16[152,256]{1,0:T(8,128)(2,1)S(1)}, bf16[152,256]{1,0:T(8,128)(2,1)S(1)}, u32[]{:S(2)}, u32[]{:S(2)}) collective-permute-start(bf16[152,256]{1,0:T(8,128)(2,1)S(1)} %get-tuple-element.35.refs_0_), channel_id=1, source_target_pairs={{0,2},{1,3},{2,0},{3,1},{4,6},{5,7},{6,4},{7,5},{8,10},{9,11},{10,... | collective-permute-start | bytes 233480 | tf_op jit(solution)/shard_map/ppermute | solution.py:434
  24.3 5.7 %collective-permute-start.4 = (bf16[152,256]{1,0:T(8,128)(2,1)S(1)}, bf16[152,256]{1,0:T(8,128)(2,1)S(1)}, u32[]{:S(2)}, u32[]{:S(2)}) collective-permute-start(bf16[152,256]{1,0:T(8,128)(2,1)S(1)} %get-tuple-element.35.refs_0_), channel_id=1, source_target_pairs={{0,1},{1,0},{2,3},{3,2},{4,5},{5,4},{6,7},{7,6},{8,9},{9,8},{10,11... | collective-permute-start | bytes 233480 | tf_op jit(solution)/shard_map/ppermute | solution.py:434
  33.6 1.2 %collective-permute-start.7 = (bf16[64,256]{1,0:T(8,128)(2,1)S(1)}, bf16[64,256]{1,0:T(8,128)(2,1)S(1)}, u32[]{:S(2)}, u32[]{:S(2)}) collective-permute-start(bf16[64,256]{1,0:T(8,128)(2,1)S(1)} %get-tuple-element.42.refs_0_), channel_id=1, source_target_pairs={{0,4},{4,0},{8,12},{12,8},{16,20},{20,16},{24,28},{28,24},{1,5},{5... | collective-permute-start | bytes 98312 | tf_op jit(solution)/shard_map/ppermute | solution.py:434
  35.0 4.9 %collective-permute-start.10 = (bf16[64,256]{1,0:T(8,128)(2,1)S(1)}, bf16[64,256]{1,0:T(8,128)(2,1)S(1)}, u32[]{:S(2)}, u32[]{:S(2)}) collective-permute-start(bf16[64,256]{1,0:T(8,128)(2,1)S(1)} %pair.4.refs_0_), channel_id=1, source_target_pairs={{0,24},{4,28},{8,16},{12,20},{16,8},{20,12},{24,0},{28,4},{1,25},{... | collective-permute-start | bytes 98312 | tf_op jit(solution)/shard_map/ppermute | solution.py:434
  36.8 3.9 %collective-permute-start.9 = (bf16[64,256]{1,0:T(8,128)(2,1)S(1)}, bf16[64,256]{1,0:T(8,128)(2,1)S(1)}, u32[]{:S(2)}, u32[]{:S(2)}) collective-permute-start(bf16[64,256]{1,0:T(8,128)(2,1)S(1)} %pair.4.refs_0_), channel_id=1, source_target_pairs={{0,16},{4,20},{8,24},{12,28},{16,0},{20,4},{24,8},{28,12},{1,17},{... | collective-permute-start | bytes 98312 | tf_op jit(solution)/shard_map/ppermute | solution.py:434
  37.4 3.9 %collective-permute-start.8 = (bf16[64,256]{1,0:T(8,128)(2,1)S(1)}, bf16[64,256]{1,0:T(8,128)(2,1)S(1)}, u32[]{:S(2)}, u32[]{:S(2)}) collective-permute-start(bf16[64,256]{1,0:T(8,128)(2,1)S(1)} %pair.4.refs_0_), channel_id=1, source_target_pairs={{0,8},{4,12},{8,0},{12,4},{16,24},{20,28},{24,16},{28,20},{1,9},{5... | collective-permute-start | bytes 98312 | tf_op jit(solution)/shard_map/ppermute | solution.py:434
  44.2 7.1 %collective-permute-start.13 = (bf16[152,256]{1,0:T(8,128)(2,1)S(1)}, bf16[152,256]{1,0:T(8,128)(2,1)S(1)}, u32[]{:S(2)}, u32[]{:S(2)}) collective-permute-start(bf16[152,256]{1,0:T(8,128)(2,1)S(1)} %get-tuple-element.44.refs_0_), channel_id=1, source_target_pairs={{0,3},{1,2},{2,1},{3,0},{4,7},{5,6},{6,5},{7,4},{8,11},{9,10},{10,... | collective-permute-start | bytes 233480 | tf_op jit(solution)/shard_map/ppermute | solution.py:434
  46.4 6.7 %collective-permute-start.12 = (bf16[152,256]{1,0:T(8,128)(2,1)S(1)}, bf16[152,256]{1,0:T(8,128)(2,1)S(1)}, u32[]{:S(2)}, u32[]{:S(2)}) collective-permute-start(bf16[152,256]{1,0:T(8,128)(2,1)S(1)} %get-tuple-element.44.refs_0_), channel_id=1, source_target_pairs={{0,2},{1,3},{2,0},{3,1},{4,6},{5,7},{6,4},{7,5},{8,10},{9,11},{10,... | collective-permute-start | bytes 233480 | tf_op jit(solution)/shard_map/ppermute | solution.py:434
  46.4 6.7 %collective-permute-start.11 = (bf16[152,256]{1,0:T(8,128)(2,1)S(1)}, bf16[152,256]{1,0:T(8,128)(2,1)S(1)}, u32[]{:S(2)}, u32[]{:S(2)}) collective-permute-start(bf16[152,256]{1,0:T(8,128)(2,1)S(1)} %get-tuple-element.44.refs_0_), channel_id=1, source_target_pairs={{0,1},{1,0},{2,3},{3,2},{4,5},{5,4},{6,7},{7,6},{8,9},{9,8},{10,11... | collective-permute-start | bytes 233480 | tf_op jit(solution)/shard_map/ppermute | solution.py:434
  56.7 1.2 %collective-permute-start.14 = (bf16[64,256]{1,0:T(8,128)(2,1)S(1)}, bf16[64,256]{1,0:T(8,128)(2,1)S(1)}, u32[]{:S(2)}, u32[]{:S(2)}) collective-permute-start(bf16[64,256]{1,0:T(8,128)(2,1)S(1)} %get-tuple-element.50.refs_0_), channel_id=1, source_target_pairs={{0,4},{4,0},{8,12},{12,8},{16,20},{20,16},{24,28},{28,24},{1,5},{5... | collective-permute-start | bytes 98312 | tf_op jit(solution)/shard_map/ppermute | solution.py:434
  58.2 4.8 %collective-permute-start.17 = (bf16[64,256]{1,0:T(8,128)(2,1)S(1)}, bf16[64,256]{1,0:T(8,128)(2,1)S(1)}, u32[]{:S(2)}, u32[]{:S(2)}) collective-permute-start(bf16[64,256]{1,0:T(8,128)(2,1)S(1)} %pair.5.refs_0_), channel_id=1, source_target_pairs={{0,24},{4,28},{8,16},{12,20},{16,8},{20,12},{24,0},{28,4},{1,25},{... | collective-permute-start | bytes 98312 | tf_op jit(solution)/shard_map/ppermute | solution.py:434
  60.4 3.9 %collective-permute-start.16 = (bf16[64,256]{1,0:T(8,128)(2,1)S(1)}, bf16[64,256]{1,0:T(8,128)(2,1)S(1)}, u32[]{:S(2)}, u32[]{:S(2)}) collective-permute-start(bf16[64,256]{1,0:T(8,128)(2,1)S(1)} %pair.5.refs_0_), channel_id=1, source_target_pairs={{0,16},{4,20},{8,24},{12,28},{16,0},{20,4},{24,8},{28,12},{1,17},{... | collective-permute-start | bytes 98312 | tf_op jit(solution)/shard_map/ppermute | solution.py:434
  60.6 3.9 %collective-permute-start.15 = (bf16[64,256]{1,0:T(8,128)(2,1)S(1)}, bf16[64,256]{1,0:T(8,128)(2,1)S(1)}, u32[]{:S(2)}, u32[]{:S(2)}) collective-permute-start(bf16[64,256]{1,0:T(8,128)(2,1)S(1)} %pair.5.refs_0_), channel_id=1, source_target_pairs={{0,8},{4,12},{8,0},{12,4},{16,24},{20,28},{24,16},{28,20},{1,9},{5... | collective-permute-start | bytes 98312 | tf_op jit(solution)/shard_map/ppermute | solution.py:434
  67.3 7.2 %collective-permute-start.20 = (bf16[152,256]{1,0:T(8,128)(2,1)S(1)}, bf16[152,256]{1,0:T(8,128)(2,1)S(1)}, u32[]{:S(2)}, u32[]{:S(2)}) collective-permute-start(bf16[152,256]{1,0:T(8,128)(2,1)S(1)} %get-tuple-element.52.refs_0_), channel_id=1, source_target_pairs={{0,3},{1,2},{2,1},{3,0},{4,7},{5,6},{6,5},{7,4},{8,11},{9,10},{10,... | collective-permute-start | bytes 233480 | tf_op jit(solution)/shard_map/ppermute | solution.py:434
  69.5 6.7 %collective-permute-start.19 = (bf16[152,256]{1,0:T(8,128)(2,1)S(1)}, bf16[152,256]{1,0:T(8,128)(2,1)S(1)}, u32[]{:S(2)}, u32[]{:S(2)}) collective-permute-start(bf16[152,256]{1,0:T(8,128)(2,1)S(1)} %get-tuple-element.52.refs_0_), channel_id=1, source_target_pairs={{0,2},{1,3},{2,0},{3,1},{4,6},{5,7},{6,4},{7,5},{8,10},{9,11},{10,... | collective-permute-start | bytes 233480 | tf_op jit(solution)/shard_map/ppermute | solution.py:434
  69.5 6.7 %collective-permute-start.18 = (bf16[152,256]{1,0:T(8,128)(2,1)S(1)}, bf16[152,256]{1,0:T(8,128)(2,1)S(1)}, u32[]{:S(2)}, u32[]{:S(2)}) collective-permute-start(bf16[152,256]{1,0:T(8,128)(2,1)S(1)} %get-tuple-element.52.refs_0_), channel_id=1, source_target_pairs={{0,1},{1,0},{2,3},{3,2},{4,5},{5,4},{6,7},{7,6},{8,9},{9,8},{10,11... | collective-permute-start | bytes 233480 | tf_op jit(solution)/shard_map/ppermute | solution.py:434

commit v4 on v3

--- a/solution.py
+++ b/solution.py
@@ -14,9 +14,9 @@
 VMEM = pl.BlockSpec(memory_space=pltpu.VMEM)
 HBM = pl.BlockSpec(memory_space=pltpu.HBM)
 NT = (((1,), (1,)), ((), ()))
-FETCHES = 4
+FETCHES = (0, 16, 40, 56, 64)
 TAIL = 8
-BACKWARD_SHARE = 7
+BACKWARD_SHARE = 6
 
 
 def in_hbm(value):
@@ -61,10 +61,8 @@
 
 def read_scalars(tile, count):
     row = tile[0:1, :]
-    return [
-        row[:, 3 * n : 3 * n + 1] + row[:, 3 * n + 1 : 3 * n + 2] + row[:, 3 * n + 2 : 3 * n + 3]
-        for n in range(count)
-    ]
+    number = iota(row.shape, 1) % 16 // 3
+    return [total(jnp.where(number == n, row, 0.0)) for n in range(count)]
 
 
 def sym_rows(matrix, size, rows, vector):
@@ -80,20 +78,39 @@
     return jnp.where(iota((tiles, at.shape[1]), 0) == at, 1.0, 0.0).astype(BF16)
 
 
+def swap_halves(even, odd):
+    low = iota(even.shape, 1) < 64
+    return (
+        jnp.where(low, even, pltpu.roll(odd, 64, 1)),
+        jnp.where(low, pltpu.roll(even, 64, 1), odd),
+    )
+
+
+def plane_pairs(size):
+    return [(j, min(j + 1, size - 1)) for j in range(0, size, 2)]
+
+
 def to_tiles(z_ref, zt_ref):
-    planes = z_ref.shape[1]
-    for j in range(z_ref.shape[0]):
-        turned = z_ref[j].T
-        parts = [turned[16 * q : 16 * q + 16, :] for q in range(8)]
-        zt_ref[16 * j : 16 * j + 16, :] = jnp.concatenate(parts, axis=1).astype(BF16)
+    for pair in plane_pairs(z_ref.shape[0]):
+        turned = jnp.concatenate([z_ref[j] for j in pair], axis=0).T
+        for h in range(4):
+            even, odd = (turned[16 * q : 16 * q + 16, :] for q in (2 * h, 2 * h + 1))
+            for j, block in zip(pair, swap_halves(even, odd)):
+                zt_ref[16 * j : 16 * j + 16, 128 * h : 128 * h + 128] = block.astype(BF16)
 
 
 def from_tiles(tiles, t4_ref):
     planes = t4_ref.shape[1]
-    for j in range(t4_ref.shape[0]):
-        block = tiles[16 * j : 16 * j + 16, :]
-        parts = [block[:, q * planes : (q + 1) * planes] for q in range(8)]
-        t4_ref[j] = jnp.concatenate(parts, axis=0).T
+    for pair in plane_pairs(t4_ref.shape[0]):
+        blocks = []
+        for h in range(4):
+            first, second = (
+                tiles[16 * j : 16 * j + 16, 128 * h : 128 * h + 128] for j in pair
+            )
+            blocks += swap_halves(first, second)
+        turned = jnp.concatenate(blocks, axis=0).T
+        for n, j in enumerate(pair):
+            t4_ref[j] = turned[n * planes : (n + 1) * planes, :]
 
 
 def gather_rows(zt_ref, onehot, rows_ref):
@@ -168,11 +185,12 @@
     rn, mn, m8, cn, c8, vn, index_ref, count_ref, split, vrow, zt_ref, rows_ref, part_ref, sems, e_sems,
 ):
     planes, count = r_ref.shape[1], e_ref.shape[0]
-    step = count // FETCHES
+    ends = [count * end // 64 for end in FETCHES]
+    parts = list(zip(ends[:-1], ends[1:]))
     inner = pl.ds(0, 8)
 
     def fetch(n):
-        part = pl.ds(n * step, step)
+        part = pl.ds(parts[n][0], parts[n][1] - parts[n][0])
         return pltpu.make_async_copy(e_hbm.at[part], e_ref.at[part], e_sems.at[n])
 
     def copy(n, src, dst):
@@ -183,8 +201,8 @@
     precond = [copy(3, m_hbm.at[inner, inner], mn), copy(4, m_hbm.at[8], m8)]
     camera = [copy(5, c_hbm.at[inner, inner], cn), copy(6, c_hbm.at[8], c8)]
     inverse = [copy(7, v_hbm, vn)]
-    early = [fetch(n) for n in range(FETCHES // 2)]
-    late = [fetch(n) for n in range(FETCHES // 2, FETCHES)]
+    early = [fetch(n) for n in range(2)]
+    late = [fetch(n) for n in range(2, len(parts))]
     for one in rhs + precond + indices + early + camera + inverse + late:
         one.start()
 
@@ -249,7 +267,7 @@
 
     def forward_chunk(n, one):
         one.wait()
-        forward_pairs(e_ref, rows_ref, part_ref, range(n * step // 2, (n + 1) * step // 2))
+        forward_pairs(e_ref, rows_ref, part_ref, range(parts[n][0] // 2, parts[n][1] // 2))
 
     for n, one in enumerate(early):
         forward_chunk(n, one)
@@ -286,35 +304,48 @@
 
 def pair_kernel(*refs):
     *in_refs, out_ref = refs
-    value = tree_sum([ref[...].astype(F32) for ref in in_refs])
-    scalars = scalar_lanes(read_scalars(value[:, 192:], 3), value.shape[0])
-    out_ref[...] = jnp.concatenate([value[:, :192], scalars], axis=1).astype(BF16)
+    values = [ref[...].astype(F32) for ref in in_refs]
+    scalars = []
+    for k, value in enumerate(values):
+        lanes = value[:, 192:]
+        if k > 0:
+            lanes = jnp.concatenate([lanes[:, 64 - 16 * k :], lanes[:, : 64 - 16 * k]], axis=1)
+        scalars.append(lanes)
+    points = tree_sum([value[:, :192] for value in values])
+    out_ref[...] = jnp.concatenate([points, tree_sum(scalars)], axis=1).astype(BF16)
 
 
 def points_kernel(parts, first, last, *refs):
     summed = tree_sum([ref[...].astype(F32) for ref in refs[:parts]])
     refs = refs[parts:]
     if not first:
-        p_old_ref, scal_old_ref, *refs = refs
+        scal_old_ref, y_old_ref, ct_old_ref, *refs = refs
     e_ref, v_ref, slot_ref, msg_ref, scal_ref, *refs = refs
-    *p_out, yc_ref, c_ref, ct_ref = refs
+    *kept, yc_ref, c_ref, ct_ref = refs
     inner_now, z_c_z, z_c_d = read_scalars(summed[:, 192:], 3)
-    point_sum = summed[:, :192]
     beta, curve = jnp.zeros((1, 1), F32), z_c_z
     if not first:
         beta = inner_now / scal_old_ref[0:1, 0:1]
         curve = z_c_z + beta * (2.0 * z_c_d + beta * scal_old_ref[1:2, 0:1])
-        point_sum = point_sum + beta * p_old_ref[...]
-    if not last:
-        p_out[0][...] = point_sum
-    row = iota((8, 128), 0)
-    scal_ref[...] = jnp.where(row == 0, inner_now, jnp.where(row == 1, curve, beta))
-    p = [point_sum[:, 64 * i : 64 * i + 64] for i in range(3)]
+    p = [summed[:, 64 * i : 64 * i + 64] for i in range(3)]
     y = [tree_sum([v_ref[sym(3, i, j)][:, :64] * p[j] for j in range(3)]) for i in range(3)]
     taken = total(tree_sum([a * b for a, b in zip(p, y)]))
-    rows = c_ref.shape[1]
-    msg_ref[0:rows, :] = backward(e_ref, y, yc_ref, c_ref, ct_ref).astype(BF16)
-    width = msg_ref.shape[1]
+    ct = backward(e_ref, y, yc_ref, c_ref, ct_ref)
+    if not first:
+        crossed = total(tree_sum([p[i] * y_old_ref[i] for i in range(3)]))
+        taken = taken + beta * (2.0 * crossed + beta * scal_old_ref[3:4, 0:1])
+        ct = ct + beta * ct_old_ref[...]
+        y = [y[i] + beta * y_old_ref[i] for i in range(3)]
+    if not last:
+        y_ref, ct_out_ref = kept
+        for i in range(3):
+            y_ref[i] = y[i]
+        ct_out_ref[...] = ct
+    row = iota((8, 128), 0)
+    scal = jnp.where(row == 0, inner_now, jnp.where(row == 1, curve, beta))
+    scal_ref[...] = jnp.where(row == 3, taken, scal)
+    rows, width = ct.shape
+    msg_ref[0:rows, :] = ct.astype(BF16)
     row = iota((TAIL, width), 0)
     tail = jnp.zeros((TAIL, width), F32)
     for at, value in enumerate([slot_ref[0:1, :], slot_ref[1:2, :], *pieces(taken)]):
@@ -322,14 +353,14 @@
     msg_ref[rows : rows + TAIL, :] = tail.astype(BF16)
 
 
-def camera_kernel(parts, first, last, *refs):
+def camera_kernel(masks, first, last, *refs):
+    parts = len(masks)
     msgs, refs = refs[:parts], refs[parts:]
     scal_ref, z_ref, cz_ref, r_ref, *refs = refs
     if not first:
         d_old_ref, cd_old_ref, sol_old_ref, *refs = refs
     if last:
-        sol_out, res_out, all_ref, t4_ref, sol_ref, split = refs
-        res_ref = t4_ref
+        sol_hbm, res_hbm, all_ref, t4_ref, sol_ref, split, sol_out, res_out, sems = refs
     else:
         e_ref, m_ref, c_ref, slot_ref, *refs = refs
         msg_ref, res_ref, sol_ref, zn_ref, czn_ref, *refs = refs
@@ -339,8 +370,8 @@
     planes = z_ref.shape[1]
     rows_all = all_ref.shape[1] - TAIL
     me = lax.axis_index("pts")
-    for k in range(parts):
-        all_ref[me ^ k] = msgs[k][...]
+    for mask, msg in zip(masks, msgs):
+        all_ref[me ^ mask] = msg[...]
     taken, tiles = [], []
     for k in range(parts):
         tail = all_ref[k, rows_all : rows_all + TAIL, :].astype(F32)
@@ -353,6 +384,33 @@
     step_size = inner_now / (curve - tree_sum(taken))
     from_tiles(tree_sum(tiles), t4_ref)
 
+    def update_last(g, carry):
+        rows = pl.ds(pl.multiple_of(g * 8, 8), 8)
+        for j in range(9):
+            d = z_ref[j, rows, :] + beta * d_old_ref[j, rows, :]
+            c_d = cz_ref[j, rows, :] + beta * cd_old_ref[j, rows, :]
+            sol_ref[j, rows, :] = sol_old_ref[j, rows, :] + step_size * d
+            t4_ref[j, rows, :] = r_ref[j, rows, :] - step_size * (c_d - t4_ref[j, rows, :])
+        return carry
+
+    def write(n, src, wide, dst):
+        buffer = split.at[n]
+        for j in range(8):
+            buffer[pl.ds(j, planes, 8), :] = src[j]
+        for a in range(planes):
+            wide[0:8, 128 * a : 128 * a + 128] = buffer[8 * a : 8 * a + 8, :]
+            wide[8:9, 128 * a : 128 * a + 128] = src[8, a : a + 1, :]
+        copy = pltpu.make_async_copy(wide, dst, sems.at[n])
+        copy.start()
+        return copy
+
+    if last:
+        lax.fori_loop(0, planes // 8, update_last, 0, unroll=True)
+        copies = [write(0, sol_ref, sol_out, sol_hbm), write(1, t4_ref, res_out, res_hbm)]
+        for copy in copies:
+            copy.wait()
+        return
+
     def update(g, sums):
         rows = pl.ds(pl.multiple_of(g * 8, 8), 8)
         r, cd = [], []
@@ -361,17 +419,14 @@
             if not first:
                 d = d + beta * d_old_ref[j, rows, :]
                 c_d = c_d + beta * cd_old_ref[j, rows, :]
-                if not last:
-                    d_ref[j, rows, :] = d
-                    cd_ref[j, rows, :] = c_d
+                d_ref[j, rows, :] = d
+                cd_ref[j, rows, :] = c_d
             step = step_size * d
             sol_ref[j, rows, :] = step if first else sol_old_ref[j, rows, :] + step
             r.append(r_ref[j, rows, :] - step_size * (c_d - t4_ref[j, rows, :]))
             cd.append(c_d)
         for j in range(9):
             res_ref[j, rows, :] = r[j]
-        if last:
-            return sums
         z = sym_rows(m_ref, 9, rows, r)
         cz = sym_rows(c_ref, 9, rows, z)
         for j in range(9):
@@ -381,19 +436,6 @@
         return tuple(s + tree_sum([a * b for a, b in p]) for s, p in zip(sums, pairs))
 
     sums = lax.fori_loop(0, planes // 8, update, (jnp.zeros((8, 128), F32),) * 3, unroll=True)
-    if last:
-        for src, dst in ((sol_ref, sol_out), (res_ref, res_out)):
-            for j in range(8):
-                split[pl.ds(j, planes, 8), :] = src[j]
-
-            def body(a, carry):
-                lanes = pl.ds(pl.multiple_of(a * 128, 128), 128)
-                dst[0:8, lanes] = split[pl.ds(pl.multiple_of(a * 8, 8), 8), :]
-                dst[8:9, lanes] = src[8, pl.ds(a, 1), :]
-                return carry
-
-            lax.fori_loop(0, planes, body, 0, unroll=16)
-        return
     to_tiles(zn_ref, zt_ref)
     onehot = tile_onehot(slot_ref[...], 8 * planes, planes)
     gather_rows(zt_ref, onehot, rows_ref)
@@ -418,12 +460,12 @@
     cols_scratch = pltpu.VMEM((rows, width), F32)
     zt_scratch = pltpu.VMEM((rows, tiles), BF16)
 
-    def call(kernel, outs, args, in_specs=None, scratch=(), megabytes=8, name=None):
+    def call(kernel, outs, args, in_specs=None, scratch=(), megabytes=8, out_spec=VMEM, name=None):
         return pl.pallas_call(
             kernel,
             out_shape=outs,
             in_specs=in_specs or [VMEM] * len(args),
-            out_specs=jax.tree.map(lambda _: VMEM, outs),
+            out_specs=jax.tree.map(lambda _: out_spec, outs),
             scratch_shapes=list(scratch),
             compiler_params=pltpu.CompilerParams(vmem_limit_bytes=megabytes * 2**20),
             name=name,
@@ -469,7 +511,7 @@
             rows_scratch,
             part_scratch,
             pltpu.SemaphoreType.DMA((8,)),
-            pltpu.SemaphoreType.DMA((FETCHES,)),
+            pltpu.SemaphoreType.DMA((len(FETCHES) - 1,)),
         ],
         megabytes=16,
         name="start",
@@ -483,16 +525,18 @@
             message_now = call(pair_kernel, message, pair, name="pair")
         parts = exchange(message_now, "cam", n_cam, range(inner, n_cam, inner))
         outs = [shape((rows + TAIL, width), BF16), shape((8, 128), F32)]
-        tile_message, scal, *point_sum = call(
+        kept = [] if last else [shape((3, count, 64), F32), shape((rows, width), F32)]
+        tile_message, scal, *kept = call(
             functools.partial(points_kernel, len(parts), first, last),
-            outs + ([] if last else [shape((count, 192), F32)]),
+            outs + kept,
             (*parts, *old_points, coupling, v6, slot),
             scratch=[pltpu.VMEM((count, cols), F32), rows_scratch, cols_scratch],
             name="points",
         )
-        old_points = (*point_sum, scal)
-        parts = exchange(tile_message, "pts", n_pts, range(1, n_pts))
-        kernel = functools.partial(camera_kernel, len(parts), first, last)
+        old_points = (scal, *kept)
+        masks = (*range(1, n_pts, 2), *range(2, n_pts, 2))
+        parts = exchange(tile_message, "pts", n_pts, masks)
+        kernel = functools.partial(camera_kernel, (0, *masks), first, last)
         common = [
             pltpu.VMEM((n_pts, rows + TAIL, width), BF16),
             pltpu.VMEM((size, planes, 128), F32),
@@ -500,8 +544,17 @@
         args = (*parts, scal, z, cz, residual, *old_camera)
         if last:
             plain = shape((size, cams), F32)
-            scratch = [*common, pltpu.VMEM((size, planes, 128), F32), pltpu.VMEM((8 * planes, 128), F32)]
-            return tuple(call(kernel, [plain, plain], args, scratch=scratch, name="finish"))
+            scratch = [
+                *common,
+                pltpu.VMEM((size, planes, 128), F32),
+                pltpu.VMEM((2, 8 * planes, 128), F32),
+                pltpu.VMEM((size, cams), F32),
+                pltpu.VMEM((size, cams), F32),
+                pltpu.SemaphoreType.DMA((2,)),
+            ]
+            return tuple(
+                call(kernel, [plain, plain], args, scratch=scratch, out_spec=HBM, name="finish")
+            )
         outs = [message, vector, vector, vector, vector] + ([] if first else [vector, vector])
         message_now, residual, solution, z_new, cz_new, *direction = call(
             kernel,

time: 78.4 us -> 77.6 us (0.990)
  starting transfers between devices: 25.3 us -> 23.3 us
  waiting for transfers between devices: 26.5 us -> 28.2 us
    ppermute x21, starting transfers between devices: 25.3 us -> 23.3 us  [exchange(): lax.ppermute(value, axis, [(i, i ^ k) for i in range(axis_size)])]
    ppermute x21, waiting for transfers between devices: 26.5 us -> 28.2 us  [exchange(): lax.ppermute(value, axis, [(i, i ^ k) for i in range(axis_size)])]
  transfers between devices with their start and end apart: 21 -> 21, of which waited for: 18 -> 20; matrix products, arithmetic and copies ran while one was open for 0% -> 0% of each run, Pallas kernels for 0% -> 0%
where the time goes in v4:
time: 77.6 us; the launch traced here: 77.4 us
  waiting for transfers between devices  28.2 us (36%)
  Pallas kernels  25 us (32%)
  starting transfers between devices  23.3 us (30%)
  between operations  0.85 us (1%)
    ppermute x21, waiting for transfers between devices, exchange(): lax.ppermute(value, axis, [(i, i ^ k) for i in range(axis_size)])  28.2 us
    pallas_call x10, Pallas kernels, call(): pl.pallas_call(kernel, out_shape=outs, in_specs=in_specs or [VMEM] * len(...  25 us
    ppermute x21, starting transfers between devices, exchange(): lax.ppermute(value, axis, [(i, i ^ k) for i in range(axis_size)])  23.3 us
  transfers between devices with their start and end apart: 21, of which 20 were waited for; matrix products, arithmetic and copies ran while one was open for 0% of the time, Pallas kernels for 0%

profile of v4, /device:TPU:0, one launch (start us, length us, event | category | flops | bytes accessed | tf_op | source)
XLA Modules:
  0.0 77.4 jit_solution(17277316926642701984)
XLA Ops:
  0.6 7.4 %start.1 = (bf16[64,144,768]{2,1,0:T(8,128)(2,1)S(1)}, f32[45,64,128]{2,1,0:T(8,128)S(1)}, f32[45,64,128]{2,1,0:T(8,128)S(1)}, f32[6,64,128]{2,1,0:T(8,128)S(1)}...) custom-call(f32[9,8192]{1,0:T(8,128)} %rhs_hbm.1, ...), custom_call_target="tpu_custom_call" | custom-call | tf_op jit(solution)/shard_map/start/pallas_call | solution.py:464
  9.6 3.8 %collective-permute-start.3 = (bf16[64,256]{1,0:T(8,128)(2,1)S(1)}, bf16[64,256]{1,0:T(8,128)(2,1)S(1)}, u32[]{:S(2)}, u32[]{:S(2)}) collective-permute-start(bf16[64,256]{1,0:T(8,128)(2,1)S(1)} %pair.3.refs_0_), channel_id=1, source_target_pairs={{0,24},{4,28},{8,16},{12,20},{16,8},{20,12},{24,0},{28,4},{1,25},{... | collective-permute-start | bytes 98312 | tf_op jit(solution)/shard_map/ppermute | solution.py:476
  15.3 2.0 %collective-permute-done.2.refs_2_ = bf16[64,256]{1,0:T(8,128)(2,1)S(1)} collective-permute-done((bf16[64,256]{1,0:T(8,128)(2,1)S(1)}, bf16[64,256]{1,0:T(8,128)(2,1)S(1)}, u32[]{:S(2)}, u32[]{:S(2)}) %collective-permute-start.2) | collective-permute-done | bytes 32800 | tf_op jit(solution)/shard_map/ppermute | solution.py:476
  17.8 2.7 %points.3 = (bf16[152,256]{1,0:T(8,128)(2,1)S(1)}, f32[8,128]{1,0:T(8,128)S(1)}, f32[3,64,64]{2,1,0:T(8,128)S(1)}, f32[144,256]{1,0:T(8,128)S(1)}) custom-call(bf16[64,256]{1,0:T(8,128)(2,1)S(1)} %pair.3.refs_0_, bf16[64,256]{1,0:T(8,128)(2,1)S(1)} %collective-permute-done.1.refs_1_, bf16[64,256]{1,0:T(8,128)(2,1)S(1)} %collective-permute-done.2.refs_2_, ...), custom_call_target="tpu_custom_call" | custom-call | tf_op jit(solution)/shard_map/points/pallas_call | solution.py:464
  20.5 2.7 %collective-permute-start.6 = (bf16[152,256]{1,0:T(8,128)(2,1)S(1)}, bf16[152,256]{1,0:T(8,128)(2,1)S(1)}, u32[]{:S(2)}, u32[]{:S(2)}) collective-permute-start(bf16[152,256]{1,0:T(8,128)(2,1)S(1)} %get-tuple-element.37.refs_0_), channel_id=1, source_target_pairs={{0,2},{1,3},{2,0},{3,1},{4,6},{5,7},{6,4},{7,5},{8,10},{9,11},{10,... | collective-permute-start | bytes 233480 | tf_op jit(solution)/shard_map/ppermute | solution.py:476
  23.1 1.3 %collective-permute-start.5 = (bf16[152,256]{1,0:T(8,128)(2,1)S(1)}, bf16[152,256]{1,0:T(8,128)(2,1)S(1)}, u32[]{:S(2)}, u32[]{:S(2)}) collective-permute-start(bf16[152,256]{1,0:T(8,128)(2,1)S(1)} %get-tuple-element.37.refs_0_), channel_id=1, source_target_pairs={{0,3},{1,2},{2,1},{3,0},{4,7},{5,6},{6,5},{7,4},{8,11},{9,10},{10,... | collective-permute-start | bytes 233480 | tf_op jit(solution)/shard_map/ppermute | solution.py:476
  24.7 3.5 %collective-permute-done.6.refs_3_ = bf16[152,256]{1,0:T(8,128)(2,1)S(1)} collective-permute-done((bf16[152,256]{1,0:T(8,128)(2,1)S(1)}, bf16[152,256]{1,0:T(8,128)(2,1)S(1)}, u32[]{:S(2)}, u32[]{:S(2)}) %collective-permute-start.6) | collective-permute-done | bytes 77856 | tf_op jit(solution)/shard_map/ppermute | solution.py:476
  29.9 3.5 %camera.2 = (bf16[64,256]{1,0:T(8,128)(2,1)S(1)}, f32[9,64,128]{2,1,0:T(8,128)S(1)}, f32[9,64,128]{2,1,0:T(8,128)S(1)}, f32[9,64,128]{2,1,0:T(8,128)S(1)}, f32[9,64,128]{2,1,0:T(8,128)S(1)}) custom-call(bf16[152,256]{1,0:T(8,128)(2,1)S(1)} %get-tuple-element.37.refs_0_, bf16[152,256]{1,0:T(8,128)(2,1)S(1)} %collective-permute-done.4.refs_1_, ...), custom_call_target="tpu_custom_call" | custom-call | tf_op jit(solution)/shard_map/camera/pallas_call | solution.py:464
  34.8 1.4 %collective-permute-start.10 = (bf16[64,256]{1,0:T(8,128)(2,1)S(1)}, bf16[64,256]{1,0:T(8,128)(2,1)S(1)}, u32[]{:S(2)}, u32[]{:S(2)}) collective-permute-start(bf16[64,256]{1,0:T(8,128)(2,1)S(1)} %pair.4.refs_0_), channel_id=1, source_target_pairs={{0,24},{4,28},{8,16},{12,20},{16,8},{20,12},{24,0},{28,4},{1,25},{... | collective-permute-start | bytes 98312 | tf_op jit(solution)/shard_map/ppermute | solution.py:476
  36.6 1.6 %collective-permute-start.8 = (bf16[64,256]{1,0:T(8,128)(2,1)S(1)}, bf16[64,256]{1,0:T(8,128)(2,1)S(1)}, u32[]{:S(2)}, u32[]{:S(2)}) collective-permute-start(bf16[64,256]{1,0:T(8,128)(2,1)S(1)} %pair.4.refs_0_), channel_id=1, source_target_pairs={{0,8},{4,12},{8,0},{12,4},{16,24},{20,28},{24,16},{28,20},{1,9},{5... | collective-permute-start | bytes 98312 | tf_op jit(solution)/shard_map/ppermute | solution.py:476
  38.3 1.3 %collective-permute-done.10.refs_3_ = bf16[64,256]{1,0:T(8,128)(2,1)S(1)} collective-permute-done((bf16[64,256]{1,0:T(8,128)(2,1)S(1)}, bf16[64,256]{1,0:T(8,128)(2,1)S(1)}, u32[]{:S(2)}, u32[]{:S(2)}) %collective-permute-start.10) | collective-permute-done | bytes 32800 | tf_op jit(solution)/shard_map/ppermute | solution.py:476
  40.5 2.8 %points.4 = (bf16[152,256]{1,0:T(8,128)(2,1)S(1)}, f32[8,128]{1,0:T(8,128)S(1)}, f32[3,64,64]{2,1,0:T(8,128)S(1)}, f32[144,256]{1,0:T(8,128)S(1)}) custom-call(bf16[64,256]{1,0:T(8,128)(2,1)S(1)} %pair.4.refs_0_, bf16[64,256]{1,0:T(8,128)(2,1)S(1)} %collective-permute-done.8.refs_1_, bf16[64,256]{1,0:T(8,128)(2,1)S(1)} %collective-permute-done.9.refs_2_, ...), custom_call_target="tpu_custom_call" | custom-call | tf_op jit(solution)/shard_map/points/pallas_call | solution.py:464
  43.4 2.4 %collective-permute-start.13 = (bf16[152,256]{1,0:T(8,128)(2,1)S(1)}, bf16[152,256]{1,0:T(8,128)(2,1)S(1)}, u32[]{:S(2)}, u32[]{:S(2)}) collective-permute-start(bf16[152,256]{1,0:T(8,128)(2,1)S(1)} %get-tuple-element.47.refs_0_), channel_id=1, source_target_pairs={{0,2},{1,3},{2,0},{3,1},{4,6},{5,7},{6,4},{7,5},{8,10},{9,11},{10,... | collective-permute-start | bytes 233480 | tf_op jit(solution)/shard_map/ppermute | solution.py:476
  46.9 3.9 %collective-permute-done.13.refs_3_ = bf16[152,256]{1,0:T(8,128)(2,1)S(1)} collective-permute-done((bf16[152,256]{1,0:T(8,128)(2,1)S(1)}, bf16[152,256]{1,0:T(8,128)(2,1)S(1)}, u32[]{:S(2)}, u32[]{:S(2)}) %collective-permute-start.13) | collective-permute-done | bytes 77856 | tf_op jit(solution)/shard_map/ppermute | solution.py:476
  50.8 1.4 %collective-permute-done.12.refs_2_ = bf16[152,256]{1,0:T(8,128)(2,1)S(1)} collective-permute-done((bf16[152,256]{1,0:T(8,128)(2,1)S(1)}, bf16[152,256]{1,0:T(8,128)(2,1)S(1)}, u32[]{:S(2)}, u32[]{:S(2)}) %collective-permute-start.12) | collective-permute-done | bytes 77856 | tf_op jit(solution)/shard_map/ppermute | solution.py:476
  52.3 3.6 %camera.3 = (bf16[64,256]{1,0:T(8,128)(2,1)S(1)}, f32[9,64,128]{2,1,0:T(8,128)S(1)}, f32[9,64,128]{2,1,0:T(8,128)S(1)}, f32[9,64,128]{2,1,0:T(8,128)S(1)}, f32[9...) custom-call(bf16[152,256]{1,0:T(8,128)(2,1)S(1)} %get-tuple-element.47.refs_0_, ...), custom_call_target="tpu_custom_call" | custom-call | tf_op jit(solution)/shard_map/camera/pallas_call | solution.py:464
  57.2 2.5 %collective-permute-start.17 = (bf16[64,256]{1,0:T(8,128)(2,1)S(1)}, bf16[64,256]{1,0:T(8,128)(2,1)S(1)}, u32[]{:S(2)}, u32[]{:S(2)}) collective-permute-start(bf16[64,256]{1,0:T(8,128)(2,1)S(1)} %pair.5.refs_0_), channel_id=1, source_target_pairs={{0,24},{4,28},{8,16},{12,20},{16,8},{20,12},{24,0},{28,4},{1,25},{... | collective-permute-start | bytes 98312 | tf_op jit(solution)/shard_map/ppermute | solution.py:476
  60.7 1.3 %collective-permute-done.17.refs_3_ = bf16[64,256]{1,0:T(8,128)(2,1)S(1)} collective-permute-done((bf16[64,256]{1,0:T(8,128)(2,1)S(1)}, bf16[64,256]{1,0:T(8,128)(2,1)S(1)}, u32[]{:S(2)}, u32[]{:S(2)}) %collective-permute-start.17) | collective-permute-done | bytes 32800 | tf_op jit(solution)/shard_map/ppermute | solution.py:476
  62.0 1.6 %collective-permute-done.16.refs_2_ = bf16[64,256]{1,0:T(8,128)(2,1)S(1)} collective-permute-done((bf16[64,256]{1,0:T(8,128)(2,1)S(1)}, bf16[64,256]{1,0:T(8,128)(2,1)S(1)}, u32[]{:S(2)}, u32[]{:S(2)}) %collective-permute-start.16) | collective-permute-done | bytes 32800 | tf_op jit(solution)/shard_map/ppermute | solution.py:476
  64.0 2.7 %points.5 = (bf16[152,256]{1,0:T(8,128)(2,1)S(1)}, f32[8,128]{1,0:T(8,128)S(1)}) custom-call(bf16[64,256]{1,0:T(8,128)(2,1)S(1)} %pair.5.refs_0_, bf16[64,256]{1,0:T(8,128)(2,1)S(1)} %collective-permute-done.15.refs_1_, bf16[64,256]{1,0:T(8,128)(2,1)S(1)} %collective-permute-done.16.refs_2_, bf16[64,256]{1,0:T(8,128)(2,1)S(1)} %collective-permute-done.17.refs_3_, ...), custom_call_target="tpu_custom_call" | custom-call | tf_op jit(solution)/shard_map/points/pallas_call | solution.py:464
  66.7 1.5 %collective-permute-start.20 = (bf16[152,256]{1,0:T(8,128)(2,1)S(1)}, bf16[152,256]{1,0:T(8,128)(2,1)S(1)}, u32[]{:S(2)}, u32[]{:S(2)}) collective-permute-start(bf16[152,256]{1,0:T(8,128)(2,1)S(1)} %get-tuple-element.56.refs_0_), channel_id=1, source_target_pairs={{0,2},{1,3},{2,0},{3,1},{4,6},{5,7},{6,4},{7,5},{8,10},{9,11},{10,... | collective-permute-start | bytes 233480 | tf_op jit(solution)/shard_map/ppermute | solution.py:476
  68.2 1.5 %collective-permute-start.19 = (bf16[152,256]{1,0:T(8,128)(2,1)S(1)}, bf16[152,256]{1,0:T(8,128)(2,1)S(1)}, u32[]{:S(2)}, u32[]{:S(2)}) collective-permute-start(bf16[152,256]{1,0:T(8,128)(2,1)S(1)} %get-tuple-element.56.refs_0_), channel_id=1, source_target_pairs={{0,3},{1,2},{2,1},{3,0},{4,7},{5,6},{6,5},{7,4},{8,11},{9,10},{10,... | collective-permute-start | bytes 233480 | tf_op jit(solution)/shard_map/ppermute | solution.py:476
  70.3 4.4 %collective-permute-done.20.refs_3_ = bf16[152,256]{1,0:T(8,128)(2,1)S(1)} collective-permute-done((bf16[152,256]{1,0:T(8,128)(2,1)S(1)}, bf16[152,256]{1,0:T(8,128)(2,1)S(1)}, u32[]{:S(2)}, u32[]{:S(2)}) %collective-permute-start.20) | collective-permute-done | bytes 77856 | tf_op jit(solution)/shard_map/ppermute | solution.py:476
  75.4 1.9 %finish.1 = (f32[9,8192]{1,0:T(8,128)}, f32[9,8192]{1,0:T(8,128)}) custom-call(bf16[152,256]{1,0:T(8,128)(2,1)S(1)} %get-tuple-element.56.refs_0_, bf16[152,256]{1,0:T(8,128)(2,1)S(1)} %collective-permute-done.18.refs_1_, bf16[152,256]{1,0:T(8,128)(2,1)S(1)} %collective-permute-done.19.refs_2_, bf16[152,256]{1,0:T(8,128)(2,1)S(1)} %collective-permute-done.20.refs_3_, ...), custom_call_target="tpu_custom_call" | custom-call | tf_op jit(solution)/shard_map/finish/pallas_call | solution.py:464
  (28 shorter events, 13.8 us)
Async XLA Ops:
  8.1 1.4 %collective-permute-start = (bf16[64,256]{1,0:T(8,128)(2,1)S(1)}, bf16[64,256]{1,0:T(8,128)(2,1)S(1)}, u32[]{:S(2)}, u32[]{:S(2)}) collective-permute-start(bf16[64,256]{1,0:T(8,128)(2,1)S(1)} %get-tuple-element.33.refs_0_), channel_id=1, source_target_pairs={{0,4},{4,0},{8,12},{12,8},{16,20},{20,16},{24,28},{28,24},{1,5},{5... | collective-permute-start | bytes 98312 | tf_op jit(solution)/shard_map/ppermute | solution.py:476
  9.6 5.7 %collective-permute-start.3 = (bf16[64,256]{1,0:T(8,128)(2,1)S(1)}, bf16[64,256]{1,0:T(8,128)(2,1)S(1)}, u32[]{:S(2)}, u32[]{:S(2)}) collective-permute-start(bf16[64,256]{1,0:T(8,128)(2,1)S(1)} %pair.3.refs_0_), channel_id=1, source_target_pairs={{0,24},{4,28},{8,16},{12,20},{16,8},{20,12},{24,0},{28,4},{1,25},{... | collective-permute-start | bytes 98312 | tf_op jit(solution)/shard_map/ppermute | solution.py:476
  13.4 3.9 %collective-permute-start.2 = (bf16[64,256]{1,0:T(8,128)(2,1)S(1)}, bf16[64,256]{1,0:T(8,128)(2,1)S(1)}, u32[]{:S(2)}, u32[]{:S(2)}) collective-permute-start(bf16[64,256]{1,0:T(8,128)(2,1)S(1)} %pair.3.refs_0_), channel_id=1, source_target_pairs={{0,16},{4,20},{8,24},{12,28},{16,0},{20,4},{24,8},{28,12},{1,17},{... | collective-permute-start | bytes 98312 | tf_op jit(solution)/shard_map/ppermute | solution.py:476
  13.9 3.9 %collective-permute-start.1 = (bf16[64,256]{1,0:T(8,128)(2,1)S(1)}, bf16[64,256]{1,0:T(8,128)(2,1)S(1)}, u32[]{:S(2)}, u32[]{:S(2)}) collective-permute-start(bf16[64,256]{1,0:T(8,128)(2,1)S(1)} %pair.3.refs_0_), channel_id=1, source_target_pairs={{0,8},{4,12},{8,0},{12,4},{16,24},{20,28},{24,16},{28,20},{1,9},{5... | collective-permute-start | bytes 98312 | tf_op jit(solution)/shard_map/ppermute | solution.py:476
  20.5 7.8 %collective-permute-start.6 = (bf16[152,256]{1,0:T(8,128)(2,1)S(1)}, bf16[152,256]{1,0:T(8,128)(2,1)S(1)}, u32[]{:S(2)}, u32[]{:S(2)}) collective-permute-start(bf16[152,256]{1,0:T(8,128)(2,1)S(1)} %get-tuple-element.37.refs_0_), channel_id=1, source_target_pairs={{0,2},{1,3},{2,0},{3,1},{4,6},{5,7},{6,4},{7,5},{8,10},{9,11},{10,... | collective-permute-start | bytes 233480 | tf_op jit(solution)/shard_map/ppermute | solution.py:476
  23.1 6.4 %collective-permute-start.5 = (bf16[152,256]{1,0:T(8,128)(2,1)S(1)}, bf16[152,256]{1,0:T(8,128)(2,1)S(1)}, u32[]{:S(2)}, u32[]{:S(2)}) collective-permute-start(bf16[152,256]{1,0:T(8,128)(2,1)S(1)} %get-tuple-element.37.refs_0_), channel_id=1, source_target_pairs={{0,3},{1,2},{2,1},{3,0},{4,7},{5,6},{6,5},{7,4},{8,11},{9,10},{10,... | collective-permute-start | bytes 233480 | tf_op jit(solution)/shard_map/ppermute | solution.py:476
  24.5 5.4 %collective-permute-start.4 = (bf16[152,256]{1,0:T(8,128)(2,1)S(1)}, bf16[152,256]{1,0:T(8,128)(2,1)S(1)}, u32[]{:S(2)}, u32[]{:S(2)}) collective-permute-start(bf16[152,256]{1,0:T(8,128)(2,1)S(1)} %get-tuple-element.37.refs_0_), channel_id=1, source_target_pairs={{0,1},{1,0},{2,3},{3,2},{4,5},{5,4},{6,7},{7,6},{8,9},{9,8},{10,11... | collective-permute-start | bytes 233480 | tf_op jit(solution)/shard_map/ppermute | solution.py:476
  33.4 1.2 %collective-permute-start.7 = (bf16[64,256]{1,0:T(8,128)(2,1)S(1)}, bf16[64,256]{1,0:T(8,128)(2,1)S(1)}, u32[]{:S(2)}, u32[]{:S(2)}) collective-permute-start(bf16[64,256]{1,0:T(8,128)(2,1)S(1)} %get-tuple-element.44.refs_0_), channel_id=1, source_target_pairs={{0,4},{4,0},{8,12},{12,8},{16,20},{20,16},{24,28},{28,24},{1,5},{5... | collective-permute-start | bytes 98312 | tf_op jit(solution)/shard_map/ppermute | solution.py:476
  34.8 4.8 %collective-permute-start.10 = (bf16[64,256]{1,0:T(8,128)(2,1)S(1)}, bf16[64,256]{1,0:T(8,128)(2,1)S(1)}, u32[]{:S(2)}, u32[]{:S(2)}) collective-permute-start(bf16[64,256]{1,0:T(8,128)(2,1)S(1)} %pair.4.refs_0_), channel_id=1, source_target_pairs={{0,24},{4,28},{8,16},{12,20},{16,8},{20,12},{24,0},{28,4},{1,25},{... | collective-permute-start | bytes 98312 | tf_op jit(solution)/shard_map/ppermute | solution.py:476
  36.2 3.9 %collective-permute-start.9 = (bf16[64,256]{1,0:T(8,128)(2,1)S(1)}, bf16[64,256]{1,0:T(8,128)(2,1)S(1)}, u32[]{:S(2)}, u32[]{:S(2)}) collective-permute-start(bf16[64,256]{1,0:T(8,128)(2,1)S(1)} %pair.4.refs_0_), channel_id=1, source_target_pairs={{0,16},{4,20},{8,24},{12,28},{16,0},{20,4},{24,8},{28,12},{1,17},{... | collective-permute-start | bytes 98312 | tf_op jit(solution)/shard_map/ppermute | solution.py:476
  36.6 3.9 %collective-permute-start.8 = (bf16[64,256]{1,0:T(8,128)(2,1)S(1)}, bf16[64,256]{1,0:T(8,128)(2,1)S(1)}, u32[]{:S(2)}, u32[]{:S(2)}) collective-permute-start(bf16[64,256]{1,0:T(8,128)(2,1)S(1)} %pair.4.refs_0_), channel_id=1, source_target_pairs={{0,8},{4,12},{8,0},{12,4},{16,24},{20,28},{24,16},{28,20},{1,9},{5... | collective-permute-start | bytes 98312 | tf_op jit(solution)/shard_map/ppermute | solution.py:476
  43.4 7.4 %collective-permute-start.13 = (bf16[152,256]{1,0:T(8,128)(2,1)S(1)}, bf16[152,256]{1,0:T(8,128)(2,1)S(1)}, u32[]{:S(2)}, u32[]{:S(2)}) collective-permute-start(bf16[152,256]{1,0:T(8,128)(2,1)S(1)} %get-tuple-element.47.refs_0_), channel_id=1, source_target_pairs={{0,2},{1,3},{2,0},{3,1},{4,6},{5,7},{6,4},{7,5},{8,10},{9,11},{10,... | collective-permute-start | bytes 233480 | tf_op jit(solution)/shard_map/ppermute | solution.py:476
  45.8 6.4 %collective-permute-start.12 = (bf16[152,256]{1,0:T(8,128)(2,1)S(1)}, bf16[152,256]{1,0:T(8,128)(2,1)S(1)}, u32[]{:S(2)}, u32[]{:S(2)}) collective-permute-start(bf16[152,256]{1,0:T(8,128)(2,1)S(1)} %get-tuple-element.47.refs_0_), channel_id=1, source_target_pairs={{0,3},{1,2},{2,1},{3,0},{4,7},{5,6},{6,5},{7,4},{8,11},{9,10},{10,... | collective-permute-start | bytes 233480 | tf_op jit(solution)/shard_map/ppermute | solution.py:476
  46.3 5.9 %collective-permute-start.11 = (bf16[152,256]{1,0:T(8,128)(2,1)S(1)}, bf16[152,256]{1,0:T(8,128)(2,1)S(1)}, u32[]{:S(2)}, u32[]{:S(2)}) collective-permute-start(bf16[152,256]{1,0:T(8,128)(2,1)S(1)} %get-tuple-element.47.refs_0_), channel_id=1, source_target_pairs={{0,1},{1,0},{2,3},{3,2},{4,5},{5,4},{6,7},{7,6},{8,9},{9,8},{10,11... | collective-permute-start | bytes 233480 | tf_op jit(solution)/shard_map/ppermute | solution.py:476
  55.8 1.2 %collective-permute-start.14 = (bf16[64,256]{1,0:T(8,128)(2,1)S(1)}, bf16[64,256]{1,0:T(8,128)(2,1)S(1)}, u32[]{:S(2)}, u32[]{:S(2)}) collective-permute-start(bf16[64,256]{1,0:T(8,128)(2,1)S(1)} %get-tuple-element.53.refs_0_), channel_id=1, source_target_pairs={{0,4},{4,0},{8,12},{12,8},{16,20},{20,16},{24,28},{28,24},{1,5},{5... | collective-permute-start | bytes 98312 | tf_op jit(solution)/shard_map/ppermute | solution.py:476
  57.2 4.8 %collective-permute-start.17 = (bf16[64,256]{1,0:T(8,128)(2,1)S(1)}, bf16[64,256]{1,0:T(8,128)(2,1)S(1)}, u32[]{:S(2)}, u32[]{:S(2)}) collective-permute-start(bf16[64,256]{1,0:T(8,128)(2,1)S(1)} %pair.5.refs_0_), channel_id=1, source_target_pairs={{0,24},{4,28},{8,16},{12,20},{16,8},{20,12},{24,0},{28,4},{1,25},{... | collective-permute-start | bytes 98312 | tf_op jit(solution)/shard_map/ppermute | solution.py:476
  59.7 3.9 %collective-permute-start.16 = (bf16[64,256]{1,0:T(8,128)(2,1)S(1)}, bf16[64,256]{1,0:T(8,128)(2,1)S(1)}, u32[]{:S(2)}, u32[]{:S(2)}) collective-permute-start(bf16[64,256]{1,0:T(8,128)(2,1)S(1)} %pair.5.refs_0_), channel_id=1, source_target_pairs={{0,16},{4,20},{8,24},{12,28},{16,0},{20,4},{24,8},{28,12},{1,17},{... | collective-permute-start | bytes 98312 | tf_op jit(solution)/shard_map/ppermute | solution.py:476
  60.1 3.9 %collective-permute-start.15 = (bf16[64,256]{1,0:T(8,128)(2,1)S(1)}, bf16[64,256]{1,0:T(8,128)(2,1)S(1)}, u32[]{:S(2)}, u32[]{:S(2)}) collective-permute-start(bf16[64,256]{1,0:T(8,128)(2,1)S(1)} %pair.5.refs_0_), channel_id=1, source_target_pairs={{0,8},{4,12},{8,0},{12,4},{16,24},{20,28},{24,16},{28,20},{1,9},{5... | collective-permute-start | bytes 98312 | tf_op jit(solution)/shard_map/ppermute | solution.py:476
  66.7 7.9 %collective-permute-start.20 = (bf16[152,256]{1,0:T(8,128)(2,1)S(1)}, bf16[152,256]{1,0:T(8,128)(2,1)S(1)}, u32[]{:S(2)}, u32[]{:S(2)}) collective-permute-start(bf16[152,256]{1,0:T(8,128)(2,1)S(1)} %get-tuple-element.56.refs_0_), channel_id=1, source_target_pairs={{0,2},{1,3},{2,0},{3,1},{4,6},{5,7},{6,4},{7,5},{8,10},{9,11},{10,... | collective-permute-start | bytes 233480 | tf_op jit(solution)/shard_map/ppermute | solution.py:476
  68.2 6.4 %collective-permute-start.19 = (bf16[152,256]{1,0:T(8,128)(2,1)S(1)}, bf16[152,256]{1,0:T(8,128)(2,1)S(1)}, u32[]{:S(2)}, u32[]{:S(2)}) collective-permute-start(bf16[152,256]{1,0:T(8,128)(2,1)S(1)} %get-tuple-element.56.refs_0_), channel_id=1, source_target_pairs={{0,3},{1,2},{2,1},{3,0},{4,7},{5,6},{6,5},{7,4},{8,11},{9,10},{10,... | collective-permute-start | bytes 233480 | tf_op jit(solution)/shard_map/ppermute | solution.py:476
  69.7 5.7 %collective-permute-start.18 = (bf16[152,256]{1,0:T(8,128)(2,1)S(1)}, bf16[152,256]{1,0:T(8,128)(2,1)S(1)}, u32[]{:S(2)}, u32[]{:S(2)}) collective-permute-start(bf16[152,256]{1,0:T(8,128)(2,1)S(1)} %get-tuple-element.56.refs_0_), channel_id=1, source_target_pairs={{0,1},{1,0},{2,3},{3,2},{4,5},{5,4},{6,7},{7,6},{8,9},{9,8},{10,11... | collective-permute-start | bytes 233480 | tf_op jit(solution)/shard_map/ppermute | solution.py:476

commit v5 on v4

--- a/solution.py
+++ b/solution.py
@@ -370,8 +370,9 @@
     planes = z_ref.shape[1]
     rows_all = all_ref.shape[1] - TAIL
     me = lax.axis_index("pts")
-    for mask, msg in zip(masks, msgs):
-        all_ref[me ^ mask] = msg[...]
+    odd = lax.axis_index("cam") % 2
+    for (even_mask, odd_mask), msg in zip(masks, msgs):
+        all_ref[me ^ (even_mask + odd * (odd_mask - even_mask))] = msg[...]
     taken, tiles = [], []
     for k in range(parts):
         tail = all_ref[k, rows_all : rows_all + TAIL, :].astype(F32)
@@ -411,36 +412,50 @@
             copy.wait()
         return
 
+    def rows_of(g):
+        return pl.ds(8 * g, 8)
+
+    direction_of_c = cz_ref if first else cd_ref
+    for g in range(planes // 8):
+        rows, r = rows_of(g), []
+        for j in range(9):
+            c_d = cz_ref[j, rows, :]
+            if not first:
+                c_d = c_d + beta * cd_old_ref[j, rows, :]
+                cd_ref[j, rows, :] = c_d
+            r.append(r_ref[j, rows, :] - step_size * (c_d - t4_ref[j, rows, :]))
+        z = sym_rows(m_ref, 9, rows, r)
+        for j in range(9):
+            res_ref[j, rows, :] = r[j]
+            zn_ref[j, rows, :] = z[j]
+
     def update(g, sums):
-        rows = pl.ds(pl.multiple_of(g * 8, 8), 8)
-        r, cd = [], []
+        rows = rows_of(g)
+        z = [zn_ref[j, rows, :] for j in range(9)]
+        r = [res_ref[j, rows, :] for j in range(9)]
+        cd = [direction_of_c[j, rows, :] for j in range(9)]
+        cz = sym_rows(c_ref, 9, rows, z)
         for j in range(9):
-            d, c_d = z_ref[j, rows, :], cz_ref[j, rows, :]
+            czn_ref[j, rows, :] = cz[j]
+            d = z_ref[j, rows, :]
             if not first:
                 d = d + beta * d_old_ref[j, rows, :]
-                c_d = c_d + beta * cd_old_ref[j, rows, :]
                 d_ref[j, rows, :] = d
-                cd_ref[j, rows, :] = c_d
             step = step_size * d
             sol_ref[j, rows, :] = step if first else sol_old_ref[j, rows, :] + step
-            r.append(r_ref[j, rows, :] - step_size * (c_d - t4_ref[j, rows, :]))
-            cd.append(c_d)
-        for j in range(9):
-            res_ref[j, rows, :] = r[j]
-        z = sym_rows(m_ref, 9, rows, r)
-        cz = sym_rows(c_ref, 9, rows, z)
-        for j in range(9):
-            zn_ref[j, rows, :] = z[j]
-            czn_ref[j, rows, :] = cz[j]
         pairs = (zip(r, z), zip(z, cz), zip(z, cd))
-        return tuple(s + tree_sum([a * b for a, b in p]) for s, p in zip(sums, pairs))
-
-    sums = lax.fori_loop(0, planes // 8, update, (jnp.zeros((8, 128), F32),) * 3, unroll=True)
+        return [s + tree_sum([a * b for a, b in p]) for s, p in zip(sums, pairs)]
+
     to_tiles(zn_ref, zt_ref)
-    onehot = tile_onehot(slot_ref[...], 8 * planes, planes)
-    gather_rows(zt_ref, onehot, rows_ref)
+    gather_rows(zt_ref, tile_onehot(slot_ref[...], 8 * planes, planes), rows_ref)
     count = e_ref.shape[0]
-    forward_pairs(e_ref, rows_ref, part_ref, range(count // 2))
+    sums = [jnp.zeros((8, 128), F32)] * 3
+    steps = planes // 8
+    for g in range(2 * steps):
+        pairs = range(g * count // (4 * steps), (g + 1) * count // (4 * steps))
+        forward_pairs(e_ref, rows_ref, part_ref, pairs)
+        if g < steps:
+            sums = update(g, sums)
     scalars = scalar_lanes([total(s) for s in sums], count)
     msg_ref[...] = jnp.concatenate([forward_sum(part_ref, count), scalars], axis=1).astype(BF16)
 
@@ -475,6 +490,17 @@
         return [value] + [
             lax.ppermute(value, axis, [(i, i ^ k) for i in range(axis_size)]) for k in masks
         ]
+
+    odd_order = (*range(1, n_pts, 2), *range(2, n_pts, 2))
+    pts_masks = tuple(zip(odd_order[-1:] + odd_order[:-1], odd_order))
+
+    def points_permute(value, masks):
+        pairs = [
+            (cam * n_pts + pts, cam * n_pts + (pts ^ masks[cam % 2]))
+            for cam in range(n_cam)
+            for pts in range(n_pts)
+        ]
+        return lax.ppermute(value, ("cam", "pts"), pairs)
 
     coupling, m4, c4, v6, residual, z, cz, slot, message_now = call(
         start_kernel,
@@ -534,9 +560,8 @@
             name="points",
         )
         old_points = (scal, *kept)
-        masks = (*range(1, n_pts, 2), *range(2, n_pts, 2))
-        parts = exchange(tile_message, "pts", n_pts, masks)
-        kernel = functools.partial(camera_kernel, (0, *masks), first, last)
+        parts = [tile_message] + [points_permute(tile_message, masks) for masks in pts_masks]
+        kernel = functools.partial(camera_kernel, ((0, 0), *pts_masks), first, last)
         common = [
             pltpu.VMEM((n_pts, rows + TAIL, width), BF16),
             pltpu.VMEM((size, planes, 128), F32),

time: 77.6 us -> 76.8 us (0.990)
  waiting for transfers between devices: 28.2 us -> 25.7 us
  starting transfers between devices: 23.3 us -> 25.4 us
    ppermute x21 -> x12, waiting for transfers between devices: 28.2 us -> 12.3 us  [exchange(): lax.ppermute(value, axis, [(i, i ^ k) for i in range(axis_size)])]
    ppermute x0 -> x9, waiting for transfers between devices: none -> 13.4 us  [points_permute(): return lax.ppermute(value, ('cam', 'pts'), pairs)]
    ppermute x0 -> x9, starting transfers between devices: none -> 13.4 us  [points_permute(): return lax.ppermute(value, ('cam', 'pts'), pairs)]
    ppermute x21 -> x12, starting transfers between devices: 23.3 us -> 12 us  [exchange(): lax.ppermute(value, axis, [(i, i ^ k) for i in range(axis_size)])]
  transfers between devices with their start and end apart: 21 -> 21, of which waited for: 20 -> 19; matrix products, arithmetic and copies ran while one was open for 0% -> 0% of each run, Pallas kernels for 0% -> 0%
where the time goes in v5:
time: 76.8 us; the launch traced here: 76.7 us
  waiting for transfers between devices  25.7 us (33%)
  starting transfers between devices  25.4 us (33%)
  Pallas kernels  24.8 us (32%)
  between operations  0.85 us (1%)
    pallas_call x10, Pallas kernels, call(): pl.pallas_call(kernel, out_shape=outs, in_specs=in_specs or [VMEM] * len(...  24.8 us
    ppermute x9, waiting for transfers between devices, points_permute(): return lax.ppermute(value, ('cam', 'pts'), pairs)  13.4 us
    ppermute x9, starting transfers between devices, points_permute(): return lax.ppermute(value, ('cam', 'pts'), pairs)  13.4 us
    ppermute x12, waiting for transfers between devices, exchange(): lax.ppermute(value, axis, [(i, i ^ k) for i in range(axis_size)])  12.3 us
    ppermute x12, starting transfers between devices, exchange(): lax.ppermute(value, axis, [(i, i ^ k) for i in range(axis_size)])  12 us
  transfers between devices with their start and end apart: 21, of which 19 were waited for; matrix products, arithmetic and copies ran while one was open for 0% of the time, Pallas kernels for 0%

profile of v5, /device:TPU:0, one launch (start us, length us, event | category | flops | bytes accessed | tf_op | source)
XLA Modules:
  0.0 76.7 jit_solution(11450562627576504937)
XLA Ops:
  0.6 7.4 %start.1 = (bf16[64,144,768]{2,1,0:T(8,128)(2,1)S(1)}, f32[45,64,128]{2,1,0:T(8,128)S(1)}, f32[45,64,128]{2,1,0:T(8,128)S(1)}, f32[6,64,128]{2,1,0:T(8,128)S(1)}...) custom-call(f32[9,8192]{1,0:T(8,128)} %rhs_hbm.1, ...), custom_call_target="tpu_custom_call" | custom-call | tf_op jit(solution)/shard_map/start/pallas_call | solution.py:479
  9.6 3.8 %collective-permute-start.3 = (bf16[64,256]{1,0:T(8,128)(2,1)S(1)}, bf16[64,256]{1,0:T(8,128)(2,1)S(1)}, u32[]{:S(2)}, u32[]{:S(2)}) collective-permute-start(bf16[64,256]{1,0:T(8,128)(2,1)S(1)} %pair.3.refs_0_), channel_id=1, source_target_pairs={{0,24},{4,28},{8,16},{12,20},{16,8},{20,12},{24,0},{28,4},{1,25},{... | collective-permute-start | bytes 98312 | tf_op jit(solution)/shard_map/ppermute | solution.py:491
  14.0 1.3 %collective-permute-done.3.refs_3_ = bf16[64,256]{1,0:T(8,128)(2,1)S(1)} collective-permute-done((bf16[64,256]{1,0:T(8,128)(2,1)S(1)}, bf16[64,256]{1,0:T(8,128)(2,1)S(1)}, u32[]{:S(2)}, u32[]{:S(2)}) %collective-permute-start.3) | collective-permute-done | bytes 32800 | tf_op jit(solution)/shard_map/ppermute | solution.py:491
  15.3 2.0 %collective-permute-done.2.refs_2_ = bf16[64,256]{1,0:T(8,128)(2,1)S(1)} collective-permute-done((bf16[64,256]{1,0:T(8,128)(2,1)S(1)}, bf16[64,256]{1,0:T(8,128)(2,1)S(1)}, u32[]{:S(2)}, u32[]{:S(2)}) %collective-permute-start.2) | collective-permute-done | bytes 32800 | tf_op jit(solution)/shard_map/ppermute | solution.py:491
  17.8 2.7 %points.3 = (bf16[152,256]{1,0:T(8,128)(2,1)S(1)}, f32[8,128]{1,0:T(8,128)S(1)}, f32[3,64,64]{2,1,0:T(8,128)S(1)}, f32[144,256]{1,0:T(8,128)S(1)}) custom-call(bf16[64,256]{1,0:T(8,128)(2,1)S(1)} %pair.3.refs_0_, bf16[64,256]{1,0:T(8,128)(2,1)S(1)} %collective-permute-done.1.refs_1_, bf16[64,256]{1,0:T(8,128)(2,1)S(1)} %collective-permute-done.2.refs_2_, ...), custom_call_target="tpu_custom_call" | custom-call | tf_op jit(solution)/shard_map/points/pallas_call | solution.py:479
  20.5 3.7 %collective-permute-start.6 = (bf16[152,256]{1,0:T(8,128)(2,1)S(1)}, bf16[152,256]{1,0:T(8,128)(2,1)S(1)}, u32[]{:S(2)}, u32[]{:S(2)}) collective-permute-start(bf16[152,256]{1,0:T(8,128)(2,1)S(1)} %get-tuple-element.37.refs_0_), channel_id=1, source_target_pairs={{0,3},{1,2},{2,1},{3,0},{4,6},{5,7},{6,4},{7,5},{8,11},{9,10},{10,... | collective-permute-start | bytes 233480 | tf_op jit(solution)/shard_map/ppermute | solution.py:503
  24.9 2.7 %collective-permute-done.6.refs_3_ = bf16[152,256]{1,0:T(8,128)(2,1)S(1)} collective-permute-done((bf16[152,256]{1,0:T(8,128)(2,1)S(1)}, bf16[152,256]{1,0:T(8,128)(2,1)S(1)}, u32[]{:S(2)}, u32[]{:S(2)}) %collective-permute-start.6) | collective-permute-done | bytes 77856 | tf_op jit(solution)/shard_map/ppermute | solution.py:503
  29.5 3.5 %camera.2 = (bf16[64,256]{1,0:T(8,128)(2,1)S(1)}, f32[9,64,128]{2,1,0:T(8,128)S(1)}, f32[9,64,128]{2,1,0:T(8,128)S(1)}, f32[9,64,128]{2,1,0:T(8,128)S(1)}, f32[9,64,128]{2,1,0:T(8,128)S(1)}) custom-call(bf16[152,256]{1,0:T(8,128)(2,1)S(1)} %get-tuple-element.37.refs_0_, bf16[152,256]{1,0:T(8,128)(2,1)S(1)} %collective-permute-done.4.refs_1_, ...), custom_call_target="tpu_custom_call" | custom-call | tf_op jit(solution)/shard_map/camera/pallas_call | solution.py:479
  34.3 1.5 %collective-permute-start.10 = (bf16[64,256]{1,0:T(8,128)(2,1)S(1)}, bf16[64,256]{1,0:T(8,128)(2,1)S(1)}, u32[]{:S(2)}, u32[]{:S(2)}) collective-permute-start(bf16[64,256]{1,0:T(8,128)(2,1)S(1)} %pair.4.refs_0_), channel_id=1, source_target_pairs={{0,24},{4,28},{8,16},{12,20},{16,8},{20,12},{24,0},{28,4},{1,25},{... | collective-permute-start | bytes 98312 | tf_op jit(solution)/shard_map/ppermute | solution.py:491
  36.3 1.5 %collective-permute-start.8 = (bf16[64,256]{1,0:T(8,128)(2,1)S(1)}, bf16[64,256]{1,0:T(8,128)(2,1)S(1)}, u32[]{:S(2)}, u32[]{:S(2)}) collective-permute-start(bf16[64,256]{1,0:T(8,128)(2,1)S(1)} %pair.4.refs_0_), channel_id=1, source_target_pairs={{0,8},{4,12},{8,0},{12,4},{16,24},{20,28},{24,16},{28,20},{1,9},{5... | collective-permute-start | bytes 98312 | tf_op jit(solution)/shard_map/ppermute | solution.py:491
  37.8 1.3 %collective-permute-done.10.refs_3_ = bf16[64,256]{1,0:T(8,128)(2,1)S(1)} collective-permute-done((bf16[64,256]{1,0:T(8,128)(2,1)S(1)}, bf16[64,256]{1,0:T(8,128)(2,1)S(1)}, u32[]{:S(2)}, u32[]{:S(2)}) %collective-permute-start.10) | collective-permute-done | bytes 32800 | tf_op jit(solution)/shard_map/ppermute | solution.py:491
  40.2 2.8 %points.4 = (bf16[152,256]{1,0:T(8,128)(2,1)S(1)}, f32[8,128]{1,0:T(8,128)S(1)}, f32[3,64,64]{2,1,0:T(8,128)S(1)}, f32[144,256]{1,0:T(8,128)S(1)}) custom-call(bf16[64,256]{1,0:T(8,128)(2,1)S(1)} %pair.4.refs_0_, bf16[64,256]{1,0:T(8,128)(2,1)S(1)} %collective-permute-done.8.refs_1_, bf16[64,256]{1,0:T(8,128)(2,1)S(1)} %collective-permute-done.9.refs_2_, ...), custom_call_target="tpu_custom_call" | custom-call | tf_op jit(solution)/shard_map/points/pallas_call | solution.py:479
  43.1 3.6 %collective-permute-start.13 = (bf16[152,256]{1,0:T(8,128)(2,1)S(1)}, bf16[152,256]{1,0:T(8,128)(2,1)S(1)}, u32[]{:S(2)}, u32[]{:S(2)}) collective-permute-start(bf16[152,256]{1,0:T(8,128)(2,1)S(1)} %get-tuple-element.47.refs_0_), channel_id=1, source_target_pairs={{0,3},{1,2},{2,1},{3,0},{4,6},{5,7},{6,4},{7,5},{8,11},{9,10},{10,... | collective-permute-start | bytes 233480 | tf_op jit(solution)/shard_map/ppermute | solution.py:503
  47.5 2.6 %collective-permute-done.13.refs_3_ = bf16[152,256]{1,0:T(8,128)(2,1)S(1)} collective-permute-done((bf16[152,256]{1,0:T(8,128)(2,1)S(1)}, bf16[152,256]{1,0:T(8,128)(2,1)S(1)}, u32[]{:S(2)}, u32[]{:S(2)}) %collective-permute-start.13) | collective-permute-done | bytes 77856 | tf_op jit(solution)/shard_map/ppermute | solution.py:503
  50.1 2.1 %collective-permute-done.12.refs_2_ = bf16[152,256]{1,0:T(8,128)(2,1)S(1)} collective-permute-done((bf16[152,256]{1,0:T(8,128)(2,1)S(1)}, bf16[152,256]{1,0:T(8,128)(2,1)S(1)}, u32[]{:S(2)}, u32[]{:S(2)}) %collective-permute-start.12) | collective-permute-done | bytes 77856 | tf_op jit(solution)/shard_map/ppermute | solution.py:503
  52.2 3.4 %camera.3 = (bf16[64,256]{1,0:T(8,128)(2,1)S(1)}, f32[9,64,128]{2,1,0:T(8,128)S(1)}, f32[9,64,128]{2,1,0:T(8,128)S(1)}, f32[9,64,128]{2,1,0:T(8,128)S(1)}, f32[9...) custom-call(bf16[152,256]{1,0:T(8,128)(2,1)S(1)} %get-tuple-element.47.refs_0_, ...), custom_call_target="tpu_custom_call" | custom-call | tf_op jit(solution)/shard_map/camera/pallas_call | solution.py:479
  57.0 2.1 %collective-permute-start.17 = (bf16[64,256]{1,0:T(8,128)(2,1)S(1)}, bf16[64,256]{1,0:T(8,128)(2,1)S(1)}, u32[]{:S(2)}, u32[]{:S(2)}) collective-permute-start(bf16[64,256]{1,0:T(8,128)(2,1)S(1)} %pair.5.refs_0_), channel_id=1, source_target_pairs={{0,24},{4,28},{8,16},{12,20},{16,8},{20,12},{24,0},{28,4},{1,25},{... | collective-permute-start | bytes 98312 | tf_op jit(solution)/shard_map/ppermute | solution.py:491
  60.5 1.4 %collective-permute-done.17.refs_3_ = bf16[64,256]{1,0:T(8,128)(2,1)S(1)} collective-permute-done((bf16[64,256]{1,0:T(8,128)(2,1)S(1)}, bf16[64,256]{1,0:T(8,128)(2,1)S(1)}, u32[]{:S(2)}, u32[]{:S(2)}) %collective-permute-start.17) | collective-permute-done | bytes 32800 | tf_op jit(solution)/shard_map/ppermute | solution.py:491
  63.3 2.7 %points.5 = (bf16[152,256]{1,0:T(8,128)(2,1)S(1)}, f32[8,128]{1,0:T(8,128)S(1)}) custom-call(bf16[64,256]{1,0:T(8,128)(2,1)S(1)} %pair.5.refs_0_, bf16[64,256]{1,0:T(8,128)(2,1)S(1)} %collective-permute-done.15.refs_1_, bf16[64,256]{1,0:T(8,128)(2,1)S(1)} %collective-permute-done.16.refs_2_, bf16[64,256]{1,0:T(8,128)(2,1)S(1)} %collective-permute-done.17.refs_3_, ...), custom_call_target="tpu_custom_call" | custom-call | tf_op jit(solution)/shard_map/points/pallas_call | solution.py:479
  66.0 2.8 %collective-permute-start.20 = (bf16[152,256]{1,0:T(8,128)(2,1)S(1)}, bf16[152,256]{1,0:T(8,128)(2,1)S(1)}, u32[]{:S(2)}, u32[]{:S(2)}) collective-permute-start(bf16[152,256]{1,0:T(8,128)(2,1)S(1)} %get-tuple-element.56.refs_0_), channel_id=1, source_target_pairs={{0,3},{1,2},{2,1},{3,0},{4,6},{5,7},{6,4},{7,5},{8,11},{9,10},{10,... | collective-permute-start | bytes 233480 | tf_op jit(solution)/shard_map/ppermute | solution.py:503
  68.8 1.7 %collective-permute-start.18 = (bf16[152,256]{1,0:T(8,128)(2,1)S(1)}, bf16[152,256]{1,0:T(8,128)(2,1)S(1)}, u32[]{:S(2)}, u32[]{:S(2)}) collective-permute-start(bf16[152,256]{1,0:T(8,128)(2,1)S(1)} %get-tuple-element.56.refs_0_), channel_id=1, source_target_pairs={{0,2},{1,3},{2,0},{3,1},{4,5},{5,4},{6,7},{7,6},{8,10},{9,11},{10,... | collective-permute-start | bytes 233480 | tf_op jit(solution)/shard_map/ppermute | solution.py:503
  70.5 2.5 %collective-permute-done.20.refs_3_ = bf16[152,256]{1,0:T(8,128)(2,1)S(1)} collective-permute-done((bf16[152,256]{1,0:T(8,128)(2,1)S(1)}, bf16[152,256]{1,0:T(8,128)(2,1)S(1)}, u32[]{:S(2)}, u32[]{:S(2)}) %collective-permute-start.20) | collective-permute-done | bytes 77856 | tf_op jit(solution)/shard_map/ppermute | solution.py:503
  73.0 1.7 %collective-permute-done.19.refs_2_ = bf16[152,256]{1,0:T(8,128)(2,1)S(1)} collective-permute-done((bf16[152,256]{1,0:T(8,128)(2,1)S(1)}, bf16[152,256]{1,0:T(8,128)(2,1)S(1)}, u32[]{:S(2)}, u32[]{:S(2)}) %collective-permute-start.19) | collective-permute-done | bytes 77856 | tf_op jit(solution)/shard_map/ppermute | solution.py:503
  74.7 1.9 %finish.1 = (f32[9,8192]{1,0:T(8,128)}, f32[9,8192]{1,0:T(8,128)}) custom-call(bf16[152,256]{1,0:T(8,128)(2,1)S(1)} %get-tuple-element.56.refs_0_, bf16[152,256]{1,0:T(8,128)(2,1)S(1)} %collective-permute-done.18.refs_1_, bf16[152,256]{1,0:T(8,128)(2,1)S(1)} %collective-permute-done.19.refs_2_, bf16[152,256]{1,0:T(8,128)(2,1)S(1)} %collective-permute-done.20.refs_3_, ...), custom_call_target="tpu_custom_call" | custom-call | tf_op jit(solution)/shard_map/finish/pallas_call | solution.py:479
  (28 shorter events, 13.5 us)
Async XLA Ops:
  8.1 1.4 %collective-permute-start = (bf16[64,256]{1,0:T(8,128)(2,1)S(1)}, bf16[64,256]{1,0:T(8,128)(2,1)S(1)}, u32[]{:S(2)}, u32[]{:S(2)}) collective-permute-start(bf16[64,256]{1,0:T(8,128)(2,1)S(1)} %get-tuple-element.33.refs_0_), channel_id=1, source_target_pairs={{0,4},{4,0},{8,12},{12,8},{16,20},{20,16},{24,28},{28,24},{1,5},{5... | collective-permute-start | bytes 98312 | tf_op jit(solution)/shard_map/ppermute | solution.py:491
  9.6 5.7 %collective-permute-start.3 = (bf16[64,256]{1,0:T(8,128)(2,1)S(1)}, bf16[64,256]{1,0:T(8,128)(2,1)S(1)}, u32[]{:S(2)}, u32[]{:S(2)}) collective-permute-start(bf16[64,256]{1,0:T(8,128)(2,1)S(1)} %pair.3.refs_0_), channel_id=1, source_target_pairs={{0,24},{4,28},{8,16},{12,20},{16,8},{20,12},{24,0},{28,4},{1,25},{... | collective-permute-start | bytes 98312 | tf_op jit(solution)/shard_map/ppermute | solution.py:491
  13.4 3.9 %collective-permute-start.2 = (bf16[64,256]{1,0:T(8,128)(2,1)S(1)}, bf16[64,256]{1,0:T(8,128)(2,1)S(1)}, u32[]{:S(2)}, u32[]{:S(2)}) collective-permute-start(bf16[64,256]{1,0:T(8,128)(2,1)S(1)} %pair.3.refs_0_), channel_id=1, source_target_pairs={{0,16},{4,20},{8,24},{12,28},{16,0},{20,4},{24,8},{28,12},{1,17},{... | collective-permute-start | bytes 98312 | tf_op jit(solution)/shard_map/ppermute | solution.py:491
  13.9 3.9 %collective-permute-start.1 = (bf16[64,256]{1,0:T(8,128)(2,1)S(1)}, bf16[64,256]{1,0:T(8,128)(2,1)S(1)}, u32[]{:S(2)}, u32[]{:S(2)}) collective-permute-start(bf16[64,256]{1,0:T(8,128)(2,1)S(1)} %pair.3.refs_0_), channel_id=1, source_target_pairs={{0,8},{4,12},{8,0},{12,4},{16,24},{20,28},{24,16},{28,20},{1,9},{5... | collective-permute-start | bytes 98312 | tf_op jit(solution)/shard_map/ppermute | solution.py:491
  20.5 7.1 %collective-permute-start.6 = (bf16[152,256]{1,0:T(8,128)(2,1)S(1)}, bf16[152,256]{1,0:T(8,128)(2,1)S(1)}, u32[]{:S(2)}, u32[]{:S(2)}) collective-permute-start(bf16[152,256]{1,0:T(8,128)(2,1)S(1)} %get-tuple-element.37.refs_0_), channel_id=1, source_target_pairs={{0,3},{1,2},{2,1},{3,0},{4,6},{5,7},{6,4},{7,5},{8,11},{9,10},{10,... | collective-permute-start | bytes 233480 | tf_op jit(solution)/shard_map/ppermute | solution.py:503
  24.2 4.4 %collective-permute-start.5 = (bf16[152,256]{1,0:T(8,128)(2,1)S(1)}, bf16[152,256]{1,0:T(8,128)(2,1)S(1)}, u32[]{:S(2)}, u32[]{:S(2)}) collective-permute-start(bf16[152,256]{1,0:T(8,128)(2,1)S(1)} %get-tuple-element.37.refs_0_), channel_id=1, source_target_pairs={{0,1},{1,0},{2,3},{3,2},{4,7},{5,6},{6,5},{7,4},{8,9},{9,8},{10,11... | collective-permute-start | bytes 233480 | tf_op jit(solution)/shard_map/ppermute | solution.py:503
  24.2 5.3 %collective-permute-start.4 = (bf16[152,256]{1,0:T(8,128)(2,1)S(1)}, bf16[152,256]{1,0:T(8,128)(2,1)S(1)}, u32[]{:S(2)}, u32[]{:S(2)}) collective-permute-start(bf16[152,256]{1,0:T(8,128)(2,1)S(1)} %get-tuple-element.37.refs_0_), channel_id=1, source_target_pairs={{0,2},{1,3},{2,0},{3,1},{4,5},{5,4},{6,7},{7,6},{8,10},{9,11},{10,... | collective-permute-start | bytes 233480 | tf_op jit(solution)/shard_map/ppermute | solution.py:503
  32.9 1.2 %collective-permute-start.7 = (bf16[64,256]{1,0:T(8,128)(2,1)S(1)}, bf16[64,256]{1,0:T(8,128)(2,1)S(1)}, u32[]{:S(2)}, u32[]{:S(2)}) collective-permute-start(bf16[64,256]{1,0:T(8,128)(2,1)S(1)} %get-tuple-element.44.refs_0_), channel_id=1, source_target_pairs={{0,4},{4,0},{8,12},{12,8},{16,20},{20,16},{24,28},{28,24},{1,5},{5... | collective-permute-start | bytes 98312 | tf_op jit(solution)/shard_map/ppermute | solution.py:491
  34.3 4.8 %collective-permute-start.10 = (bf16[64,256]{1,0:T(8,128)(2,1)S(1)}, bf16[64,256]{1,0:T(8,128)(2,1)S(1)}, u32[]{:S(2)}, u32[]{:S(2)}) collective-permute-start(bf16[64,256]{1,0:T(8,128)(2,1)S(1)} %pair.4.refs_0_), channel_id=1, source_target_pairs={{0,24},{4,28},{8,16},{12,20},{16,8},{20,12},{24,0},{28,4},{1,25},{... | collective-permute-start | bytes 98312 | tf_op jit(solution)/shard_map/ppermute | solution.py:491
  35.8 3.9 %collective-permute-start.9 = (bf16[64,256]{1,0:T(8,128)(2,1)S(1)}, bf16[64,256]{1,0:T(8,128)(2,1)S(1)}, u32[]{:S(2)}, u32[]{:S(2)}) collective-permute-start(bf16[64,256]{1,0:T(8,128)(2,1)S(1)} %pair.4.refs_0_), channel_id=1, source_target_pairs={{0,16},{4,20},{8,24},{12,28},{16,0},{20,4},{24,8},{28,12},{1,17},{... | collective-permute-start | bytes 98312 | tf_op jit(solution)/shard_map/ppermute | solution.py:491
  36.3 3.9 %collective-permute-start.8 = (bf16[64,256]{1,0:T(8,128)(2,1)S(1)}, bf16[64,256]{1,0:T(8,128)(2,1)S(1)}, u32[]{:S(2)}, u32[]{:S(2)}) collective-permute-start(bf16[64,256]{1,0:T(8,128)(2,1)S(1)} %pair.4.refs_0_), channel_id=1, source_target_pairs={{0,8},{4,12},{8,0},{12,4},{16,24},{20,28},{24,16},{28,20},{1,9},{5... | collective-permute-start | bytes 98312 | tf_op jit(solution)/shard_map/ppermute | solution.py:491
  43.1 7.0 %collective-permute-start.13 = (bf16[152,256]{1,0:T(8,128)(2,1)S(1)}, bf16[152,256]{1,0:T(8,128)(2,1)S(1)}, u32[]{:S(2)}, u32[]{:S(2)}) collective-permute-start(bf16[152,256]{1,0:T(8,128)(2,1)S(1)} %get-tuple-element.47.refs_0_), channel_id=1, source_target_pairs={{0,3},{1,2},{2,1},{3,0},{4,6},{5,7},{6,4},{7,5},{8,11},{9,10},{10,... | collective-permute-start | bytes 233480 | tf_op jit(solution)/shard_map/ppermute | solution.py:503
  46.6 5.6 %collective-permute-start.12 = (bf16[152,256]{1,0:T(8,128)(2,1)S(1)}, bf16[152,256]{1,0:T(8,128)(2,1)S(1)}, u32[]{:S(2)}, u32[]{:S(2)}) collective-permute-start(bf16[152,256]{1,0:T(8,128)(2,1)S(1)} %get-tuple-element.47.refs_0_), channel_id=1, source_target_pairs={{0,1},{1,0},{2,3},{3,2},{4,7},{5,6},{6,5},{7,4},{8,9},{9,8},{10,11... | collective-permute-start | bytes 233480 | tf_op jit(solution)/shard_map/ppermute | solution.py:503
  46.6 5.6 %collective-permute-start.11 = (bf16[152,256]{1,0:T(8,128)(2,1)S(1)}, bf16[152,256]{1,0:T(8,128)(2,1)S(1)}, u32[]{:S(2)}, u32[]{:S(2)}) collective-permute-start(bf16[152,256]{1,0:T(8,128)(2,1)S(1)} %get-tuple-element.47.refs_0_), channel_id=1, source_target_pairs={{0,2},{1,3},{2,0},{3,1},{4,5},{5,4},{6,7},{7,6},{8,10},{9,11},{10,... | collective-permute-start | bytes 233480 | tf_op jit(solution)/shard_map/ppermute | solution.py:503
  55.6 1.2 %collective-permute-start.14 = (bf16[64,256]{1,0:T(8,128)(2,1)S(1)}, bf16[64,256]{1,0:T(8,128)(2,1)S(1)}, u32[]{:S(2)}, u32[]{:S(2)}) collective-permute-start(bf16[64,256]{1,0:T(8,128)(2,1)S(1)} %get-tuple-element.53.refs_0_), channel_id=1, source_target_pairs={{0,4},{4,0},{8,12},{12,8},{16,20},{20,16},{24,28},{28,24},{1,5},{5... | collective-permute-start | bytes 98312 | tf_op jit(solution)/shard_map/ppermute | solution.py:491
  57.0 4.9 %collective-permute-start.17 = (bf16[64,256]{1,0:T(8,128)(2,1)S(1)}, bf16[64,256]{1,0:T(8,128)(2,1)S(1)}, u32[]{:S(2)}, u32[]{:S(2)}) collective-permute-start(bf16[64,256]{1,0:T(8,128)(2,1)S(1)} %pair.5.refs_0_), channel_id=1, source_target_pairs={{0,24},{4,28},{8,16},{12,20},{16,8},{20,12},{24,0},{28,4},{1,25},{... | collective-permute-start | bytes 98312 | tf_op jit(solution)/shard_map/ppermute | solution.py:491
  59.1 3.9 %collective-permute-start.16 = (bf16[64,256]{1,0:T(8,128)(2,1)S(1)}, bf16[64,256]{1,0:T(8,128)(2,1)S(1)}, u32[]{:S(2)}, u32[]{:S(2)}) collective-permute-start(bf16[64,256]{1,0:T(8,128)(2,1)S(1)} %pair.5.refs_0_), channel_id=1, source_target_pairs={{0,16},{4,20},{8,24},{12,28},{16,0},{20,4},{24,8},{28,12},{1,17},{... | collective-permute-start | bytes 98312 | tf_op jit(solution)/shard_map/ppermute | solution.py:491
  59.4 3.9 %collective-permute-start.15 = (bf16[64,256]{1,0:T(8,128)(2,1)S(1)}, bf16[64,256]{1,0:T(8,128)(2,1)S(1)}, u32[]{:S(2)}, u32[]{:S(2)}) collective-permute-start(bf16[64,256]{1,0:T(8,128)(2,1)S(1)} %pair.5.refs_0_), channel_id=1, source_target_pairs={{0,8},{4,12},{8,0},{12,4},{16,24},{20,28},{24,16},{28,20},{1,9},{5... | collective-permute-start | bytes 98312 | tf_op jit(solution)/shard_map/ppermute | solution.py:491
  66.0 6.9 %collective-permute-start.20 = (bf16[152,256]{1,0:T(8,128)(2,1)S(1)}, bf16[152,256]{1,0:T(8,128)(2,1)S(1)}, u32[]{:S(2)}, u32[]{:S(2)}) collective-permute-start(bf16[152,256]{1,0:T(8,128)(2,1)S(1)} %get-tuple-element.56.refs_0_), channel_id=1, source_target_pairs={{0,3},{1,2},{2,1},{3,0},{4,6},{5,7},{6,4},{7,5},{8,11},{9,10},{10,... | collective-permute-start | bytes 233480 | tf_op jit(solution)/shard_map/ppermute | solution.py:503
  68.8 5.8 %collective-permute-start.19 = (bf16[152,256]{1,0:T(8,128)(2,1)S(1)}, bf16[152,256]{1,0:T(8,128)(2,1)S(1)}, u32[]{:S(2)}, u32[]{:S(2)}) collective-permute-start(bf16[152,256]{1,0:T(8,128)(2,1)S(1)} %get-tuple-element.56.refs_0_), channel_id=1, source_target_pairs={{0,1},{1,0},{2,3},{3,2},{4,7},{5,6},{6,5},{7,4},{8,9},{9,8},{10,11... | collective-permute-start | bytes 233480 | tf_op jit(solution)/shard_map/ppermute | solution.py:503
  68.8 5.8 %collective-permute-start.18 = (bf16[152,256]{1,0:T(8,128)(2,1)S(1)}, bf16[152,256]{1,0:T(8,128)(2,1)S(1)}, u32[]{:S(2)}, u32[]{:S(2)}) collective-permute-start(bf16[152,256]{1,0:T(8,128)(2,1)S(1)} %get-tuple-element.56.refs_0_), channel_id=1, source_target_pairs={{0,2},{1,3},{2,0},{3,1},{4,5},{5,4},{6,7},{7,6},{8,10},{9,11},{10,... | collective-permute-start | bytes 233480 | tf_op jit(solution)/shard_map/ppermute | solution.py:503

commit v6 on v5

--- a/solution.py
+++ b/solution.py
@@ -373,26 +373,10 @@
     odd = lax.axis_index("cam") % 2
     for (even_mask, odd_mask), msg in zip(masks, msgs):
         all_ref[me ^ (even_mask + odd * (odd_mask - even_mask))] = msg[...]
-    taken, tiles = [], []
-    for k in range(parts):
-        tail = all_ref[k, rows_all : rows_all + TAIL, :].astype(F32)
-        taken.append(tail[2:3, 0:1] + tail[3:4, 0:1] + tail[4:5, 0:1])
-        onehot = tile_onehot(tail, 8 * planes, planes)
-        tiles.append(
-            lax.dot_general(all_ref[k, 0:rows_all, :], onehot, NT, preferred_element_type=F32)
-        )
+    tails = [all_ref[k, rows_all : rows_all + TAIL, :].astype(F32) for k in range(parts)]
+    taken = [tail[2:3, 0:1] + tail[3:4, 0:1] + tail[4:5, 0:1] for tail in tails]
     inner_now, curve, beta = scal_ref[0:1, 0:1], scal_ref[1:2, 0:1], scal_ref[2:3, 0:1]
     step_size = inner_now / (curve - tree_sum(taken))
-    from_tiles(tree_sum(tiles), t4_ref)
-
-    def update_last(g, carry):
-        rows = pl.ds(pl.multiple_of(g * 8, 8), 8)
-        for j in range(9):
-            d = z_ref[j, rows, :] + beta * d_old_ref[j, rows, :]
-            c_d = cz_ref[j, rows, :] + beta * cd_old_ref[j, rows, :]
-            sol_ref[j, rows, :] = sol_old_ref[j, rows, :] + step_size * d
-            t4_ref[j, rows, :] = r_ref[j, rows, :] - step_size * (c_d - t4_ref[j, rows, :])
-        return carry
 
     def write(n, src, wide, dst):
         buffer = split.at[n]
@@ -405,15 +389,34 @@
         copy.start()
         return copy
 
+    def rows_of(g):
+        return pl.ds(8 * g, 8)
+
+    copies = []
     if last:
-        lax.fori_loop(0, planes // 8, update_last, 0, unroll=True)
-        copies = [write(0, sol_ref, sol_out, sol_hbm), write(1, t4_ref, res_out, res_hbm)]
+        for g in range(planes // 8):
+            rows = rows_of(g)
+            for j in range(9):
+                d = z_ref[j, rows, :] + beta * d_old_ref[j, rows, :]
+                sol_ref[j, rows, :] = sol_old_ref[j, rows, :] + step_size * d
+        copies.append(write(0, sol_ref, sol_out, sol_hbm))
+    tiles = []
+    for k in range(parts):
+        onehot = tile_onehot(tails[k], 8 * planes, planes)
+        tiles.append(
+            lax.dot_general(all_ref[k, 0:rows_all, :], onehot, NT, preferred_element_type=F32)
+        )
+    from_tiles(tree_sum(tiles), t4_ref)
+    if last:
+        for g in range(planes // 8):
+            rows = rows_of(g)
+            for j in range(9):
+                c_d = cz_ref[j, rows, :] + beta * cd_old_ref[j, rows, :]
+                t4_ref[j, rows, :] = r_ref[j, rows, :] - step_size * (c_d - t4_ref[j, rows, :])
+        copies.append(write(1, t4_ref, res_out, res_hbm))
         for copy in copies:
             copy.wait()
         return
-
-    def rows_of(g):
-        return pl.ds(8 * g, 8)
 
     direction_of_c = cz_ref if first else cd_ref
     for g in range(planes // 8):

time: 76.8 us -> 76.8 us (level)
  no operation moved by 1% of the time
where the time goes in v6:
time: 76.8 us; the launch traced here: 76.7 us
  waiting for transfers between devices  25.7 us (33%)
  starting transfers between devices  25.4 us (33%)
  Pallas kernels  24.8 us (32%)
  between operations  0.85 us (1%)
    pallas_call x10, Pallas kernels, call(): pl.pallas_call(kernel, out_shape=outs, in_specs=in_specs or [VMEM] * len(...  24.8 us
    ppermute x9, waiting for transfers between devices, points_permute(): return lax.ppermute(value, ('cam', 'pts'), pairs)  13.4 us
    ppermute x9, starting transfers between devices, points_permute(): return lax.ppermute(value, ('cam', 'pts'), pairs)  13.4 us
    ppermute x12, waiting for transfers between devices, exchange(): lax.ppermute(value, axis, [(i, i ^ k) for i in range(axis_size)])  12.3 us
    ppermute x12, starting transfers between devices, exchange(): lax.ppermute(value, axis, [(i, i ^ k) for i in range(axis_size)])  12 us
  transfers between devices with their start and end apart: 21, of which 19 were waited for; matrix products, arithmetic and copies ran while one was open for 0% of the time, Pallas kernels for 0%

profile of v6, /device:TPU:0, one launch (start us, length us, event | category | flops | bytes accessed | tf_op | source)
XLA Modules:
  0.0 76.7 jit_solution(10132652662233696370)
XLA Ops:
  0.6 7.4 %start.1 = (bf16[64,144,768]{2,1,0:T(8,128)(2,1)S(1)}, f32[45,64,128]{2,1,0:T(8,128)S(1)}, f32[45,64,128]{2,1,0:T(8,128)S(1)}, f32[6,64,128]{2,1,0:T(8,128)S(1)}...) custom-call(f32[9,8192]{1,0:T(8,128)} %rhs_hbm.1, ...), custom_call_target="tpu_custom_call" | custom-call | tf_op jit(solution)/shard_map/start/pallas_call | solution.py:482
  9.6 3.8 %collective-permute-start.3 = (bf16[64,256]{1,0:T(8,128)(2,1)S(1)}, bf16[64,256]{1,0:T(8,128)(2,1)S(1)}, u32[]{:S(2)}, u32[]{:S(2)}) collective-permute-start(bf16[64,256]{1,0:T(8,128)(2,1)S(1)} %pair.3.refs_0_), channel_id=1, source_target_pairs={{0,24},{4,28},{8,16},{12,20},{16,8},{20,12},{24,0},{28,4},{1,25},{... | collective-permute-start | bytes 98312 | tf_op jit(solution)/shard_map/ppermute | solution.py:494
  14.0 1.3 %collective-permute-done.3.refs_3_ = bf16[64,256]{1,0:T(8,128)(2,1)S(1)} collective-permute-done((bf16[64,256]{1,0:T(8,128)(2,1)S(1)}, bf16[64,256]{1,0:T(8,128)(2,1)S(1)}, u32[]{:S(2)}, u32[]{:S(2)}) %collective-permute-start.3) | collective-permute-done | bytes 32800 | tf_op jit(solution)/shard_map/ppermute | solution.py:494
  15.3 2.0 %collective-permute-done.2.refs_2_ = bf16[64,256]{1,0:T(8,128)(2,1)S(1)} collective-permute-done((bf16[64,256]{1,0:T(8,128)(2,1)S(1)}, bf16[64,256]{1,0:T(8,128)(2,1)S(1)}, u32[]{:S(2)}, u32[]{:S(2)}) %collective-permute-start.2) | collective-permute-done | bytes 32800 | tf_op jit(solution)/shard_map/ppermute | solution.py:494
  17.8 2.7 %points.3 = (bf16[152,256]{1,0:T(8,128)(2,1)S(1)}, f32[8,128]{1,0:T(8,128)S(1)}, f32[3,64,64]{2,1,0:T(8,128)S(1)}, f32[144,256]{1,0:T(8,128)S(1)}) custom-call(bf16[64,256]{1,0:T(8,128)(2,1)S(1)} %pair.3.refs_0_, bf16[64,256]{1,0:T(8,128)(2,1)S(1)} %collective-permute-done.1.refs_1_, bf16[64,256]{1,0:T(8,128)(2,1)S(1)} %collective-permute-done.2.refs_2_, ...), custom_call_target="tpu_custom_call" | custom-call | tf_op jit(solution)/shard_map/points/pallas_call | solution.py:482
  20.5 3.7 %collective-permute-start.6 = (bf16[152,256]{1,0:T(8,128)(2,1)S(1)}, bf16[152,256]{1,0:T(8,128)(2,1)S(1)}, u32[]{:S(2)}, u32[]{:S(2)}) collective-permute-start(bf16[152,256]{1,0:T(8,128)(2,1)S(1)} %get-tuple-element.37.refs_0_), channel_id=1, source_target_pairs={{0,3},{1,2},{2,1},{3,0},{4,6},{5,7},{6,4},{7,5},{8,11},{9,10},{10,... | collective-permute-start | bytes 233480 | tf_op jit(solution)/shard_map/ppermute | solution.py:506
  24.9 2.7 %collective-permute-done.6.refs_3_ = bf16[152,256]{1,0:T(8,128)(2,1)S(1)} collective-permute-done((bf16[152,256]{1,0:T(8,128)(2,1)S(1)}, bf16[152,256]{1,0:T(8,128)(2,1)S(1)}, u32[]{:S(2)}, u32[]{:S(2)}) %collective-permute-start.6) | collective-permute-done | bytes 77856 | tf_op jit(solution)/shard_map/ppermute | solution.py:506
  29.5 3.5 %camera.2 = (bf16[64,256]{1,0:T(8,128)(2,1)S(1)}, f32[9,64,128]{2,1,0:T(8,128)S(1)}, f32[9,64,128]{2,1,0:T(8,128)S(1)}, f32[9,64,128]{2,1,0:T(8,128)S(1)}, f32[9,64,128]{2,1,0:T(8,128)S(1)}) custom-call(bf16[152,256]{1,0:T(8,128)(2,1)S(1)} %get-tuple-element.37.refs_0_, bf16[152,256]{1,0:T(8,128)(2,1)S(1)} %collective-permute-done.4.refs_1_, ...), custom_call_target="tpu_custom_call" | custom-call | tf_op jit(solution)/shard_map/camera/pallas_call | solution.py:482
  34.3 1.5 %collective-permute-start.10 = (bf16[64,256]{1,0:T(8,128)(2,1)S(1)}, bf16[64,256]{1,0:T(8,128)(2,1)S(1)}, u32[]{:S(2)}, u32[]{:S(2)}) collective-permute-start(bf16[64,256]{1,0:T(8,128)(2,1)S(1)} %pair.4.refs_0_), channel_id=1, source_target_pairs={{0,24},{4,28},{8,16},{12,20},{16,8},{20,12},{24,0},{28,4},{1,25},{... | collective-permute-start | bytes 98312 | tf_op jit(solution)/shard_map/ppermute | solution.py:494
  36.3 1.5 %collective-permute-start.8 = (bf16[64,256]{1,0:T(8,128)(2,1)S(1)}, bf16[64,256]{1,0:T(8,128)(2,1)S(1)}, u32[]{:S(2)}, u32[]{:S(2)}) collective-permute-start(bf16[64,256]{1,0:T(8,128)(2,1)S(1)} %pair.4.refs_0_), channel_id=1, source_target_pairs={{0,8},{4,12},{8,0},{12,4},{16,24},{20,28},{24,16},{28,20},{1,9},{5... | collective-permute-start | bytes 98312 | tf_op jit(solution)/shard_map/ppermute | solution.py:494
  37.8 1.3 %collective-permute-done.10.refs_3_ = bf16[64,256]{1,0:T(8,128)(2,1)S(1)} collective-permute-done((bf16[64,256]{1,0:T(8,128)(2,1)S(1)}, bf16[64,256]{1,0:T(8,128)(2,1)S(1)}, u32[]{:S(2)}, u32[]{:S(2)}) %collective-permute-start.10) | collective-permute-done | bytes 32800 | tf_op jit(solution)/shard_map/ppermute | solution.py:494
  40.2 2.8 %points.4 = (bf16[152,256]{1,0:T(8,128)(2,1)S(1)}, f32[8,128]{1,0:T(8,128)S(1)}, f32[3,64,64]{2,1,0:T(8,128)S(1)}, f32[144,256]{1,0:T(8,128)S(1)}) custom-call(bf16[64,256]{1,0:T(8,128)(2,1)S(1)} %pair.4.refs_0_, bf16[64,256]{1,0:T(8,128)(2,1)S(1)} %collective-permute-done.8.refs_1_, bf16[64,256]{1,0:T(8,128)(2,1)S(1)} %collective-permute-done.9.refs_2_, ...), custom_call_target="tpu_custom_call" | custom-call | tf_op jit(solution)/shard_map/points/pallas_call | solution.py:482
  43.1 3.6 %collective-permute-start.13 = (bf16[152,256]{1,0:T(8,128)(2,1)S(1)}, bf16[152,256]{1,0:T(8,128)(2,1)S(1)}, u32[]{:S(2)}, u32[]{:S(2)}) collective-permute-start(bf16[152,256]{1,0:T(8,128)(2,1)S(1)} %get-tuple-element.47.refs_0_), channel_id=1, source_target_pairs={{0,3},{1,2},{2,1},{3,0},{4,6},{5,7},{6,4},{7,5},{8,11},{9,10},{10,... | collective-permute-start | bytes 233480 | tf_op jit(solution)/shard_map/ppermute | solution.py:506
  47.5 2.6 %collective-permute-done.13.refs_3_ = bf16[152,256]{1,0:T(8,128)(2,1)S(1)} collective-permute-done((bf16[152,256]{1,0:T(8,128)(2,1)S(1)}, bf16[152,256]{1,0:T(8,128)(2,1)S(1)}, u32[]{:S(2)}, u32[]{:S(2)}) %collective-permute-start.13) | collective-permute-done | bytes 77856 | tf_op jit(solution)/shard_map/ppermute | solution.py:506
  50.1 2.1 %collective-permute-done.12.refs_2_ = bf16[152,256]{1,0:T(8,128)(2,1)S(1)} collective-permute-done((bf16[152,256]{1,0:T(8,128)(2,1)S(1)}, bf16[152,256]{1,0:T(8,128)(2,1)S(1)}, u32[]{:S(2)}, u32[]{:S(2)}) %collective-permute-start.12) | collective-permute-done | bytes 77856 | tf_op jit(solution)/shard_map/ppermute | solution.py:506
  52.2 3.4 %camera.3 = (bf16[64,256]{1,0:T(8,128)(2,1)S(1)}, f32[9,64,128]{2,1,0:T(8,128)S(1)}, f32[9,64,128]{2,1,0:T(8,128)S(1)}, f32[9,64,128]{2,1,0:T(8,128)S(1)}, f32[9...) custom-call(bf16[152,256]{1,0:T(8,128)(2,1)S(1)} %get-tuple-element.47.refs_0_, ...), custom_call_target="tpu_custom_call" | custom-call | tf_op jit(solution)/shard_map/camera/pallas_call | solution.py:482
  57.0 2.1 %collective-permute-start.17 = (bf16[64,256]{1,0:T(8,128)(2,1)S(1)}, bf16[64,256]{1,0:T(8,128)(2,1)S(1)}, u32[]{:S(2)}, u32[]{:S(2)}) collective-permute-start(bf16[64,256]{1,0:T(8,128)(2,1)S(1)} %pair.5.refs_0_), channel_id=1, source_target_pairs={{0,24},{4,28},{8,16},{12,20},{16,8},{20,12},{24,0},{28,4},{1,25},{... | collective-permute-start | bytes 98312 | tf_op jit(solution)/shard_map/ppermute | solution.py:494
  60.5 1.4 %collective-permute-done.17.refs_3_ = bf16[64,256]{1,0:T(8,128)(2,1)S(1)} collective-permute-done((bf16[64,256]{1,0:T(8,128)(2,1)S(1)}, bf16[64,256]{1,0:T(8,128)(2,1)S(1)}, u32[]{:S(2)}, u32[]{:S(2)}) %collective-permute-start.17) | collective-permute-done | bytes 32800 | tf_op jit(solution)/shard_map/ppermute | solution.py:494
  63.3 2.7 %points.5 = (bf16[152,256]{1,0:T(8,128)(2,1)S(1)}, f32[8,128]{1,0:T(8,128)S(1)}) custom-call(bf16[64,256]{1,0:T(8,128)(2,1)S(1)} %pair.5.refs_0_, bf16[64,256]{1,0:T(8,128)(2,1)S(1)} %collective-permute-done.15.refs_1_, bf16[64,256]{1,0:T(8,128)(2,1)S(1)} %collective-permute-done.16.refs_2_, bf16[64,256]{1,0:T(8,128)(2,1)S(1)} %collective-permute-done.17.refs_3_, ...), custom_call_target="tpu_custom_call" | custom-call | tf_op jit(solution)/shard_map/points/pallas_call | solution.py:482
  66.0 2.8 %collective-permute-start.20 = (bf16[152,256]{1,0:T(8,128)(2,1)S(1)}, bf16[152,256]{1,0:T(8,128)(2,1)S(1)}, u32[]{:S(2)}, u32[]{:S(2)}) collective-permute-start(bf16[152,256]{1,0:T(8,128)(2,1)S(1)} %get-tuple-element.56.refs_0_), channel_id=1, source_target_pairs={{0,3},{1,2},{2,1},{3,0},{4,6},{5,7},{6,4},{7,5},{8,11},{9,10},{10,... | collective-permute-start | bytes 233480 | tf_op jit(solution)/shard_map/ppermute | solution.py:506
  68.8 1.7 %collective-permute-start.18 = (bf16[152,256]{1,0:T(8,128)(2,1)S(1)}, bf16[152,256]{1,0:T(8,128)(2,1)S(1)}, u32[]{:S(2)}, u32[]{:S(2)}) collective-permute-start(bf16[152,256]{1,0:T(8,128)(2,1)S(1)} %get-tuple-element.56.refs_0_), channel_id=1, source_target_pairs={{0,2},{1,3},{2,0},{3,1},{4,5},{5,4},{6,7},{7,6},{8,10},{9,11},{10,... | collective-permute-start | bytes 233480 | tf_op jit(solution)/shard_map/ppermute | solution.py:506
  70.5 2.5 %collective-permute-done.20.refs_3_ = bf16[152,256]{1,0:T(8,128)(2,1)S(1)} collective-permute-done((bf16[152,256]{1,0:T(8,128)(2,1)S(1)}, bf16[152,256]{1,0:T(8,128)(2,1)S(1)}, u32[]{:S(2)}, u32[]{:S(2)}) %collective-permute-start.20) | collective-permute-done | bytes 77856 | tf_op jit(solution)/shard_map/ppermute | solution.py:506
  73.0 1.7 %collective-permute-done.19.refs_2_ = bf16[152,256]{1,0:T(8,128)(2,1)S(1)} collective-permute-done((bf16[152,256]{1,0:T(8,128)(2,1)S(1)}, bf16[152,256]{1,0:T(8,128)(2,1)S(1)}, u32[]{:S(2)}, u32[]{:S(2)}) %collective-permute-start.19) | collective-permute-done | bytes 77856 | tf_op jit(solution)/shard_map/ppermute | solution.py:506
  74.7 1.9 %finish.1 = (f32[9,8192]{1,0:T(8,128)}, f32[9,8192]{1,0:T(8,128)}) custom-call(bf16[152,256]{1,0:T(8,128)(2,1)S(1)} %get-tuple-element.56.refs_0_, bf16[152,256]{1,0:T(8,128)(2,1)S(1)} %collective-permute-done.18.refs_1_, bf16[152,256]{1,0:T(8,128)(2,1)S(1)} %collective-permute-done.19.refs_2_, bf16[152,256]{1,0:T(8,128)(2,1)S(1)} %collective-permute-done.20.refs_3_, ...), custom_call_target="tpu_custom_call" | custom-call | tf_op jit(solution)/shard_map/finish/pallas_call | solution.py:482
  (28 shorter events, 13.5 us)
Async XLA Ops:
  8.1 1.4 %collective-permute-start = (bf16[64,256]{1,0:T(8,128)(2,1)S(1)}, bf16[64,256]{1,0:T(8,128)(2,1)S(1)}, u32[]{:S(2)}, u32[]{:S(2)}) collective-permute-start(bf16[64,256]{1,0:T(8,128)(2,1)S(1)} %get-tuple-element.33.refs_0_), channel_id=1, source_target_pairs={{0,4},{4,0},{8,12},{12,8},{16,20},{20,16},{24,28},{28,24},{1,5},{5... | collective-permute-start | bytes 98312 | tf_op jit(solution)/shard_map/ppermute | solution.py:494
  9.6 5.7 %collective-permute-start.3 = (bf16[64,256]{1,0:T(8,128)(2,1)S(1)}, bf16[64,256]{1,0:T(8,128)(2,1)S(1)}, u32[]{:S(2)}, u32[]{:S(2)}) collective-permute-start(bf16[64,256]{1,0:T(8,128)(2,1)S(1)} %pair.3.refs_0_), channel_id=1, source_target_pairs={{0,24},{4,28},{8,16},{12,20},{16,8},{20,12},{24,0},{28,4},{1,25},{... | collective-permute-start | bytes 98312 | tf_op jit(solution)/shard_map/ppermute | solution.py:494
  13.4 3.9 %collective-permute-start.2 = (bf16[64,256]{1,0:T(8,128)(2,1)S(1)}, bf16[64,256]{1,0:T(8,128)(2,1)S(1)}, u32[]{:S(2)}, u32[]{:S(2)}) collective-permute-start(bf16[64,256]{1,0:T(8,128)(2,1)S(1)} %pair.3.refs_0_), channel_id=1, source_target_pairs={{0,16},{4,20},{8,24},{12,28},{16,0},{20,4},{24,8},{28,12},{1,17},{... | collective-permute-start | bytes 98312 | tf_op jit(solution)/shard_map/ppermute | solution.py:494
  13.9 3.9 %collective-permute-start.1 = (bf16[64,256]{1,0:T(8,128)(2,1)S(1)}, bf16[64,256]{1,0:T(8,128)(2,1)S(1)}, u32[]{:S(2)}, u32[]{:S(2)}) collective-permute-start(bf16[64,256]{1,0:T(8,128)(2,1)S(1)} %pair.3.refs_0_), channel_id=1, source_target_pairs={{0,8},{4,12},{8,0},{12,4},{16,24},{20,28},{24,16},{28,20},{1,9},{5... | collective-permute-start | bytes 98312 | tf_op jit(solution)/shard_map/ppermute | solution.py:494
  20.5 7.1 %collective-permute-start.6 = (bf16[152,256]{1,0:T(8,128)(2,1)S(1)}, bf16[152,256]{1,0:T(8,128)(2,1)S(1)}, u32[]{:S(2)}, u32[]{:S(2)}) collective-permute-start(bf16[152,256]{1,0:T(8,128)(2,1)S(1)} %get-tuple-element.37.refs_0_), channel_id=1, source_target_pairs={{0,3},{1,2},{2,1},{3,0},{4,6},{5,7},{6,4},{7,5},{8,11},{9,10},{10,... | collective-permute-start | bytes 233480 | tf_op jit(solution)/shard_map/ppermute | solution.py:506
  24.2 4.4 %collective-permute-start.5 = (bf16[152,256]{1,0:T(8,128)(2,1)S(1)}, bf16[152,256]{1,0:T(8,128)(2,1)S(1)}, u32[]{:S(2)}, u32[]{:S(2)}) collective-permute-start(bf16[152,256]{1,0:T(8,128)(2,1)S(1)} %get-tuple-element.37.refs_0_), channel_id=1, source_target_pairs={{0,1},{1,0},{2,3},{3,2},{4,7},{5,6},{6,5},{7,4},{8,9},{9,8},{10,11... | collective-permute-start | bytes 233480 | tf_op jit(solution)/shard_map/ppermute | solution.py:506
  24.2 5.3 %collective-permute-start.4 = (bf16[152,256]{1,0:T(8,128)(2,1)S(1)}, bf16[152,256]{1,0:T(8,128)(2,1)S(1)}, u32[]{:S(2)}, u32[]{:S(2)}) collective-permute-start(bf16[152,256]{1,0:T(8,128)(2,1)S(1)} %get-tuple-element.37.refs_0_), channel_id=1, source_target_pairs={{0,2},{1,3},{2,0},{3,1},{4,5},{5,4},{6,7},{7,6},{8,10},{9,11},{10,... | collective-permute-start | bytes 233480 | tf_op jit(solution)/shard_map/ppermute | solution.py:506
  32.9 1.2 %collective-permute-start.7 = (bf16[64,256]{1,0:T(8,128)(2,1)S(1)}, bf16[64,256]{1,0:T(8,128)(2,1)S(1)}, u32[]{:S(2)}, u32[]{:S(2)}) collective-permute-start(bf16[64,256]{1,0:T(8,128)(2,1)S(1)} %get-tuple-element.44.refs_0_), channel_id=1, source_target_pairs={{0,4},{4,0},{8,12},{12,8},{16,20},{20,16},{24,28},{28,24},{1,5},{5... | collective-permute-start | bytes 98312 | tf_op jit(solution)/shard_map/ppermute | solution.py:494
  34.3 4.8 %collective-permute-start.10 = (bf16[64,256]{1,0:T(8,128)(2,1)S(1)}, bf16[64,256]{1,0:T(8,128)(2,1)S(1)}, u32[]{:S(2)}, u32[]{:S(2)}) collective-permute-start(bf16[64,256]{1,0:T(8,128)(2,1)S(1)} %pair.4.refs_0_), channel_id=1, source_target_pairs={{0,24},{4,28},{8,16},{12,20},{16,8},{20,12},{24,0},{28,4},{1,25},{... | collective-permute-start | bytes 98312 | tf_op jit(solution)/shard_map/ppermute | solution.py:494
  35.8 3.9 %collective-permute-start.9 = (bf16[64,256]{1,0:T(8,128)(2,1)S(1)}, bf16[64,256]{1,0:T(8,128)(2,1)S(1)}, u32[]{:S(2)}, u32[]{:S(2)}) collective-permute-start(bf16[64,256]{1,0:T(8,128)(2,1)S(1)} %pair.4.refs_0_), channel_id=1, source_target_pairs={{0,16},{4,20},{8,24},{12,28},{16,0},{20,4},{24,8},{28,12},{1,17},{... | collective-permute-start | bytes 98312 | tf_op jit(solution)/shard_map/ppermute | solution.py:494
  36.3 3.9 %collective-permute-start.8 = (bf16[64,256]{1,0:T(8,128)(2,1)S(1)}, bf16[64,256]{1,0:T(8,128)(2,1)S(1)}, u32[]{:S(2)}, u32[]{:S(2)}) collective-permute-start(bf16[64,256]{1,0:T(8,128)(2,1)S(1)} %pair.4.refs_0_), channel_id=1, source_target_pairs={{0,8},{4,12},{8,0},{12,4},{16,24},{20,28},{24,16},{28,20},{1,9},{5... | collective-permute-start | bytes 98312 | tf_op jit(solution)/shard_map/ppermute | solution.py:494
  43.1 7.0 %collective-permute-start.13 = (bf16[152,256]{1,0:T(8,128)(2,1)S(1)}, bf16[152,256]{1,0:T(8,128)(2,1)S(1)}, u32[]{:S(2)}, u32[]{:S(2)}) collective-permute-start(bf16[152,256]{1,0:T(8,128)(2,1)S(1)} %get-tuple-element.47.refs_0_), channel_id=1, source_target_pairs={{0,3},{1,2},{2,1},{3,0},{4,6},{5,7},{6,4},{7,5},{8,11},{9,10},{10,... | collective-permute-start | bytes 233480 | tf_op jit(solution)/shard_map/ppermute | solution.py:506
  46.6 5.6 %collective-permute-start.12 = (bf16[152,256]{1,0:T(8,128)(2,1)S(1)}, bf16[152,256]{1,0:T(8,128)(2,1)S(1)}, u32[]{:S(2)}, u32[]{:S(2)}) collective-permute-start(bf16[152,256]{1,0:T(8,128)(2,1)S(1)} %get-tuple-element.47.refs_0_), channel_id=1, source_target_pairs={{0,1},{1,0},{2,3},{3,2},{4,7},{5,6},{6,5},{7,4},{8,9},{9,8},{10,11... | collective-permute-start | bytes 233480 | tf_op jit(solution)/shard_map/ppermute | solution.py:506
  46.6 5.6 %collective-permute-start.11 = (bf16[152,256]{1,0:T(8,128)(2,1)S(1)}, bf16[152,256]{1,0:T(8,128)(2,1)S(1)}, u32[]{:S(2)}, u32[]{:S(2)}) collective-permute-start(bf16[152,256]{1,0:T(8,128)(2,1)S(1)} %get-tuple-element.47.refs_0_), channel_id=1, source_target_pairs={{0,2},{1,3},{2,0},{3,1},{4,5},{5,4},{6,7},{7,6},{8,10},{9,11},{10,... | collective-permute-start | bytes 233480 | tf_op jit(solution)/shard_map/ppermute | solution.py:506
  55.6 1.2 %collective-permute-start.14 = (bf16[64,256]{1,0:T(8,128)(2,1)S(1)}, bf16[64,256]{1,0:T(8,128)(2,1)S(1)}, u32[]{:S(2)}, u32[]{:S(2)}) collective-permute-start(bf16[64,256]{1,0:T(8,128)(2,1)S(1)} %get-tuple-element.53.refs_0_), channel_id=1, source_target_pairs={{0,4},{4,0},{8,12},{12,8},{16,20},{20,16},{24,28},{28,24},{1,5},{5... | collective-permute-start | bytes 98312 | tf_op jit(solution)/shard_map/ppermute | solution.py:494
  57.0 4.9 %collective-permute-start.17 = (bf16[64,256]{1,0:T(8,128)(2,1)S(1)}, bf16[64,256]{1,0:T(8,128)(2,1)S(1)}, u32[]{:S(2)}, u32[]{:S(2)}) collective-permute-start(bf16[64,256]{1,0:T(8,128)(2,1)S(1)} %pair.5.refs_0_), channel_id=1, source_target_pairs={{0,24},{4,28},{8,16},{12,20},{16,8},{20,12},{24,0},{28,4},{1,25},{... | collective-permute-start | bytes 98312 | tf_op jit(solution)/shard_map/ppermute | solution.py:494
  59.1 3.9 %collective-permute-start.16 = (bf16[64,256]{1,0:T(8,128)(2,1)S(1)}, bf16[64,256]{1,0:T(8,128)(2,1)S(1)}, u32[]{:S(2)}, u32[]{:S(2)}) collective-permute-start(bf16[64,256]{1,0:T(8,128)(2,1)S(1)} %pair.5.refs_0_), channel_id=1, source_target_pairs={{0,16},{4,20},{8,24},{12,28},{16,0},{20,4},{24,8},{28,12},{1,17},{... | collective-permute-start | bytes 98312 | tf_op jit(solution)/shard_map/ppermute | solution.py:494
  59.4 3.9 %collective-permute-start.15 = (bf16[64,256]{1,0:T(8,128)(2,1)S(1)}, bf16[64,256]{1,0:T(8,128)(2,1)S(1)}, u32[]{:S(2)}, u32[]{:S(2)}) collective-permute-start(bf16[64,256]{1,0:T(8,128)(2,1)S(1)} %pair.5.refs_0_), channel_id=1, source_target_pairs={{0,8},{4,12},{8,0},{12,4},{16,24},{20,28},{24,16},{28,20},{1,9},{5... | collective-permute-start | bytes 98312 | tf_op jit(solution)/shard_map/ppermute | solution.py:494
  66.0 6.9 %collective-permute-start.20 = (bf16[152,256]{1,0:T(8,128)(2,1)S(1)}, bf16[152,256]{1,0:T(8,128)(2,1)S(1)}, u32[]{:S(2)}, u32[]{:S(2)}) collective-permute-start(bf16[152,256]{1,0:T(8,128)(2,1)S(1)} %get-tuple-element.56.refs_0_), channel_id=1, source_target_pairs={{0,3},{1,2},{2,1},{3,0},{4,6},{5,7},{6,4},{7,5},{8,11},{9,10},{10,... | collective-permute-start | bytes 233480 | tf_op jit(solution)/shard_map/ppermute | solution.py:506
  68.8 5.8 %collective-permute-start.19 = (bf16[152,256]{1,0:T(8,128)(2,1)S(1)}, bf16[152,256]{1,0:T(8,128)(2,1)S(1)}, u32[]{:S(2)}, u32[]{:S(2)}) collective-permute-start(bf16[152,256]{1,0:T(8,128)(2,1)S(1)} %get-tuple-element.56.refs_0_), channel_id=1, source_target_pairs={{0,1},{1,0},{2,3},{3,2},{4,7},{5,6},{6,5},{7,4},{8,9},{9,8},{10,11... | collective-permute-start | bytes 233480 | tf_op jit(solution)/shard_map/ppermute | solution.py:506
  68.8 5.8 %collective-permute-start.18 = (bf16[152,256]{1,0:T(8,128)(2,1)S(1)}, bf16[152,256]{1,0:T(8,128)(2,1)S(1)}, u32[]{:S(2)}, u32[]{:S(2)}) collective-permute-start(bf16[152,256]{1,0:T(8,128)(2,1)S(1)} %get-tuple-element.56.refs_0_), channel_id=1, source_target_pairs={{0,2},{1,3},{2,0},{3,1},{4,5},{5,4},{6,7},{7,6},{8,10},{9,11},{10,... | collective-permute-start | bytes 233480 | tf_op jit(solution)/shard_map/ppermute | solution.py:506
